TPU v7x, 512 devices: a whole 4x4x16 slice. The times are simulated.
512 devices in a mesh: sec: 8 (over z_hi, x), tile: 64 (over z_lo, y, core).
Axes of the slice: x: 4, y: 4, z: 16 (z_hi: 2, z_lo: 8; z = z_hi * 8 + z_lo), core: 2. Of those that a mesh axis runs over, the one named last changes fastest.
Arguments:
- depth: float32 [512, 8192], P('sec', 'tile'), may hold values from 0 to 2
- elevation: float32 [512, 8192], P('sec', 'tile'), may hold values from -6 to 6
- land_mask: int32 [512, 8192], P('sec', 'tile'), may hold values 0 or 1
- pressure: float32 [5, 512, 8, 1024], P(None, ('sec', 'tile')), may hold values from -6 to 6
- saturated_conductance: float32 [5, 512, 8, 1024], P(None, ('sec', 'tile')), may hold values from 0.2 to 5
Outputs:
- depth_final: float32 [512, 8192], P('sec', 'tile')
- pressure_final: float32 [5, 512, 8, 1024], P(None, ('sec', 'tile'))
All inputs are finite; a program needn't handle non-finite values. No bound on the sum of `land_mask` on one device may be relied on, other than what follows from the above.
Results may differ from a plain program's by a relative error of at most 0.000035.
Values sent between devices are 32-bit elements; how exact they have to be, the bound alone decides.
No kernel may reach another device: no remote copies, remote signals or barrier semaphores. Data moves between devices by JAX's collectives and lax.ppermute only.
A program may use at most 64 MiB of HBM per device.

v0:
```python
import math

import jax
import jax.numpy as jnp
from jax import lax
from jax.sharding import PartitionSpec as P

SWEEPS = 3
STEPS = 4


STORAGE = 0.3
VERTICAL = 2.0
ROUTING = 0.15
LEAKANCE = 0.25
SPECTRUM_MID = 1.025
SPECTRUM_HALF = 0.975


def swapped(value, axis, distance):
    return lax.ppermute(value, axis, [(i, i ^ 1 << distance) for i in range(lax.axis_size(axis))])


def with_halo(value, sides, width):
    for axis, dim in sides:
        peers, length = (lax.axis_size(axis), value.shape[dim])
        up = [(i, (i + 1) % peers) for i in range(peers - 1)]
        down = [(j, i) for i, j in up]
        last = lax.slice_in_dim(value, length - width, length, axis=dim)
        leading = lax.slice_in_dim(value, 0, width, axis=dim)
        before = lax.ppermute(last, axis, up)
        after = lax.ppermute(leading, axis, down)
        value = jnp.concatenate([before, value, after], axis=dim)
    return value


def sweep_factors(number):
    return [
        1.0
        / (SPECTRUM_MID - SPECTRUM_HALF * math.cos(math.pi * (2 * sweep_index + 1) / (2 * number)))
        for sweep_index in range(number)
    ]


def surface_pair(depth, elevation):
    return jnp.stack([depth + elevation, 1.0 + 0.5 * jnp.tanh(depth)])


def surface_change(padded):
    heads = padded[0]
    mobile = padded[1]
    middle_head = heads[1:-1, 1:-1]
    middle_mobile = mobile[1:-1, 1:-1]
    change = jnp.zeros_like(middle_head)
    others = (
        (heads[2:, 1:-1], mobile[2:, 1:-1]),
        (heads[:-2, 1:-1], mobile[:-2, 1:-1]),
        (heads[1:-1, 2:], mobile[1:-1, 2:]),
        (heads[1:-1, :-2], mobile[1:-1, :-2]),
    )
    for other_head, other_mobile in others:
        change = change + 0.5 * (middle_mobile + other_mobile) * (other_head - middle_head)
    return ROUTING * change


def coefficients(conduct):
    middle = conduct[:, 1:-1, 1:-1]
    row_before = 0.5 * (middle + conduct[:, :-2, 1:-1])
    row_after = 0.5 * (middle + conduct[:, 2:, 1:-1])
    col_before = 0.5 * (middle + conduct[:, 1:-1, :-2])
    col_after = 0.5 * (middle + conduct[:, 1:-1, 2:])
    between = VERTICAL * 0.5 * (middle[:-1] + middle[1:])
    nothing = jnp.zeros_like(middle[:1])
    layer_above = jnp.concatenate([nothing, between], 0)
    layer_below = jnp.concatenate([between, nothing], 0)
    diagonal = STORAGE + row_before + row_after + col_before + col_after + layer_above + layer_below
    return (row_before, row_after, col_before, col_after, layer_above, layer_below, diagonal)


def relaxation(iterate, stencil, right_side, factor):
    row_before, row_after, col_before, col_after, layer_above, layer_below, diagonal = stencil
    middle = iterate[:, 1:-1, 1:-1]
    layers_pad = jnp.pad(middle, ((1, 1), (0, 0), (0, 0)))
    neighbours = (
        row_before * iterate[:, :-2, 1:-1]
        + row_after * iterate[:, 2:, 1:-1]
        + col_before * iterate[:, 1:-1, :-2]
        + col_after * iterate[:, 1:-1, 2:]
        + layer_above * layers_pad[:-2]
        + layer_below * layers_pad[2:]
    )
    return middle + factor * (right_side - diagonal * middle + neighbours) / diagonal


def storage_side(pressure, flux):
    extra = jnp.concatenate([flux[None], jnp.zeros_like(pressure[1:])], 0)
    return STORAGE * pressure + extra


def regroup(pieces, send):
    own_index = lax.axis_index("tile")
    for bit in range(3):
        dims = pieces.shape
        split = pieces.reshape((8 >> bit + 1, 2, 1 << bit) + dims[1:])
        lower = split[:, 0]
        higher = split[:, 1]
        upper = own_index >> bit & 1 == 1
        incoming = send(jnp.where(upper, lower, higher), bit)
        lower = jnp.where(upper, incoming, lower)
        higher = jnp.where(upper, higher, incoming)
        pieces = jnp.stack([lower, higher], 1).reshape(dims)
    return pieces


def shuttle_move(piece, bit):
    return swapped(piece, "tile", bit)


def surface_rims(depth, elevation):
    return with_halo(surface_pair(depth, elevation), (("sec", 1), ("tile", 2)), 1)


def block_rims(field):
    return with_halo(field, (("sec", 1), ("tile", 2)), 1)


def bands_to_surface(field, send, block_rows, block_cols):
    soil_layers = field.shape[0]
    sub_rows = field.shape[1]
    parts = field.reshape(soil_layers, sub_rows, 8, block_cols)
    moved = regroup(jnp.moveaxis(parts, 2, 0), send)
    return jnp.moveaxis(moved, 0, 1).reshape(soil_layers, block_rows, block_cols)


def surface_to_bands(field, send, sub_rows, band_cols):
    soil_layers = field.shape[0]
    block_cols = field.shape[2]
    outgoing = jnp.moveaxis(field.reshape(soil_layers, 8, sub_rows, block_cols), 1, 0)
    moved = regroup(outgoing, send)
    return jnp.moveaxis(moved, 0, 2).reshape(soil_layers, sub_rows, band_cols)


def subsurface_step(current, soil_wide, flux, factors, rims):
    widened = rims(current)
    stencil = coefficients(soil_wide / (1.0 + widened * widened))
    right_side = storage_side(current, flux)
    iterate = relaxation(widened, stencil, right_side, factors[0])
    for factor in factors[1:]:
        iterate = relaxation(rims(iterate), stencil, right_side, factor)
    return iterate


def local(depth, elevation, land_mask, pressure, saturated_conductance):
    land_share = land_mask.astype(jnp.float32)
    factors = sweep_factors(SWEEPS)
    sub_rows = pressure.shape[2]
    band_cols = pressure.shape[3]
    block_rows = depth.shape[0]
    block_cols = depth.shape[1]
    current = pressure[:, 0]
    soil_here = saturated_conductance[:, 0]
    soil_wide = block_rims(bands_to_surface(soil_here, shuttle_move, block_rows, block_cols))
    for step_number in range(STEPS):
        blocks = bands_to_surface(current, shuttle_move, block_rows, block_cols)
        flux = LEAKANCE * (depth - blocks[0])
        new_depth = land_share * (depth + surface_change(surface_rims(depth, elevation)) - flux)
        blocks = subsurface_step(blocks, soil_wide, flux, factors, block_rims)
        current = surface_to_bands(blocks, shuttle_move, sub_rows, band_cols)
        depth = new_depth
    return (depth, current[:, None])


def solution(mesh):
    placed = (
        P("sec", "tile"),
        P("sec", "tile"),
        P("sec", "tile"),
        P(None, ("sec", "tile"), None, None),
        P(None, ("sec", "tile"), None, None),
    )
    return jax.shard_map(
        local,
        mesh=mesh,
        in_specs=placed,
        out_specs=(P("sec", "tile"), P(None, ("sec", "tile"), None, None)),
        check_vma=False,
    )
```

profile of v0, /device:TPU:38, one launch (start us, length us, event | category | flops | bytes accessed | tf_op | source)
XLA Modules:
  0.0 621.0 jit_solution(17454861958322671953)
XLA Ops:
  24.3 14.7 %collective-permute-start.14 = (f32[5,1,128]{2,1,0:T(1,128)S(1)}, f32[5,1,128]{2,1,0:T(1,128)S(1)}, u32[]{:S(2)}, u32[]{:S(2)}) collective-permute-start(f32[5,1,128]{2,1,0:T(1,128)S(1)} %get-tuple-element.116), channel_id=1, source_target_pairs={{0,64},{64,128},{128,192},{192,256},{256,320},{320,384},{384,448},... | collective-permute-start | bytes 7688 | tf_op jit(solution)/shard_map/ppermute | solution.py:31
  41.1 14.7 %collective-permute-start.18 = (f32[5,1,128]{2,1,0:T(1,128)S(1)}, f32[5,1,128]{2,1,0:T(1,128)S(1)}, u32[]{:S(2)}, u32[]{:S(2)}) collective-permute-start(f32[5,1,128]{2,1,0:T(1,128)S(1)} %get-tuple-element.120), channel_id=1, source_target_pairs={{0,64},{64,128},{128,192},{192,256},{256,320},{320,384},{384,448},... | collective-permute-start | bytes 7688 | tf_op jit(solution)/shard_map/ppermute | solution.py:31
  59.8 5.8 collective-permute-start.17
  65.6 6.5 %collective-permute-done.19 = f32[5,1,128]{2,1,0:T(1,128)S(1)} collective-permute-done((f32[5,1,128]{2,1,0:T(1,128)S(1)}, f32[5,1,128]{2,1,0:T(1,128)S(1)}, u32[]{:S(2)}, u32[]{:S(2)}) %collective-permute-start.19) | collective-permute-done | bytes 2592 | tf_op jit(solution)/shard_map/ppermute | solution.py:32
  74.2 5.8 collective-permute-start.21
  84.0 8.2 %collective-permute-start.22 = (f32[5,1,128]{2,1,0:T(1,128)S(1)}, f32[5,1,128]{2,1,0:T(1,128)S(1)}, u32[]{:S(2)}, u32[]{:S(2)}) collective-permute-start(f32[5,1,128]{2,1,0:T(1,128)S(1)} %get-tuple-element.112), channel_id=1, source_target_pairs={{0,64},{64,128},{128,192},{192,256},{256,320},{320,384},{384,448},... | collective-permute-start | bytes 7688 | tf_op jit(solution)/shard_map/ppermute | solution.py:31
  94.2 14.4 %collective-permute-done.23 = f32[5,1,128]{2,1,0:T(1,128)S(1)} collective-permute-done((f32[5,1,128]{2,1,0:T(1,128)S(1)}, f32[5,1,128]{2,1,0:T(1,128)S(1)}, u32[]{:S(2)}, u32[]{:S(2)}) %collective-permute-start.23) | collective-permute-done | bytes 2592 | tf_op jit(solution)/shard_map/ppermute | solution.py:32
  110.7 5.8 collective-permute-start.25
  125.8 12.4 %collective-permute-done.27 = f32[5,1,128]{2,1,0:T(1,128)S(1)} collective-permute-done((f32[5,1,128]{2,1,0:T(1,128)S(1)}, f32[5,1,128]{2,1,0:T(1,128)S(1)}, u32[]{:S(2)}, u32[]{:S(2)}) %collective-permute-start.27) | collective-permute-done | bytes 2592 | tf_op jit(solution)/shard_map/ppermute | solution.py:32
  140.3 5.8 collective-permute-start.29
  172.6 10.3 %collective-permute-done.1 = f32[2,1,128]{2,1,0:T(1,128)S(1)} collective-permute-done((f32[2,1,128]{2,1,0:T(1,128)S(1)}, f32[2,1,128]{2,1,0:T(1,128)S(1)}, u32[]{:S(2)}, u32[]{:S(2)}) %collective-permute-start.1) | collective-permute-done | bytes 1056 | tf_op jit(solution)/shard_map/ppermute | solution.py:32
  188.1 5.8 collective-permute-start.3
  207.7 14.0 %collective-permute-done.41 = f32[5,1,128]{2,1,0:T(1,128)S(1)} collective-permute-done((f32[5,1,128]{2,1,0:T(1,128)S(1)}, f32[5,1,128]{2,1,0:T(1,128)S(1)}, u32[]{:S(2)}, u32[]{:S(2)}) %collective-permute-start.41) | collective-permute-done | bytes 2592 | tf_op jit(solution)/shard_map/ppermute | solution.py:32
  223.8 5.8 collective-permute-start.43
  239.5 12.4 %collective-permute-done.45 = f32[5,1,128]{2,1,0:T(1,128)S(1)} collective-permute-done((f32[5,1,128]{2,1,0:T(1,128)S(1)}, f32[5,1,128]{2,1,0:T(1,128)S(1)}, u32[]{:S(2)}, u32[]{:S(2)}) %collective-permute-start.45) | collective-permute-done | bytes 2592 | tf_op jit(solution)/shard_map/ppermute | solution.py:32
  254.0 5.8 collective-permute-start.47
  269.1 12.4 %collective-permute-done.49 = f32[5,1,128]{2,1,0:T(1,128)S(1)} collective-permute-done((f32[5,1,128]{2,1,0:T(1,128)S(1)}, f32[5,1,128]{2,1,0:T(1,128)S(1)}, u32[]{:S(2)}, u32[]{:S(2)}) %collective-permute-start.49) | collective-permute-done | bytes 2592 | tf_op jit(solution)/shard_map/ppermute | solution.py:32
  283.6 5.8 collective-permute-start.51
  315.9 10.3 %collective-permute-done.8 = f32[2,1,128]{2,1,0:T(1,128)S(1)} collective-permute-done((f32[2,1,128]{2,1,0:T(1,128)S(1)}, f32[2,1,128]{2,1,0:T(1,128)S(1)}, u32[]{:S(2)}, u32[]{:S(2)}) %collective-permute-start.8) | collective-permute-done | bytes 1056 | tf_op jit(solution)/shard_map/ppermute | solution.py:32
  331.3 5.8 collective-permute-start.10
  351.0 14.0 %collective-permute-done.63 = f32[5,1,128]{2,1,0:T(1,128)S(1)} collective-permute-done((f32[5,1,128]{2,1,0:T(1,128)S(1)}, f32[5,1,128]{2,1,0:T(1,128)S(1)}, u32[]{:S(2)}, u32[]{:S(2)}) %collective-permute-start.63) | collective-permute-done | bytes 2592 | tf_op jit(solution)/shard_map/ppermute | solution.py:32
  367.1 5.8 collective-permute-start.65
  382.8 12.4 %collective-permute-done.67 = f32[5,1,128]{2,1,0:T(1,128)S(1)} collective-permute-done((f32[5,1,128]{2,1,0:T(1,128)S(1)}, f32[5,1,128]{2,1,0:T(1,128)S(1)}, u32[]{:S(2)}, u32[]{:S(2)}) %collective-permute-start.67) | collective-permute-done | bytes 2592 | tf_op jit(solution)/shard_map/ppermute | solution.py:32
  397.2 5.9 collective-permute-start.69
  412.5 12.4 %collective-permute-done.71 = f32[5,1,128]{2,1,0:T(1,128)S(1)} collective-permute-done((f32[5,1,128]{2,1,0:T(1,128)S(1)}, f32[5,1,128]{2,1,0:T(1,128)S(1)}, u32[]{:S(2)}, u32[]{:S(2)}) %collective-permute-start.71) | collective-permute-done | bytes 2592 | tf_op jit(solution)/shard_map/ppermute | solution.py:32
  427.0 5.8 collective-permute-start.73
  445.9 10.3 %collective-permute-start.76 = (f32[1,4,5,8,128]{4,3,2,1,0:T(8,128)S(1)}, f32[1,4,5,8,128]{4,3,2,1,0:T(8,128)S(1)}, u32[]{:S(2)}, u32[]{:S(2)}) collective-permute-start(f32[1,4,5,8,128]{4,3,2,1,0:T(8,128)S(1)} %fusion.237), channel_id=1, source_target_pairs={{0,4},{1,5},{2,6},{3,7},{4,0},{5,1},{6,2},{7,3},{8,12},{9,13},{10,... | collective-permute-start | bytes 245768 | tf_op jit(solution)/shard_map/ppermute | solution.py:21
  464.1 10.3 %collective-permute-done.37 = f32[2,1,128]{2,1,0:T(1,128)S(1)} collective-permute-done((f32[2,1,128]{2,1,0:T(1,128)S(1)}, f32[2,1,128]{2,1,0:T(1,128)S(1)}, u32[]{:S(2)}, u32[]{:S(2)}) %collective-permute-start.37) | collective-permute-done | bytes 1056 | tf_op jit(solution)/shard_map/ppermute | solution.py:32
  499.2 14.0 %collective-permute-done.81 = f32[5,1,128]{2,1,0:T(1,128)S(1)} collective-permute-done((f32[5,1,128]{2,1,0:T(1,128)S(1)}, f32[5,1,128]{2,1,0:T(1,128)S(1)}, u32[]{:S(2)}, u32[]{:S(2)}) %collective-permute-start.81) | collective-permute-done | bytes 2592 | tf_op jit(solution)/shard_map/ppermute | solution.py:32
  531.0 12.3 %collective-permute-done.85 = f32[5,1,128]{2,1,0:T(1,128)S(1)} collective-permute-done((f32[5,1,128]{2,1,0:T(1,128)S(1)}, f32[5,1,128]{2,1,0:T(1,128)S(1)}, u32[]{:S(2)}, u32[]{:S(2)}) %collective-permute-start.85) | collective-permute-done | bytes 2592 | tf_op jit(solution)/shard_map/ppermute | solution.py:32
  557.6 12.7 %collective-permute-start.88 = (f32[5,1,128]{2,1,0:T(1,128)S(1)}, f32[5,1,128]{2,1,0:T(1,128)S(1)}, u32[]{:S(2)}, u32[]{:S(2)}) collective-permute-start(f32[5,1,128]{2,1,0:T(1,128)S(1)} %get-tuple-element.80), channel_id=1, source_target_pairs={{0,64},{64,128},{128,192},{192,256},{256,320},{320,384},{384,448},... | collective-permute-start | bytes 7688 | tf_op jit(solution)/shard_map/ppermute | solution.py:31
  572.3 14.3 %collective-permute-done.89 = f32[5,1,128]{2,1,0:T(1,128)S(1)} collective-permute-done((f32[5,1,128]{2,1,0:T(1,128)S(1)}, f32[5,1,128]{2,1,0:T(1,128)S(1)}, u32[]{:S(2)}, u32[]{:S(2)}) %collective-permute-start.89) | collective-permute-done | bytes 2592 | tf_op jit(solution)/shard_map/ppermute | solution.py:32
  (348 shorter events, 305.4 us)
Async XLA Ops:
  21.2 19.8 %collective-permute-start.6 = (f32[1,4,5,8,128]{4,3,2,1,0:T(8,128)S(1)}, f32[1,4,5,8,128]{4,3,2,1,0:T(8,128)S(1)}, u32[]{:S(2)}, u32[]{:S(2)}) collective-permute-start(f32[1,4,5,8,128]{4,3,2,1,0:T(8,128)S(1)} %fusion.225), channel_id=1, source_target_pairs={{0,4},{1,5},{2,6},{3,7},{4,0},{5,1},{6,2},{7,3},{8,12},{9,13},{10,... | collective-permute-start | bytes 245768 | tf_op jit(solution)/shard_map/ppermute | solution.py:21
  24.3 33.5 %collective-permute-start.14 = (f32[5,1,128]{2,1,0:T(1,128)S(1)}, f32[5,1,128]{2,1,0:T(1,128)S(1)}, u32[]{:S(2)}, u32[]{:S(2)}) collective-permute-start(f32[5,1,128]{2,1,0:T(1,128)S(1)} %get-tuple-element.116), channel_id=1, source_target_pairs={{0,64},{64,128},{128,192},{192,256},{256,320},{320,384},{384,448},... | collective-permute-start | bytes 7688 | tf_op jit(solution)/shard_map/ppermute | solution.py:31
  39.0 18.7 %collective-permute-start.15 = (f32[5,1,128]{2,1,0:T(1,128)S(1)}, f32[5,1,128]{2,1,0:T(1,128)S(1)}, u32[]{:S(2)}, u32[]{:S(2)}) collective-permute-start(f32[5,1,128]{2,1,0:T(1,128)S(1)} %get-tuple-element.117), channel_id=1, source_target_pairs={{64,0},{128,64},{192,128},{256,192},{320,256},{384,320},{448,384},... | collective-permute-start | bytes 7688 | tf_op jit(solution)/shard_map/ppermute | solution.py:32
  41.1 24.5 %collective-permute-start.18 = (f32[5,1,128]{2,1,0:T(1,128)S(1)}, f32[5,1,128]{2,1,0:T(1,128)S(1)}, u32[]{:S(2)}, u32[]{:S(2)}) collective-permute-start(f32[5,1,128]{2,1,0:T(1,128)S(1)} %get-tuple-element.120), channel_id=1, source_target_pairs={{0,64},{64,128},{128,192},{192,256},{256,320},{320,384},{384,448},... | collective-permute-start | bytes 7688 | tf_op jit(solution)/shard_map/ppermute | solution.py:31
  55.8 16.3 %collective-permute-start.19 = (f32[5,1,128]{2,1,0:T(1,128)S(1)}, f32[5,1,128]{2,1,0:T(1,128)S(1)}, u32[]{:S(2)}, u32[]{:S(2)}) collective-permute-start(f32[5,1,128]{2,1,0:T(1,128)S(1)} %get-tuple-element.121), channel_id=1, source_target_pairs={{64,0},{128,64},{192,128},{256,192},{320,256},{384,320},{448,384},... | collective-permute-start | bytes 7688 | tf_op jit(solution)/shard_map/ppermute | solution.py:32
  57.9 22.1 %collective-permute-start.16 = (f32[5,66,1]{2,1,0:T(8,128)S(1)}, f32[5,66,1]{2,1,0:T(8,128)S(1)}, u32[]{:S(2)}, u32[]{:S(2)}) collective-permute-start(f32[5,66,1]{2,1,0:T(8,128)S(1)} %get-tuple-element.74), channel_id=1, source_target_pairs={{0,1},{1,2},{2,3},{3,4},{4,5},{5,6},{6,7},{7,8},{8,9},{9,10},{10,1... | collective-permute-start | bytes 3968 | tf_op jit(solution)/shard_map/ppermute | solution.py:31
  59.8 20.2 %collective-permute-start.17 = (f32[5,66,1]{2,1,0:T(8,128)S(1)}, f32[5,66,1]{2,1,0:T(8,128)S(1)}, u32[]{:S(2)}, u32[]{:S(2)}) collective-permute-start(f32[5,66,1]{2,1,0:T(8,128)S(1)} %get-tuple-element.75), channel_id=1, source_target_pairs={{1,0},{2,1},{3,2},{4,3},{5,4},{6,5},{7,6},{8,7},{9,8},{10,9},{11,1... | collective-permute-start | bytes 3968 | tf_op jit(solution)/shard_map/ppermute | solution.py:32
  92.3 16.3 %collective-permute-start.23 = (f32[5,1,128]{2,1,0:T(1,128)S(1)}, f32[5,1,128]{2,1,0:T(1,128)S(1)}, u32[]{:S(2)}, u32[]{:S(2)}) collective-permute-start(f32[5,1,128]{2,1,0:T(1,128)S(1)} %get-tuple-element.113), channel_id=1, source_target_pairs={{64,0},{128,64},{192,128},{256,192},{320,256},{384,320},{448,384},... | collective-permute-start | bytes 7688 | tf_op jit(solution)/shard_map/ppermute | solution.py:32
  121.9 16.3 %collective-permute-start.27 = (f32[5,1,128]{2,1,0:T(1,128)S(1)}, f32[5,1,128]{2,1,0:T(1,128)S(1)}, u32[]{:S(2)}, u32[]{:S(2)}) collective-permute-start(f32[5,1,128]{2,1,0:T(1,128)S(1)} %get-tuple-element.111), channel_id=1, source_target_pairs={{64,0},{128,64},{192,128},{256,192},{320,256},{384,320},{448,384},... | collective-permute-start | bytes 7688 | tf_op jit(solution)/shard_map/ppermute | solution.py:32
  166.7 16.3 %collective-permute-start.1 = (f32[2,1,128]{2,1,0:T(1,128)S(1)}, f32[2,1,128]{2,1,0:T(1,128)S(1)}, u32[]{:S(2)}, u32[]{:S(2)}) collective-permute-start(f32[2,1,128]{2,1,0:T(1,128)S(1)} %get-tuple-element.155), channel_id=1, source_target_pairs={{64,0},{128,64},{192,128},{256,192},{320,256},{384,320},{448,384},... | collective-permute-start | bytes 3080 | tf_op jit(solution)/shard_map/ppermute | solution.py:32
  170.7 12.3 %collective-permute-start.33 = (f32[4,1,5,8,128]{4,3,2,0,1:T(8,128)S(1)}, f32[4,1,5,8,128]{4,3,2,0,1:T(8,128)S(1)}, u32[]{:S(2)}, u32[]{:S(2)}) collective-permute-start(f32[4,1,5,8,128]{4,3,2,0,1:T(8,128)S(1)} %fusion.229), channel_id=1, source_target_pairs={{0,1},{1,0},{2,3},{3,2},{4,5},{5,4},{6,7},{7,6},{8,9},{9,8},{10,11... | collective-permute-start | bytes 245768 | tf_op jit(solution)/shard_map/ppermute | solution.py:21
  205.5 16.3 %collective-permute-start.41 = (f32[5,1,128]{2,1,0:T(1,128)S(1)}, f32[5,1,128]{2,1,0:T(1,128)S(1)}, u32[]{:S(2)}, u32[]{:S(2)}) collective-permute-start(f32[5,1,128]{2,1,0:T(1,128)S(1)} %get-tuple-element.107), channel_id=1, source_target_pairs={{64,0},{128,64},{192,128},{256,192},{320,256},{384,320},{448,384},... | collective-permute-start | bytes 7688 | tf_op jit(solution)/shard_map/ppermute | solution.py:32
  235.6 16.3 %collective-permute-start.45 = (f32[5,1,128]{2,1,0:T(1,128)S(1)}, f32[5,1,128]{2,1,0:T(1,128)S(1)}, u32[]{:S(2)}, u32[]{:S(2)}) collective-permute-start(f32[5,1,128]{2,1,0:T(1,128)S(1)} %get-tuple-element.103), channel_id=1, source_target_pairs={{64,0},{128,64},{192,128},{256,192},{320,256},{384,320},{448,384},... | collective-permute-start | bytes 7688 | tf_op jit(solution)/shard_map/ppermute | solution.py:32
  265.2 16.3 %collective-permute-start.49 = (f32[5,1,128]{2,1,0:T(1,128)S(1)}, f32[5,1,128]{2,1,0:T(1,128)S(1)}, u32[]{:S(2)}, u32[]{:S(2)}) collective-permute-start(f32[5,1,128]{2,1,0:T(1,128)S(1)} %get-tuple-element.101), channel_id=1, source_target_pairs={{64,0},{128,64},{192,128},{256,192},{320,256},{384,320},{448,384},... | collective-permute-start | bytes 7688 | tf_op jit(solution)/shard_map/ppermute | solution.py:32
  309.9 16.3 %collective-permute-start.8 = (f32[2,1,128]{2,1,0:T(1,128)S(1)}, f32[2,1,128]{2,1,0:T(1,128)S(1)}, u32[]{:S(2)}, u32[]{:S(2)}) collective-permute-start(f32[2,1,128]{2,1,0:T(1,128)S(1)} %get-tuple-element.153), channel_id=1, source_target_pairs={{64,0},{128,64},{192,128},{256,192},{320,256},{384,320},{448,384},... | collective-permute-start | bytes 3080 | tf_op jit(solution)/shard_map/ppermute | solution.py:32
  313.9 12.3 %collective-permute-start.55 = (f32[4,1,5,8,128]{4,3,2,0,1:T(8,128)S(1)}, f32[4,1,5,8,128]{4,3,2,0,1:T(8,128)S(1)}, u32[]{:S(2)}, u32[]{:S(2)}) collective-permute-start(f32[4,1,5,8,128]{4,3,2,0,1:T(8,128)S(1)} %fusion.234), channel_id=1, source_target_pairs={{0,1},{1,0},{2,3},{3,2},{4,5},{5,4},{6,7},{7,6},{8,9},{9,8},{10,11... | collective-permute-start | bytes 245768 | tf_op jit(solution)/shard_map/ppermute | solution.py:21
  348.7 16.3 %collective-permute-start.63 = (f32[5,1,128]{2,1,0:T(1,128)S(1)}, f32[5,1,128]{2,1,0:T(1,128)S(1)}, u32[]{:S(2)}, u32[]{:S(2)}) collective-permute-start(f32[5,1,128]{2,1,0:T(1,128)S(1)} %get-tuple-element.97), channel_id=1, source_target_pairs={{64,0},{128,64},{192,128},{256,192},{320,256},{384,320},{448,384},... | collective-permute-start | bytes 7688 | tf_op jit(solution)/shard_map/ppermute | solution.py:32
  378.8 16.3 %collective-permute-start.67 = (f32[5,1,128]{2,1,0:T(1,128)S(1)}, f32[5,1,128]{2,1,0:T(1,128)S(1)}, u32[]{:S(2)}, u32[]{:S(2)}) collective-permute-start(f32[5,1,128]{2,1,0:T(1,128)S(1)} %get-tuple-element.93), channel_id=1, source_target_pairs={{64,0},{128,64},{192,128},{256,192},{320,256},{384,320},{448,384},... | collective-permute-start | bytes 7688 | tf_op jit(solution)/shard_map/ppermute | solution.py:32
  408.6 16.3 %collective-permute-start.71 = (f32[5,1,128]{2,1,0:T(1,128)S(1)}, f32[5,1,128]{2,1,0:T(1,128)S(1)}, u32[]{:S(2)}, u32[]{:S(2)}) collective-permute-start(f32[5,1,128]{2,1,0:T(1,128)S(1)} %get-tuple-element.91), channel_id=1, source_target_pairs={{64,0},{128,64},{192,128},{256,192},{320,256},{384,320},{448,384},... | collective-permute-start | bytes 7688 | tf_op jit(solution)/shard_map/ppermute | solution.py:32
  445.9 16.2 %collective-permute-start.76 = (f32[1,4,5,8,128]{4,3,2,1,0:T(8,128)S(1)}, f32[1,4,5,8,128]{4,3,2,1,0:T(8,128)S(1)}, u32[]{:S(2)}, u32[]{:S(2)}) collective-permute-start(f32[1,4,5,8,128]{4,3,2,1,0:T(8,128)S(1)} %fusion.237), channel_id=1, source_target_pairs={{0,4},{1,5},{2,6},{3,7},{4,0},{5,1},{6,2},{7,3},{8,12},{9,13},{10,... | collective-permute-start | bytes 245768 | tf_op jit(solution)/shard_map/ppermute | solution.py:21
  458.2 16.3 %collective-permute-start.37 = (f32[2,1,128]{2,1,0:T(1,128)S(1)}, f32[2,1,128]{2,1,0:T(1,128)S(1)}, u32[]{:S(2)}, u32[]{:S(2)}) collective-permute-start(f32[2,1,128]{2,1,0:T(1,128)S(1)} %get-tuple-element.151), channel_id=1, source_target_pairs={{64,0},{128,64},{192,128},{256,192},{320,256},{384,320},{448,384},... | collective-permute-start | bytes 3080 | tf_op jit(solution)/shard_map/ppermute | solution.py:32
  462.2 12.3 %collective-permute-start.77 = (f32[4,1,5,8,128]{4,3,2,0,1:T(8,128)S(1)}, f32[4,1,5,8,128]{4,3,2,0,1:T(8,128)S(1)}, u32[]{:S(2)}, u32[]{:S(2)}) collective-permute-start(f32[4,1,5,8,128]{4,3,2,0,1:T(8,128)S(1)} %fusion.239), channel_id=1, source_target_pairs={{0,1},{1,0},{2,3},{3,2},{4,5},{5,4},{6,7},{7,6},{8,9},{9,8},{10,11... | collective-permute-start | bytes 245768 | tf_op jit(solution)/shard_map/ppermute | solution.py:21
  497.0 16.3 %collective-permute-start.81 = (f32[5,1,128]{2,1,0:T(1,128)S(1)}, f32[5,1,128]{2,1,0:T(1,128)S(1)}, u32[]{:S(2)}, u32[]{:S(2)}) collective-permute-start(f32[5,1,128]{2,1,0:T(1,128)S(1)} %get-tuple-element.85), channel_id=1, source_target_pairs={{64,0},{128,64},{192,128},{256,192},{320,256},{384,320},{448,384},... | collective-permute-start | bytes 7688 | tf_op jit(solution)/shard_map/ppermute | solution.py:32
  527.1 16.3 %collective-permute-start.85 = (f32[5,1,128]{2,1,0:T(1,128)S(1)}, f32[5,1,128]{2,1,0:T(1,128)S(1)}, u32[]{:S(2)}, u32[]{:S(2)}) collective-permute-start(f32[5,1,128]{2,1,0:T(1,128)S(1)} %get-tuple-element.83), channel_id=1, source_target_pairs={{64,0},{128,64},{192,128},{256,192},{320,256},{384,320},{448,384},... | collective-permute-start | bytes 7688 | tf_op jit(solution)/shard_map/ppermute | solution.py:32
  543.5 13.6 %collective-permute-start.86 = (f32[5,66,1]{2,1,0:T(8,128)S(1)}, f32[5,66,1]{2,1,0:T(8,128)S(1)}, u32[]{:S(2)}, u32[]{:S(2)}) collective-permute-start(f32[5,66,1]{2,1,0:T(8,128)S(1)} %get-tuple-element.54), channel_id=1, source_target_pairs={{0,1},{1,2},{2,3},{3,4},{4,5},{5,6},{6,7},{7,8},{8,9},{9,10},{10,1... | collective-permute-start | bytes 3968 | tf_op jit(solution)/shard_map/ppermute | solution.py:31
  545.5 11.6 %collective-permute-start.87 = (f32[5,66,1]{2,1,0:T(8,128)S(1)}, f32[5,66,1]{2,1,0:T(8,128)S(1)}, u32[]{:S(2)}, u32[]{:S(2)}) collective-permute-start(f32[5,66,1]{2,1,0:T(8,128)S(1)} %get-tuple-element.55), channel_id=1, source_target_pairs={{1,0},{2,1},{3,2},{4,3},{5,4},{6,5},{7,6},{8,7},{9,8},{10,9},{11,1... | collective-permute-start | bytes 3968 | tf_op jit(solution)/shard_map/ppermute | solution.py:32
  551.2 21.0 %collective-permute-start.58 = (f32[2,1,128]{2,1,0:T(1,128)S(1)}, f32[2,1,128]{2,1,0:T(1,128)S(1)}, u32[]{:S(2)}, u32[]{:S(2)}) collective-permute-start(f32[2,1,128]{2,1,0:T(1,128)S(1)} %get-tuple-element.148), channel_id=1, source_target_pairs={{0,64},{64,128},{128,192},{192,256},{256,320},{320,384},{384,448},... | collective-permute-start | bytes 3080 | tf_op jit(solution)/shard_map/ppermute | solution.py:31
  553.2 19.1 %collective-permute-start.59 = (f32[2,1,128]{2,1,0:T(1,128)S(1)}, f32[2,1,128]{2,1,0:T(1,128)S(1)}, u32[]{:S(2)}, u32[]{:S(2)}) collective-permute-start(f32[2,1,128]{2,1,0:T(1,128)S(1)} %get-tuple-element.149), channel_id=1, source_target_pairs={{64,0},{128,64},{192,128},{256,192},{320,256},{384,320},{448,384},... | collective-permute-start | bytes 3080 | tf_op jit(solution)/shard_map/ppermute | solution.py:32
  557.6 14.7 %collective-permute-start.88 = (f32[5,1,128]{2,1,0:T(1,128)S(1)}, f32[5,1,128]{2,1,0:T(1,128)S(1)}, u32[]{:S(2)}, u32[]{:S(2)}) collective-permute-start(f32[5,1,128]{2,1,0:T(1,128)S(1)} %get-tuple-element.80), channel_id=1, source_target_pairs={{0,64},{64,128},{128,192},{192,256},{256,320},{320,384},{384,448},... | collective-permute-start | bytes 7688 | tf_op jit(solution)/shard_map/ppermute | solution.py:31
  570.3 16.3 %collective-permute-start.89 = (f32[5,1,128]{2,1,0:T(1,128)S(1)}, f32[5,1,128]{2,1,0:T(1,128)S(1)}, u32[]{:S(2)}, u32[]{:S(2)}) collective-permute-start(f32[5,1,128]{2,1,0:T(1,128)S(1)} %get-tuple-element.81), channel_id=1, source_target_pairs={{64,0},{128,64},{192,128},{256,192},{320,256},{384,320},{448,384},... | collective-permute-start | bytes 7688 | tf_op jit(solution)/shard_map/ppermute | solution.py:32
  586.8 15.5 %collective-permute-start.90 = (f32[5,66,1]{2,1,0:T(8,128)S(1)}, f32[5,66,1]{2,1,0:T(8,128)S(1)}, u32[]{:S(2)}, u32[]{:S(2)}) collective-permute-start(f32[5,66,1]{2,1,0:T(8,128)S(1)} %get-tuple-element.52), channel_id=1, source_target_pairs={{0,1},{1,2},{2,3},{3,4},{4,5},{5,6},{6,7},{7,8},{8,9},{9,10},{10,1... | collective-permute-start | bytes 3968 | tf_op jit(solution)/shard_map/ppermute | solution.py:31
  588.7 13.5 %collective-permute-start.91 = (f32[5,66,1]{2,1,0:T(8,128)S(1)}, f32[5,66,1]{2,1,0:T(8,128)S(1)}, u32[]{:S(2)}, u32[]{:S(2)}) collective-permute-start(f32[5,66,1]{2,1,0:T(8,128)S(1)} %get-tuple-element.53), channel_id=1, source_target_pairs={{1,0},{2,1},{3,2},{4,3},{5,4},{6,5},{7,6},{8,7},{9,8},{10,9},{11,1... | collective-permute-start | bytes 3968 | tf_op jit(solution)/shard_map/ppermute | solution.py:32
  (67 other events, 516.9 us)
where the time goes:
time: 624 us; the launch traced here: 621 us
  starting transfers between devices  342 us (55%)
  waiting for transfers between devices  262 us (42%)
  other arithmetic  10.5 us (2%)
    ppermute x34, waiting for transfers between devices, with_halo(): after = lax.ppermute(leading, axis, down)  200 us
    ppermute x34, starting transfers between devices, with_halo(): after = lax.ppermute(leading, axis, down)  152 us
    ppermute x34, starting transfers between devices, with_halo(): before = lax.ppermute(last, axis, up)  113 us
    ppermute x27, starting transfers between devices, swapped(): lax.ppermute(value, axis, [(i, i ^ 1 << distance) for i in range(lax.axis...  77.2 us
    ppermute x27, waiting for transfers between devices, swapped(): lax.ppermute(value, axis, [(i, i ^ 1 << distance) for i in range(lax.axis...  49 us
  transfers between devices with their start and end apart: 95, of which 50 were waited for; matrix products, arithmetic and copies ran while one was open for 1% of the time, Pallas kernels for 0%

commit v1 on v0

v1 whole, which is shorter than its diff:
```python
import math

import jax
import jax.numpy as jnp
from jax import lax
from jax.experimental import pallas as pl
from jax.experimental.pallas import tpu as pltpu
from jax.sharding import Mesh
from jax.sharding import PartitionSpec as P

SWEEPS = 3
STEPS = 4
STORAGE = 0.3
ROUTING = 0.15
LEAKANCE = 0.25
SPECTRUM_MID = 1.025
SPECTRUM_HALF = 0.975

LAYERS = 5
GROUP = 8
HALO = SWEEPS * STEPS
SOIL = 2 * LAYERS
FIELDS = SOIL + 3
SUB = 8
LANES = 128
ROWS = 64
OFF = 24
TALL = OFF + ROWS + 24
STRIP = FIELDS * HALO + 3 * HALO


def sweep_factors(number):
    return [
        1.0
        / (SPECTRUM_MID - SPECTRUM_HALF * math.cos(math.pi * (2 * k + 1) / (2 * number)))
        for k in range(number)
    ]


def lane_index(rows):
    return lax.broadcasted_iota(jnp.int32, (rows, LANES), 1)


def turn(value, shift):
    shift %= LANES
    return pltpu.roll(value, shift, 1) if shift else value


def own_rows(soil, depth, elevation, mask, field, p):
    if field < SOIL:
        return soil[p, field]
    rows = pl.ds(p * SUB, SUB)
    return (depth, elevation, mask)[field - SOIL][rows, :].astype(jnp.float32)


def pack_columns(soil, depth, elevation, mask, left, right):
    lane = lane_index(SUB)
    for p in range(GROUP):
        for plane, fields in ((0, range(SOIL)), (1, range(SOIL, FIELDS))):
            lefts = jnp.zeros((SUB, LANES), jnp.float32)
            rights = jnp.zeros((SUB, LANES), jnp.float32)
            for slot, field in enumerate(fields):
                value = own_rows(soil, depth, elevation, mask, field, p)
                here = (lane >= slot * HALO) & (lane < slot * HALO + HALO)
                lefts = jnp.where(here, turn(value, slot * HALO), lefts)
                rights = jnp.where(here, turn(value, slot * HALO + HALO), rights)
            left[plane, pl.ds(p * SUB, SUB), :] = lefts
            right[plane, pl.ds(p * SUB, SUB), :] = rights


def pack_rows(soil, depth, elevation, mask, from_left, from_right, top, bottom):
    half = HALO - SUB
    for field in range(FIELDS):
        at = field * HALO
        get = lambda p: own_rows(soil, depth, elevation, mask, field, p)
        top[pl.ds(at, SUB), :] = get(0)
        top[pl.ds(at + SUB, half), :] = get(1)[:half]
        bottom[pl.ds(at, half), :] = get(GROUP - 2)[SUB - half :]
        bottom[pl.ds(at + half, SUB), :] = get(GROUP - 1)
    lane = lane_index(HALO)
    for out, first in ((top, 0), (bottom, ROWS - HALO)):
        rows = pl.ds(first, HALO)
        out[pl.ds(FIELDS * HALO, HALO), :] = from_left[0, rows, :]
        out[pl.ds((FIELDS + 1) * HALO, HALO), :] = from_right[0, rows, :]
        out[pl.ds((FIELDS + 2) * HALO, HALO), :] = jnp.where(
            lane < 64, from_left[1, rows, :], turn(from_right[1, rows, :], 64)
        )


def beside(one, two, lane):
    r1, r2 = turn(one, -1), turn(two, -1)
    l1, l2 = turn(one, 1), turn(two, 1)
    last, first = lane == LANES - 1, lane == 0
    right = (jnp.where(last, r2, r1), jnp.where(last, r1, r2))
    left = (jnp.where(first, l2, l1), jnp.where(first, l1, l2))
    return right, left


def march(
    soil, depth_in, elevation_in, mask_in, from_left, from_right, above, below,
    depth_out, pressure_out,
    K, U, X, Y, C, east, west, south, down, inverse, side, D, E, M, H, B,
):
    factors = sweep_factors(SWEEPS)
    zeros = jnp.zeros((SUB, LANES), jnp.float32)
    for plane in range(2):
        for row in (0, TALL - SUB):
            rows = pl.ds(row, SUB)
            for ref in (X, Y, C, south, K, U):
                for layer in range(LAYERS):
                    ref[plane, layer, rows, :] = zeros
            for ref in (D, E, M, H, B):
                ref[plane, rows, :] = zeros
        for row in (SUB, TALL - 2 * SUB):
            rows = pl.ds(row, SUB)
            for ref in (K, U):
                for layer in range(LAYERS):
                    ref[plane, layer, rows, :] = zeros
            for ref in (D, E, M):
                ref[plane, rows, :] = zeros

    def target(field):
        if field < LAYERS:
            return lambda plane, rows: U.at[plane, field, rows, :]
        if field < SOIL:
            return lambda plane, rows: K.at[plane, field - LAYERS, rows, :]
        ref = (D, E, M)[field - SOIL]
        return lambda plane, rows: ref.at[plane, rows, :]

    def spread(lefts, rights, lane, slot, shift=0):
        return jnp.where(
            lane < HALO,
            turn(rights, -slot * HALO - shift),
            jnp.where(lane >= LANES - HALO, turn(lefts, LANES - HALO - slot * HALO), 0.0),
        )

    lane = lane_index(SUB)
    lane_halo = lane_index(HALO)
    for field in range(FIELDS):
        at = target(field)
        slot, plane_in = (field, 0) if field < SOIL else (field - SOIL, 1)
        for p in range(GROUP):
            rows = pl.ds(OFF + p * SUB, SUB)
            at(0, rows)[...] = own_rows(soil, depth_in, elevation_in, mask_in, field, p)
            here = pl.ds(p * SUB, SUB)
            at(1, rows)[...] = spread(
                from_left[plane_in, here, :], from_right[plane_in, here, :], lane, slot
            )
        for packed, first in ((above, OFF - HALO), (below, OFF + ROWS)):
            rows = pl.ds(first, HALO)
            at(0, rows)[...] = packed[pl.ds(field * HALO, HALO), :]
            if field < SOIL:
                lefts = packed[pl.ds(FIELDS * HALO, HALO), :]
                rights = packed[pl.ds((FIELDS + 1) * HALO, HALO), :]
                at(1, rows)[...] = spread(lefts, rights, lane_halo, slot)
            else:
                both = packed[pl.ds((FIELDS + 2) * HALO, HALO), :]
                at(1, rows)[...] = spread(both, both, lane_halo, slot, 64)

    wide = 2 * SUB
    lane2 = lane_index(wide)

    def step(number, carry):
        low = jnp.where(number == 0, SUB, 2 * SUB)
        trips = jnp.where(number == 0, 6, 5)

        def begin(i, carry):
            row = pl.multiple_of(SUB + wide * i, SUB)
            rows = pl.ds(row, wide)
            for plane in range(2):
                depth = D[plane, rows, :]
                H[plane, rows, :] = depth + E[plane, rows, :]
                B[plane, rows, :] = jnp.where(
                    K[plane, 0, rows, :] > 0, 1.0 + 0.5 * jnp.tanh(depth), 0.0
                )
                for layer in range(LAYERS):
                    u = U[plane, layer, rows, :]
                    C[plane, layer, rows, :] = 0.5 * K[plane, layer, rows, :] / (1.0 + u * u)
            return carry

        lax.fori_loop(0, 6, begin, 0)

        def first(i, carry):
            row = pl.multiple_of(low + wide * i, SUB)
            rows, before, after = pl.ds(row, wide), pl.ds(row - 1, wide), pl.ds(row + 1, wide)
            head = [H[plane, rows, :] for plane in range(2)]
            mobile = [B[plane, rows, :] for plane in range(2)]
            head_sides = beside(*head, lane2)
            mobile_sides = beside(*mobile, lane2)
            flux = []
            for plane in range(2):
                depth = D[plane, rows, :]
                now = LEAKANCE * (depth - U[plane, 0, rows, :])
                flux.append(now)
                change = jnp.zeros_like(depth)
                for other_head, other_mobile in (
                    (H[plane, after, :], B[plane, after, :]),
                    (H[plane, before, :], B[plane, before, :]),
                    (head_sides[0][plane], mobile_sides[0][plane]),
                    (head_sides[1][plane], mobile_sides[1][plane]),
                ):
                    change = change + (mobile[plane] + other_mobile) * (other_head - head[plane])
                D[plane, rows, :] = M[plane, rows, :] * (depth + (0.5 * ROUTING) * change - now)
            conduct = [[C[plane, layer, rows, :] for layer in range(LAYERS)] for plane in range(2)]
            iterate = [[U[plane, layer, rows, :] for layer in range(LAYERS)] for plane in range(2)]
            between = [
                [2.0 * (conduct[plane][l] + conduct[plane][l + 1]) for l in range(LAYERS - 1)]
                for plane in range(2)
            ]
            for layer in range(LAYERS):
                c_right, c_left = beside(conduct[0][layer], conduct[1][layer], lane2)
                u_right, u_left = beside(iterate[0][layer], iterate[1][layer], lane2)
                for plane in range(2):
                    c, u = conduct[plane][layer], iterate[plane][layer]
                    e, w = c + c_right[plane], c + c_left[plane]
                    s, n = c + C[plane, layer, after, :], c + C[plane, layer, before, :]
                    diagonal = STORAGE + e + w + s + n
                    total = STORAGE * u
                    if layer == 0:
                        total = total + flux[plane]
                    side[plane, layer, rows, :] = total
                    total = total + e * u_right[plane] + w * u_left[plane]
                    total = total + s * U[plane, layer, after, :] + n * U[plane, layer, before, :]
                    if layer > 0:
                        diagonal = diagonal + between[plane][layer - 1]
                        total = total + between[plane][layer - 1] * iterate[plane][layer - 1]
                    if layer < LAYERS - 1:
                        diagonal = diagonal + between[plane][layer]
                        total = total + between[plane][layer] * iterate[plane][layer + 1]
                        down[plane, layer, rows, :] = between[plane][layer]
                    inv = jnp.where(K[plane, layer, rows, :] > 0, 1.0 / diagonal, 0.0)
                    east[plane, layer, rows, :] = e
                    west[plane, layer, rows, :] = w
                    south[plane, layer, rows, :] = s
                    inverse[plane, layer, rows, :] = inv
                    X[plane, layer, rows, :] = (1.0 - factors[0]) * u + factors[0] * (inv * total)
            return carry

        lax.fori_loop(0, trips, first, 0)

        def sweep(source, goal, factor):
            def body(i, carry):
                row = pl.multiple_of(low + wide * i, SUB)
                rows, before, after = pl.ds(row, wide), pl.ds(row - 1, wide), pl.ds(row + 1, wide)
                iterate = [
                    [source[plane, layer, rows, :] for layer in range(LAYERS)] for plane in range(2)
                ]
                between = [
                    [down[plane, layer, rows, :] for layer in range(LAYERS - 1)]
                    for plane in range(2)
                ]
                for layer in range(LAYERS):
                    u_right, u_left = beside(iterate[0][layer], iterate[1][layer], lane2)
                    for plane in range(2):
                        u = iterate[plane][layer]
                        total = side[plane, layer, rows, :]
                        total = total + east[plane, layer, rows, :] * u_right[plane]
                        total = total + west[plane, layer, rows, :] * u_left[plane]
                        total = total + south[plane, layer, rows, :] * source[plane, layer, after, :]
                        total = total + south[plane, layer, before, :] * source[plane, layer, before, :]
                        if layer > 0:
                            total = total + between[plane][layer - 1] * iterate[plane][layer - 1]
                        if layer < LAYERS - 1:
                            total = total + between[plane][layer] * iterate[plane][layer + 1]
                        inv = inverse[plane, layer, rows, :]
                        goal[plane, layer, rows, :] = (1.0 - factor) * u + factor * (inv * total)
                return carry

            lax.fori_loop(0, trips, body, 0)

        sweep(X, Y, factors[1])
        sweep(Y, U, factors[2])
        return carry

    lax.fori_loop(0, STEPS, step, 0)
    depth_out[...] = D[0, pl.ds(OFF, ROWS), :]
    for p in range(GROUP):
        for layer in range(LAYERS):
            pressure_out[p, layer] = U[0, layer, pl.ds(OFF + p * SUB, SUB), :]


def call(kernel, outs, scratch, *args):
    vmem = pl.BlockSpec(memory_space=pltpu.VMEM)
    return pl.pallas_call(
        kernel,
        out_shape=[jax.ShapeDtypeStruct(shape, jnp.float32) for shape in outs],
        in_specs=[vmem] * len(args),
        out_specs=[vmem] * len(outs),
        scratch_shapes=[pltpu.VMEM(shape, jnp.float32) for shape in scratch],
        compiler_params=pltpu.CompilerParams(vmem_limit_bytes=32 << 20),
    )(*args)


def solution(mesh):
    secs, tiles = mesh.shape["sec"], mesh.shape["tile"]
    axes = ("sec", "band", "place")
    parts = Mesh(mesh.devices.reshape(secs, tiles // GROUP, GROUP), axes)

    def pairs(along, odd):
        found = []
        for s in range(secs):
            for t in range(tiles):
                index, count = (s, secs) if along == "sec" else (t, tiles)
                other = index + 1 if index % 2 == odd else index - 1
                if 0 <= other < count:
                    goal = (other, t) if along == "sec" else (s, other)
                    found.append((s * tiles + t, goal[0] * tiles + goal[1]))
        return found

    def swap(value, along, odd):
        return lax.ppermute(value, axes, pairs(along, odd))

    def local(depth, elevation, land_mask, pressure, conductance):
        tile_odd = lax.axis_index("place") % 2 == 1
        sec_odd = lax.axis_index("sec") % 2 == 1
        blocks = jnp.concatenate([pressure[:, 0], conductance[:, 0]], 0)
        pieces = jnp.moveaxis(blocks.reshape(SOIL, SUB, GROUP, LANES), 2, 0)
        soil = lax.all_to_all(pieces, "place", 0, 0)
        own = (soil, depth, elevation, land_mask)
        left, right = call(pack_columns, [(2, ROWS, LANES)] * 2, [], *own)
        one = swap(jnp.where(tile_odd, left, right), "tile", 0)
        two = swap(jnp.where(tile_odd, right, left), "tile", 1)
        from_left = jnp.where(tile_odd, one, two)
        from_right = jnp.where(tile_odd, two, one)
        top, bottom = call(pack_rows, [(STRIP, LANES)] * 2, [], *own, from_left, from_right)
        one = swap(jnp.where(sec_odd, bottom, top), "sec", 1)
        two = swap(jnp.where(sec_odd, top, bottom), "sec", 0)
        above = jnp.where(sec_odd, two, one)
        below = jnp.where(sec_odd, one, two)
        field, layer = (2, LAYERS, TALL, LANES), (2, TALL, LANES)
        depth, soil = call(
            march,
            [(ROWS, LANES), (GROUP, LAYERS, SUB, LANES)],
            [field] * 11 + [layer] * 5,
            *own, from_left, from_right, above, below,
        )
        soil = lax.all_to_all(soil, "place", 0, 0)
        return depth, jnp.moveaxis(soil, 0, 2).reshape(LAYERS, 1, SUB, GROUP * LANES)

    surface = P("sec", ("band", "place"))
    blocked = P(None, axes, None, None)
    return jax.shard_map(
        local,
        mesh=parts,
        in_specs=(surface, surface, surface, blocked, blocked),
        out_specs=(surface, blocked),
        check_vma=False,
    )
```

time: 624 us -> 68.9 us (0.11)
  the two profiles are of different devices: /device:TPU:38 before, /device:TPU:448 now
where the time goes in v1:
time: 68.9 us; the launch traced here: 68.5 us
  waiting for transfers between devices  24.8 us (36%)
  starting transfers between devices  18.7 us (27%)
  Pallas kernels  11.4 us (17%)
  blocking collectives  9.55 us (14%)
  local copies, waits for them, and re-layouts  2.66 us (4%)
  other arithmetic  0.8 us (1%)
  between operations  0.74 us (1%)
    ppermute x4, waiting for transfers between devices, swap(): return lax.ppermute(value, axes, pairs(along, odd))  16.5 us
    ppermute x4, starting transfers between devices, swap(): return lax.ppermute(value, axes, pairs(along, odd))  14.1 us
    pallas_call x3, Pallas kernels, call(): pl.pallas_call(kernel, out_shape=[jax.ShapeDtypeStruct(shape, jnp.float32...  11.4 us
    all_to_all x1, blocking collectives, local(): soil = lax.all_to_all(soil, 'place', 0, 0)  9.55 us
    all_to_all x1, waiting for transfers between devices, local(): soil = lax.all_to_all(pieces, 'place', 0, 0)  8.24 us
    all_to_all x1, starting transfers between devices, local(): soil = lax.all_to_all(pieces, 'place', 0, 0)  4.6 us
    unnamed x10, local copies, waits for them, and re-layouts  1.86 us
  transfers between devices with their start and end apart: 5, of which 3 were waited for; matrix products, arithmetic and copies ran while one was open for 0% of the time, Pallas kernels for 0%

profile of v1, /device:TPU:448, one launch (start us, length us, event | category | flops | bytes accessed | tf_op | source)
XLA Modules:
  0.0 68.5 jit_solution(2195184499067831591)
XLA Ops:
  0.6 0.9 %copy.16 = f32[5,8,8,128]{3,2,1,0:T(8,128)S(1)} copy(f32[5,8,8,128]{3,1,2,0:T(8,128)} %bitcast.21) | data formatting | bytes 327680
  1.6 0.0 copy-start.3
  1.6 0.9 %copy-done.3 = f32[5,1,8,1024]{3,2,1,0:T(8,128)S(1)} copy-done((f32[5,1,8,1024]{3,2,1,0:T(8,128)S(1)}, f32[5,1,8,1024]{3,2,1,0:T(8,128)}, u32[]{:S(2)}) %copy-start.3) | copy-done | bytes 163864
  2.6 0.7 %maximum_bitcast_fusion = f32[8,10,8,128]{3,2,1,0:T(8,128)} fusion(f32[5,8,8,128]{3,1,0,2:T(8,128)S(1)} %copy.8, f32[5,8,8,128]{3,1,0,2:T(8,128)S(1)} %copy.7), kind=kLoop, calls=%fused_computation | loop fusion | flops 81920 | bytes 655360 | tf_op jit(solution)/shard_map/transpose | solution.py:317
  3.3 0.0 copy-start
  3.3 0.0 copy-start.1
  3.3 0.0 copy-start.2
  3.3 4.6 %all-to-all-start = ((f32[8,10,8,128]{3,2,1,0:T(8,128)}), f32[8,10,8,128]{3,2,1,0:T(8,128)S(1)}, u32[]{:S(2)}, u32[]{:S(2)}) async-start(f32[8,10,8,128]{3,2,1,0:T(8,128)} %maximum_bitcast_fusion), calls=%async_computation | async-start | bytes 655360 | tf_op jit(solution)/shard_map/all_to_all | solution.py:318
  7.9 8.2 %all-to-all-done.soil = f32[8,10,8,128]{3,2,1,0:T(8,128)S(1)} async-done(((f32[8,10,8,128]{3,2,1,0:T(8,128)}), f32[8,10,8,128]{3,2,1,0:T(8,128)S(1)}, u32[]{:S(2)}, u32[]{:S(2)}) %all-to-all-start) | async-done | bytes 327712 | tf_op jit(solution)/shard_map/all_to_all | solution.py:318
  16.2 0.0 copy-done
  16.2 0.0 copy-done.1
  16.2 0.0 copy-done.2
  16.2 0.3 shard_map.68
  16.5 2.5 %collective-permute-start.1 = (f32[2,64,128]{2,1,0:T(8,128)S(1)}, f32[2,64,128]{2,1,0:T(8,128)S(1)}, u32[]{:S(2)}, u32[]{:S(2)}) collective-permute-start(f32[2,64,128]{2,1,0:T(8,128)S(1)} %get-tuple-element.22), channel_id=1, source_target_pairs={{1,2},{2,1},{3,4},{4,3},{5,6},{6,5},{7,8},{8,7},{9,10},{10,9},{11,... | collective-permute-start | bytes 196616 | tf_op jit(solution)/shard_map/ppermute | solution.py:311
  19.0 2.0 %collective-permute-start = (f32[2,64,128]{2,1,0:T(8,128)S(1)}, f32[2,64,128]{2,1,0:T(8,128)S(1)}, u32[]{:S(2)}, u32[]{:S(2)}) collective-permute-start(f32[2,64,128]{2,1,0:T(8,128)S(1)} %get-tuple-element.23), channel_id=1, source_target_pairs={{0,1},{1,0},{2,3},{3,2},{4,5},{5,4},{6,7},{7,6},{8,9},{9,8},{10,11... | collective-permute-start | bytes 196616 | tf_op jit(solution)/shard_map/ppermute | solution.py:311
  21.0 3.2 %collective-permute-done.1 = f32[2,64,128]{2,1,0:T(8,128)S(1)} collective-permute-done((f32[2,64,128]{2,1,0:T(8,128)S(1)}, f32[2,64,128]{2,1,0:T(8,128)S(1)}, u32[]{:S(2)}, u32[]{:S(2)}) %collective-permute-start.1) | collective-permute-done | bytes 65568 | tf_op jit(solution)/shard_map/ppermute | solution.py:311
  24.2 0.0 collective-permute-done
  24.2 0.1 shard_map.69
  24.3 7.6 %collective-permute-start.3 = (f32[192,128]{1,0:T(8,128)S(1)}, f32[192,128]{1,0:T(8,128)S(1)}, u32[]{:S(2)}, u32[]{:S(2)}) collective-permute-start(f32[192,128]{1,0:T(8,128)S(1)} %get-tuple-element.18), channel_id=1, source_target_pairs={{64,128},{65,129},{66,130},{67,131},{68,132},{69,133},{70,134},{71... | collective-permute-start | bytes 294920 | tf_op jit(solution)/shard_map/ppermute | solution.py:311
  31.9 1.9 %collective-permute-start.2 = (f32[192,128]{1,0:T(8,128)S(1)}, f32[192,128]{1,0:T(8,128)S(1)}, u32[]{:S(2)}, u32[]{:S(2)}) collective-permute-start(f32[192,128]{1,0:T(8,128)S(1)} %get-tuple-element.19), channel_id=1, source_target_pairs={{0,64},{1,65},{2,66},{3,67},{4,68},{5,69},{6,70},{7,71},{8,72},{9,... | collective-permute-start | bytes 294920 | tf_op jit(solution)/shard_map/ppermute | solution.py:311
  33.9 13.3 %collective-permute-done.3 = f32[192,128]{1,0:T(8,128)S(1)} collective-permute-done((f32[192,128]{1,0:T(8,128)S(1)}, f32[192,128]{1,0:T(8,128)S(1)}, u32[]{:S(2)}, u32[]{:S(2)}) %collective-permute-start.3) | collective-permute-done | bytes 98336 | tf_op jit(solution)/shard_map/ppermute | solution.py:311
  47.2 0.0 collective-permute-done.2
  47.2 11.0 %shard_map.70 = (f32[64,128]{1,0:T(8,128)}, f32[8,5,8,128]{3,2,1,0:T(8,128)S(1)}) custom-call(f32[8,10,8,128]{3,2,1,0:T(8,128)S(1)} %all-to-all-done.soil, f32[64,128]{1,0:T(8,128)S(1)} %copy-done, f32[64,128]{1,0:T(8,128)S(1)} %copy-done.1, s32[64,128]{1,0:T(8,128)S(1)} %copy-done.2, f32[2,64,128]{2,1,0:T(8,128)S(1)} %get-tuple-element.21.from_left, ...), custom_call_target="tpu_custom_call" | custom-call | tf_op jit(solution)/shard_map/pallas_call | solution.py:284
  58.2 9.6 %all_to_all.10 = f32[8,5,8,128]{3,2,1,0:T(8,128)S(1)} all-to-all(f32[8,5,8,128]{3,2,1,0:T(8,128)S(1)} %get-tuple-element.13), channel_id=1, replica_groups=mesh['sec'=8,'band'=8,'place'=8] {'place'}, dimensions={0} | all-to-all | bytes 327680 | tf_op jit(solution)/shard_map/all_to_all | solution.py:337
  67.8 0.7 %reshape.12 = f32[5,1,8,1024]{3,2,0,1:T(8,128)} reshape(f32[5,8,8,128]{3,2,1,0:T(8,128)S(1)} %copy.9) | data formatting | bytes 327680 | tf_op jit(solution)/shard_map/reshape | solution.py:338
  (8 shorter events, 0.2 us)
Async XLA Ops:
  1.6 0.9 %copy-start.3 = (f32[5,1,8,1024]{3,2,1,0:T(8,128)S(1)}, f32[5,1,8,1024]{3,2,1,0:T(8,128)}, u32[]{:S(2)}) copy-start(f32[5,1,8,1024]{3,2,1,0:T(8,128)} %param.9) | copy-start | bytes 491524
  3.3 12.9 %copy-start = (f32[64,128]{1,0:T(8,128)S(1)}, f32[64,128]{1,0:T(8,128)}, u32[]{:S(2)}) copy-start(f32[64,128]{1,0:T(8,128)} %depth_in.1) | copy-start | bytes 98308
  3.3 12.9 %copy-start.1 = (f32[64,128]{1,0:T(8,128)S(1)}, f32[64,128]{1,0:T(8,128)}, u32[]{:S(2)}) copy-start(f32[64,128]{1,0:T(8,128)} %elevation_in.1) | copy-start | bytes 98308
  3.3 12.9 %copy-start.2 = (s32[64,128]{1,0:T(8,128)S(1)}, s32[64,128]{1,0:T(8,128)}, u32[]{:S(2)}) copy-start(s32[64,128]{1,0:T(8,128)} %mask_in.1) | copy-start | bytes 98308
  3.3 12.8 %all-to-all-start = ((f32[8,10,8,128]{3,2,1,0:T(8,128)}), f32[8,10,8,128]{3,2,1,0:T(8,128)S(1)}, u32[]{:S(2)}, u32[]{:S(2)}) async-start(f32[8,10,8,128]{3,2,1,0:T(8,128)} %maximum_bitcast_fusion), calls=%async_computation | async-start | bytes 655360 | tf_op jit(solution)/shard_map/all_to_all | solution.py:318
  16.5 7.7 %collective-permute-start.1 = (f32[2,64,128]{2,1,0:T(8,128)S(1)}, f32[2,64,128]{2,1,0:T(8,128)S(1)}, u32[]{:S(2)}, u32[]{:S(2)}) collective-permute-start(f32[2,64,128]{2,1,0:T(8,128)S(1)} %get-tuple-element.22), channel_id=1, source_target_pairs={{1,2},{2,1},{3,4},{4,3},{5,6},{6,5},{7,8},{8,7},{9,10},{10,9},{11,... | collective-permute-start | bytes 196616 | tf_op jit(solution)/shard_map/ppermute | solution.py:311
  19.0 5.2 %collective-permute-start = (f32[2,64,128]{2,1,0:T(8,128)S(1)}, f32[2,64,128]{2,1,0:T(8,128)S(1)}, u32[]{:S(2)}, u32[]{:S(2)}) collective-permute-start(f32[2,64,128]{2,1,0:T(8,128)S(1)} %get-tuple-element.23), channel_id=1, source_target_pairs={{0,1},{1,0},{2,3},{3,2},{4,5},{5,4},{6,7},{7,6},{8,9},{9,8},{10,11... | collective-permute-start | bytes 196616 | tf_op jit(solution)/shard_map/ppermute | solution.py:311
  24.3 22.9 %collective-permute-start.3 = (f32[192,128]{1,0:T(8,128)S(1)}, f32[192,128]{1,0:T(8,128)S(1)}, u32[]{:S(2)}, u32[]{:S(2)}) collective-permute-start(f32[192,128]{1,0:T(8,128)S(1)} %get-tuple-element.18), channel_id=1, source_target_pairs={{64,128},{65,129},{66,130},{67,131},{68,132},{69,133},{70,134},{71... | collective-permute-start | bytes 294920 | tf_op jit(solution)/shard_map/ppermute | solution.py:311
  31.9 15.3 %collective-permute-start.2 = (f32[192,128]{1,0:T(8,128)S(1)}, f32[192,128]{1,0:T(8,128)S(1)}, u32[]{:S(2)}, u32[]{:S(2)}) collective-permute-start(f32[192,128]{1,0:T(8,128)S(1)} %get-tuple-element.19), channel_id=1, source_target_pairs={{0,64},{1,65},{2,66},{3,67},{4,68},{5,69},{6,70},{7,71},{8,72},{9,... | collective-permute-start | bytes 294920 | tf_op jit(solution)/shard_map/ppermute | solution.py:311

commit v2 on v1

v2 whole, which is shorter than its diff:
```python
import math

import jax
import jax.numpy as jnp
from jax import lax
from jax.experimental import pallas as pl
from jax.experimental.pallas import tpu as pltpu
from jax.sharding import Mesh
from jax.sharding import PartitionSpec as P

SWEEPS = 3
STEPS = 4
STORAGE = 0.3
ROUTING = 0.15
LEAKANCE = 0.25
SPECTRUM_MID = 1.025
SPECTRUM_HALF = 0.975

LAYERS = 5
GROUP = 8
HALO = SWEEPS * STEPS
SOIL = 2 * LAYERS
FIELDS = SOIL + 3
SUB = 8
LANES = 128
ROWS = 64
STRIP = FIELDS * HALO + 3 * HALO


def sweep_factors(number):
    return [
        1.0
        / (SPECTRUM_MID - SPECTRUM_HALF * math.cos(math.pi * (2 * k + 1) / (2 * number)))
        for k in range(number)
    ]


def lane_index(rows):
    return lax.broadcasted_iota(jnp.int32, (rows, LANES), 1)


def turn(value, shift):
    shift %= LANES
    return pltpu.roll(value, shift, 1) if shift else value


def own_rows(soil, depth, elevation, mask, field, p):
    if field < SOIL:
        return soil[p, field]
    rows = pl.ds(p * SUB, SUB)
    return (depth, elevation, mask)[field - SOIL][rows, :].astype(jnp.float32)


def pack_columns(soil, depth, elevation, mask, left, right):
    lane = lane_index(SUB)
    for p in range(GROUP):
        for plane, fields in ((0, range(SOIL)), (1, range(SOIL, FIELDS))):
            lefts = jnp.zeros((SUB, LANES), jnp.float32)
            rights = jnp.zeros((SUB, LANES), jnp.float32)
            for slot, field in enumerate(fields):
                value = own_rows(soil, depth, elevation, mask, field, p)
                here = (lane >= slot * HALO) & (lane < slot * HALO + HALO)
                lefts = jnp.where(here, turn(value, slot * HALO), lefts)
                rights = jnp.where(here, turn(value, slot * HALO + HALO), rights)
            left[plane, pl.ds(p * SUB, SUB), :] = lefts
            right[plane, pl.ds(p * SUB, SUB), :] = rights


def pack_rows(soil, depth, elevation, mask, from_left, from_right, top, bottom):
    half = HALO - SUB
    for field in range(FIELDS):
        at = field * HALO
        get = lambda p: own_rows(soil, depth, elevation, mask, field, p)
        top[pl.ds(at, SUB), :] = get(0)
        top[pl.ds(at + SUB, half), :] = get(1)[:half]
        bottom[pl.ds(at, half), :] = get(GROUP - 2)[SUB - half :]
        bottom[pl.ds(at + half, SUB), :] = get(GROUP - 1)
    lane = lane_index(HALO)
    for out, first in ((top, 0), (bottom, ROWS - HALO)):
        rows = pl.ds(first, HALO)
        out[pl.ds(FIELDS * HALO, HALO), :] = from_left[0, rows, :]
        out[pl.ds((FIELDS + 1) * HALO, HALO), :] = from_right[0, rows, :]
        out[pl.ds((FIELDS + 2) * HALO, HALO), :] = jnp.where(
            lane < 64, from_left[1, rows, :], turn(from_right[1, rows, :], 64)
        )


def beside(one, two, lane):
    r1, r2 = turn(one, -1), turn(two, -1)
    l1, l2 = turn(one, 1), turn(two, 1)
    last, first = lane == LANES - 1, lane == 0
    right = (jnp.where(last, r2, r1), jnp.where(last, r1, r2))
    left = (jnp.where(first, l2, l1), jnp.where(first, l1, l2))
    return right, left


def gather_blocks(pressure, conductance, pieces):
    for j in range(GROUP):
        columns = pl.ds(j * LANES, LANES)
        for layer in range(LAYERS):
            pieces[j, layer] = pressure[layer, 0, :, columns]
            pieces[j, LAYERS + layer] = conductance[layer, 0, :, columns]


def scatter_blocks(pieces, pressure):
    for j in range(GROUP):
        for layer in range(LAYERS):
            pressure[layer, 0, :, pl.ds(j * LANES, LANES)] = pieces[j, layer]


def spread(lefts, rights, lane, slot, shift=0):
    return jnp.where(
        lane < HALO,
        turn(rights, -slot * HALO - shift),
        jnp.where(lane >= LANES - HALO, turn(lefts, LANES - HALO - slot * HALO), 0.0),
    )


PLANES = range(2)


class Field:
    def __init__(self, ref, *where):
        self.ref, self.where = ref, where

    def __getitem__(self, key):
        return self.ref[self.where + key]

    def __setitem__(self, key, value):
        self.ref[self.where + key] = value


def set_conduct(rows, K, U, C, D, E, H, B):
    for plane in PLANES:
        depth = D[plane, rows, :]
        H[plane, rows, :] = depth + E[plane, rows, :]
        B[plane, rows, :] = jnp.where(
            K[plane, 0, rows, :] > 0, 1.0 + 0.5 * jnp.tanh(depth), 0.0
        )
        for layer in range(LAYERS):
            u = U[plane, layer, rows, :]
            C[plane, layer, rows, :] = 0.5 * K[plane, layer, rows, :] / (1.0 + u * u)


def around(row, wide):
    return pl.ds(row, wide), pl.ds(row - 1, wide), pl.ds(row + 1, wide)


def first_sweep(row, wide, at, lane, factor, K, U, X, C, D, M, H, B, faces):
    east, west, south, north, down, inverse, side = faces
    rows, before, after = around(row, wide)
    head = [H[plane, rows, :] for plane in PLANES]
    mobile = [B[plane, rows, :] for plane in PLANES]
    head_sides = beside(*head, lane)
    mobile_sides = beside(*mobile, lane)
    flux = []
    for plane in PLANES:
        depth = D[plane, rows, :]
        now = LEAKANCE * (depth - U[plane, 0, rows, :])
        flux.append(now)
        change = jnp.zeros_like(depth)
        for other_head, other_mobile in (
            (H[plane, after, :], B[plane, after, :]),
            (H[plane, before, :], B[plane, before, :]),
            (head_sides[0][plane], mobile_sides[0][plane]),
            (head_sides[1][plane], mobile_sides[1][plane]),
        ):
            change = change + (mobile[plane] + other_mobile) * (other_head - head[plane])
        D[plane, rows, :] = M[plane, rows, :] * (depth + (0.5 * ROUTING) * change - now)
    conduct = [[C[plane, layer, rows, :] for layer in range(LAYERS)] for plane in PLANES]
    iterate = [[U[plane, layer, rows, :] for layer in range(LAYERS)] for plane in PLANES]
    between = [
        [2.0 * (conduct[plane][l] + conduct[plane][l + 1]) for l in range(LAYERS - 1)]
        for plane in PLANES
    ]
    for layer in range(LAYERS):
        c_right, c_left = beside(conduct[0][layer], conduct[1][layer], lane)
        u_right, u_left = beside(iterate[0][layer], iterate[1][layer], lane)
        for plane in PLANES:
            c, u = conduct[plane][layer], iterate[plane][layer]
            e, w = c + c_right[plane], c + c_left[plane]
            s, n = c + C[plane, layer, after, :], c + C[plane, layer, before, :]
            diagonal = (STORAGE + e) + w + (s + n)
            total = STORAGE * u
            if layer == 0:
                total = total + flux[plane]
            side[plane, layer, at, :] = total
            total = total + e * u_right[plane] + w * u_left[plane]
            total = total + s * U[plane, layer, after, :] + n * U[plane, layer, before, :]
            if layer > 0:
                diagonal = diagonal + between[plane][layer - 1]
                total = total + between[plane][layer - 1] * iterate[plane][layer - 1]
            if layer < LAYERS - 1:
                diagonal = diagonal + between[plane][layer]
                total = total + between[plane][layer] * iterate[plane][layer + 1]
                down[plane, layer, at, :] = between[plane][layer]
            inv = jnp.where(K[plane, layer, rows, :] > 0, 1.0 / diagonal, 0.0)
            east[plane, layer, at, :] = e
            west[plane, layer, at, :] = w
            south[plane, layer, at, :] = s
            north[plane, layer, at, :] = n
            inverse[plane, layer, at, :] = inv
            X[plane, layer, rows, :] = (1.0 - factor) * u + factor * (inv * total)


def later_sweep(row, wide, at, lane, factor, source, goal, faces):
    east, west, south, north, down, inverse, side = faces
    rows, before, after = around(row, wide)
    iterate = [[source[plane, layer, rows, :] for layer in range(LAYERS)] for plane in PLANES]
    between = [[down[plane, layer, at, :] for layer in range(LAYERS - 1)] for plane in PLANES]
    for layer in range(LAYERS):
        u_right, u_left = beside(iterate[0][layer], iterate[1][layer], lane)
        for plane in PLANES:
            u = iterate[plane][layer]
            total = side[plane, layer, at, :]
            total = total + east[plane, layer, at, :] * u_right[plane]
            total = total + west[plane, layer, at, :] * u_left[plane]
            total = total + south[plane, layer, at, :] * source[plane, layer, after, :]
            total = total + north[plane, layer, at, :] * source[plane, layer, before, :]
            if layer > 0:
                total = total + between[plane][layer - 1] * iterate[plane][layer - 1]
            if layer < LAYERS - 1:
                total = total + between[plane][layer] * iterate[plane][layer + 1]
            inv = inverse[plane, layer, at, :]
            goal[plane, layer, rows, :] = (1.0 - factor) * u + factor * (inv * total)


NEAR = 16
TOPS = (SUB, SUB + ROWS - NEAR)
INNER = SUB + ROWS + SUB


def clear(refs, rows):
    for ref in refs:
        lead = ref.shape[:-2]
        value = jnp.zeros((rows.size, LANES), jnp.float32)
        for flat in range(math.prod(lead)):
            where = []
            for size in reversed(lead):
                where.insert(0, flat % size)
                flat //= size
            ref[tuple(where) + (rows, slice(None))] = value


def inner(
    soil, depth_in, elevation_in, mask_in, from_left, from_right,
    depth_out, pressure_out, seen, seen_k, seen_d, seen_e, seen_m,
    K, U, X, Y, C, east, west, south, north, down, inverse, side, D, E, M, H, B,
):
    factors = sweep_factors(SWEEPS)
    faces = (east, west, south, north, down, inverse, side)
    for row in (0, INNER - SUB):
        clear((K, U, X, Y, C, D, E, M, H, B), pl.ds(row, SUB))
    lane = lane_index(SUB)
    for field in range(FIELDS):
        if field < SOIL:
            at, slot, half = Field((U, K)[field // LAYERS]), field, 0
            name = lambda plane, rows: (plane, field % LAYERS, rows, slice(None))
        else:
            at, slot, half = Field((D, E, M)[field - SOIL]), field - SOIL, 1
            name = lambda plane, rows: (plane, rows, slice(None))
        for p in range(GROUP):
            rows, here = pl.ds(SUB + p * SUB, SUB), pl.ds(p * SUB, SUB)
            at[name(0, rows)] = own_rows(soil, depth_in, elevation_in, mask_in, field, p)
            at[name(1, rows)] = spread(
                from_left[half, here, :], from_right[half, here, :], lane, slot
            )

    def note(source, number):
        for edge, top in enumerate(TOPS):
            for plane in PLANES:
                for layer in range(LAYERS):
                    seen[number, edge, plane, layer] = source[plane, layer, pl.ds(top, NEAR), :]

    def note_depth(number):
        for edge, top in enumerate(TOPS):
            for plane in PLANES:
                seen_d[number, edge, plane] = D[plane, pl.ds(top, NEAR), :]

    note(U, 0)
    note_depth(0)
    for edge, top in enumerate(TOPS):
        rows = pl.ds(top, NEAR)
        for plane in PLANES:
            seen_e[edge, plane] = E[plane, rows, :]
            seen_m[edge, plane] = M[plane, rows, :]
            for layer in range(LAYERS):
                seen_k[edge, plane, layer] = K[plane, layer, rows, :]

    wide = 2 * SUB
    lane2 = lane_index(wide)

    def step(number, carry):
        last = number == STEPS - 1
        low = jnp.where(last, 2 * SUB, SUB)
        trips = jnp.where(last, 3, 4)

        def loop(count, begin, body):
            def one(i, carry):
                body(pl.multiple_of(begin + wide * i, SUB))
                return carry

            lax.fori_loop(0, count, one, 0)

        loop(4, SUB, lambda row: set_conduct(pl.ds(row, wide), K, U, C, D, E, H, B))
        loop(
            trips, low,
            lambda row: first_sweep(
                row, wide, pl.ds(row, wide), lane2, factors[0], K, U, X, C, D, M, H, B, faces
            ),
        )
        note(X, 3 * number + 1)
        loop(
            trips, low,
            lambda row: later_sweep(row, wide, pl.ds(row, wide), lane2, factors[1], X, Y, faces),
        )
        note(Y, 3 * number + 2)
        loop(
            trips, low,
            lambda row: later_sweep(row, wide, pl.ds(row, wide), lane2, factors[2], Y, U, faces),
        )

        @pl.when(number < STEPS - 1)
        def _():
            note(U, 3 * number + 3)
            note_depth(number + 1)

        return carry

    lax.fori_loop(0, STEPS, step, 0)
    depth_out[...] = D[0, pl.ds(SUB, ROWS), :]
    for p in range(GROUP):
        for layer in range(LAYERS):
            pressure_out[p, layer] = U[0, layer, pl.ds(SUB + p * SUB, SUB), :]


EDGE = 56


def edges(
    inner_depth, inner_pressure, seen, seen_k, seen_d, seen_e, seen_m, above, below,
    depth_out, pressure_out,
    K, U, X, Y, C, east, west, south, north, down, inverse, side, D, E, M, H, B,
):
    factors = sweep_factors(SWEEPS)
    wide = 2 * SUB
    everything = (K, U, X, Y, D, E, M)
    clear(everything, pl.ds(0, NEAR))
    clear(everything, pl.ds(2 * NEAR, EDGE - 2 * NEAR))
    clear((X, Y), pl.ds(NEAR, NEAR))
    lane = lane_index(HALO)
    own = pl.ds(NEAR, NEAR)
    for edge, (packed, top) in enumerate(((above, NEAR - HALO), (below, 2 * NEAR))):
        rows = pl.ds(top, HALO)
        lefts = packed[pl.ds(FIELDS * HALO, HALO), :]
        rights = packed[pl.ds((FIELDS + 1) * HALO, HALO), :]
        both = packed[pl.ds((FIELDS + 2) * HALO, HALO), :]
        for field in range(FIELDS):
            value = packed[pl.ds(field * HALO, HALO), :]
            if field < SOIL:
                ref, layer = (U, K)[field // LAYERS], field % LAYERS
                ref[edge, 0, layer, rows, :] = value
                ref[edge, 1, layer, rows, :] = spread(lefts, rights, lane, field)
            else:
                ref = (D, E, M)[field - SOIL]
                ref[edge, 0, rows, :] = value
                ref[edge, 1, rows, :] = spread(both, both, lane, field - SOIL, 64)
        for plane in PLANES:
            D[edge, plane, own, :] = seen_d[0, edge, plane]
            E[edge, plane, own, :] = seen_e[edge, plane]
            M[edge, plane, own, :] = seen_m[edge, plane]
            for layer in range(LAYERS):
                U[edge, plane, layer, own, :] = seen[0, edge, plane, layer]
                K[edge, plane, layer, own, :] = seen_k[edge, plane, layer]

    lane2, lane3 = lane_index(wide), lane_index(3 * SUB)
    at = pl.ds(0, wide)

    def step(number, carry):
        starts = (NEAR - 11 + 3 * number, 2 * NEAR - 5 - 3 * number)
        both = range(2)
        of = lambda ref: [Field(ref, edge) for edge in both]
        k, u, x, y, c, d, m, h, b = map(of, (K, U, X, Y, C, D, M, H, B))
        e = of(E)
        faces = [
            [Field(ref, edge) for ref in (east, west, south, north, down, inverse, side)]
            for edge in both
        ]

        def fill(goal, sweep, count):
            for edge in both:
                row = starts[0] + wide if edge == 0 else starts[1] - count
                for plane in PLANES:
                    for layer in range(LAYERS):
                        goal[edge, plane, layer, pl.ds(row, count), :] = seen[
                            sweep, edge, plane, layer, pl.ds(row - NEAR, count), :
                        ]

        for edge in both:
            rows = pl.ds(starts[edge] - 1, 3 * SUB)
            set_conduct(rows, k[edge], u[edge], c[edge], d[edge], e[edge], h[edge], b[edge])
        for edge in both:
            first_sweep(
                starts[edge], wide, at, lane2, factors[0],
                k[edge], u[edge], x[edge], c[edge], d[edge], m[edge], h[edge], b[edge], faces[edge],
            )
        fill(X, 3 * number + 1, 1)
        for edge in both:
            later_sweep(starts[edge], wide, at, lane2, factors[1], x[edge], y[edge], faces[edge])
        fill(Y, 3 * number + 2, 1)
        for edge in both:
            later_sweep(starts[edge], wide, at, lane2, factors[2], y[edge], u[edge], faces[edge])

        @pl.when(number < STEPS - 1)
        def _():
            fill(U, 3 * number + 3, 4)
            for edge in both:
                row = starts[0] + wide if edge == 0 else starts[1] - 4
                for plane in PLANES:
                    D[edge, plane, pl.ds(row, 4), :] = seen_d[
                        number + 1, edge, plane, pl.ds(row - NEAR, 4), :
                    ]

        return carry

    lax.fori_loop(0, STEPS, step, 0)
    left = ROWS - HALO
    depth_out[pl.ds(HALO, ROWS - 2 * HALO), :] = inner_depth[pl.ds(HALO, ROWS - 2 * HALO), :]
    depth_out[pl.ds(0, HALO), :] = D[0, 0, pl.ds(NEAR, HALO), :]
    depth_out[pl.ds(left, HALO), :] = D[1, 0, pl.ds(2 * NEAR - HALO, HALO), :]
    half = HALO - SUB
    for layer in range(LAYERS):
        for p in range(2, GROUP - 2):
            pressure_out[p, layer] = inner_pressure[p, layer]
        pressure_out[0, layer] = U[0, 0, layer, pl.ds(NEAR, SUB), :]
        pressure_out[1, layer, pl.ds(0, half), :] = U[0, 0, layer, pl.ds(NEAR + SUB, half), :]
        pressure_out[1, layer, pl.ds(half, SUB - half), :] = inner_pressure[
            1, layer, pl.ds(half, SUB - half), :
        ]
        pressure_out[GROUP - 2, layer, pl.ds(0, SUB - half), :] = inner_pressure[
            GROUP - 2, layer, pl.ds(0, SUB - half), :
        ]
        pressure_out[GROUP - 2, layer, pl.ds(SUB - half, half), :] = U[
            1, 0, layer, pl.ds(2 * NEAR - HALO, half), :
        ]
        pressure_out[GROUP - 1, layer] = U[1, 0, layer, pl.ds(2 * NEAR - SUB, SUB), :]


def call(kernel, outs, scratch, *args):
    vmem = pl.BlockSpec(memory_space=pltpu.VMEM)
    return pl.pallas_call(
        kernel,
        out_shape=[jax.ShapeDtypeStruct(shape, jnp.float32) for shape in outs],
        in_specs=[vmem] * len(args),
        out_specs=[vmem] * len(outs),
        scratch_shapes=[pltpu.VMEM(shape, jnp.float32) for shape in scratch],
        compiler_params=pltpu.CompilerParams(vmem_limit_bytes=32 << 20),
    )(*args)


def solution(mesh):
    secs, tiles = mesh.shape["sec"], mesh.shape["tile"]
    axes = ("sec", "band", "place")
    parts = Mesh(mesh.devices.reshape(secs, tiles // GROUP, GROUP), axes)

    def pairs(along, odd):
        found = []
        for s in range(secs):
            for t in range(tiles):
                index, count = (s, secs) if along == "sec" else (t, tiles)
                other = index + 1 if index % 2 == odd else index - 1
                if 0 <= other < count:
                    goal = (other, t) if along == "sec" else (s, other)
                    found.append((s * tiles + t, goal[0] * tiles + goal[1]))
        return found

    def swap(value, along, odd):
        return lax.ppermute(value, axes, pairs(along, odd))

    def local(depth, elevation, land_mask, pressure, conductance):
        tile_odd = lax.axis_index("place") % 2 == 1
        sec_odd = lax.axis_index("sec") % 2 == 1
        [pieces] = call(gather_blocks, [(GROUP, SOIL, SUB, LANES)], [], pressure, conductance)
        soil = lax.all_to_all(pieces, "place", 0, 0)
        own = (soil, depth, elevation, land_mask)
        left, right = call(pack_columns, [(2, ROWS, LANES)] * 2, [], *own)
        one = swap(jnp.where(tile_odd, left, right), "tile", 0)
        two = swap(jnp.where(tile_odd, right, left), "tile", 1)
        from_left = jnp.where(tile_odd, one, two)
        from_right = jnp.where(tile_odd, two, one)
        top, bottom = call(pack_rows, [(STRIP, LANES)] * 2, [], *own, from_left, from_right)
        one = swap(jnp.where(sec_odd, bottom, top), "sec", 1)
        two = swap(jnp.where(sec_odd, top, bottom), "sec", 0)
        above = jnp.where(sec_odd, two, one)
        below = jnp.where(sec_odd, one, two)
        near = (2, 2, LAYERS, NEAR, LANES)
        field, layer = (2, LAYERS, INNER, LANES), (2, INNER, LANES)
        shapes = [(ROWS, LANES), (GROUP, LAYERS, SUB, LANES)]
        held = call(
            inner,
            shapes + [(SWEEPS * STEPS,) + near, near, (STEPS, 2, 2, NEAR, LANES)] + [(2, 2, NEAR, LANES)] * 2,
            [field] * 12 + [layer] * 5,
            *own, from_left, from_right,
        )
        field, face, layer = (
            (2, 2, LAYERS, EDGE, LANES),
            (2, 2, LAYERS, 2 * SUB, LANES),
            (2, 2, EDGE, LANES),
        )
        depth, soil = call(
            edges, shapes, [field] * 5 + [face] * 7 + [layer] * 5, *held, above, below
        )
        soil = lax.all_to_all(soil, "place", 0, 0)
        [soil] = call(scatter_blocks, [(LAYERS, 1, SUB, GROUP * LANES)], [], soil)
        return depth, soil

    surface = P("sec", ("band", "place"))
    blocked = P(None, axes, None, None)
    return jax.shard_map(
        local,
        mesh=parts,
        in_specs=(surface, surface, surface, blocked, blocked),
        out_specs=(surface, blocked),
        check_vma=False,
    )
```

time: 68.9 us -> 66.4 us (0.964)
  the two profiles are of different devices: /device:TPU:448 before, /device:TPU:4 now
where the time goes in v2:
time: 66.4 us; the launch traced here: 65.8 us
  starting transfers between devices  27.7 us (42%)
  Pallas kernels  13.3 us (20%)
  blocking collectives  10.7 us (16%)
  waiting for transfers between devices  9.11 us (14%)
  local copies, waits for them, and re-layouts  4.12 us (6%)
  between operations  0.79 us (1%)
    ppermute x4, starting transfers between devices, swap(): return lax.ppermute(value, axes, pairs(along, odd))  23.2 us
    pallas_call x6, Pallas kernels, call(): pl.pallas_call(kernel, out_shape=[jax.ShapeDtypeStruct(shape, jnp.float32...  13.3 us
    all_to_all x1, blocking collectives, local(): soil = lax.all_to_all(soil, 'place', 0, 0)  10.7 us
    all_to_all x1, waiting for transfers between devices, local(): soil = lax.all_to_all(pieces, 'place', 0, 0)  8.24 us
    all_to_all x1, starting transfers between devices, local(): soil = lax.all_to_all(pieces, 'place', 0, 0)  4.47 us
    unnamed x16, local copies, waits for them, and re-layouts  4.12 us
  transfers between devices with their start and end apart: 5, of which 2 were waited for; matrix products, arithmetic and copies ran while one was open for 0% of the time, Pallas kernels for 11%

profile of v2, /device:TPU:4, one launch (start us, length us, event | category | flops | bytes accessed | tf_op | source)
XLA Modules:
  0.0 65.8 jit_solution(10897426085798222187)
XLA Ops:
  0.6 0.0 copy-start.5
  0.6 0.0 copy-start.3
  0.7 0.0 copy-start.6
  0.7 0.9 %copy-done.6 = f32[5,1,8,1024]{3,2,1,0:T(8,128)S(1)} copy-done((f32[5,1,8,1024]{3,2,1,0:T(8,128)S(1)}, f32[5,1,8,1024]{3,2,1,0:T(8,128)}, u32[]{:S(2)}) %copy-start.6) | copy-done | bytes 163864
  1.6 0.0 copy-start.7
  1.6 0.9 %copy-done.7 = f32[5,1,8,1024]{3,2,1,0:T(8,128)S(1)} copy-done((f32[5,1,8,1024]{3,2,1,0:T(8,128)S(1)}, f32[5,1,8,1024]{3,2,1,0:T(8,128)}, u32[]{:S(2)}) %copy-start.7) | copy-done | bytes 163864
  2.5 0.0 copy-start.1
  2.5 0.8 %shard_map.68 = f32[8,10,8,128]{3,2,1,0:T(8,128)} custom-call(f32[5,1,8,1024]{3,2,1,0:T(8,128)S(1)} %copy-done.6, f32[5,1,8,1024]{3,2,1,0:T(8,128)S(1)} %copy-done.7), custom_call_target="tpu_custom_call" | custom-call | tf_op jit(solution)/shard_map/pallas_call | solution.py:451
  3.3 4.5 %all-to-all-start = ((f32[8,10,8,128]{3,2,1,0:T(8,128)}), f32[8,10,8,128]{3,2,1,0:T(8,128)S(1)}, u32[]{:S(2)}, u32[]{:S(2)}) async-start(f32[8,10,8,128]{3,2,1,0:T(8,128)} %shard_map.68), calls=%async_computation | async-start | bytes 655360 | tf_op jit(solution)/shard_map/all_to_all | solution.py:484
  7.7 8.2 %all-to-all-done.soil = f32[8,10,8,128]{3,2,1,0:T(8,128)S(1)} async-done(((f32[8,10,8,128]{3,2,1,0:T(8,128)}), f32[8,10,8,128]{3,2,1,0:T(8,128)S(1)}, u32[]{:S(2)}, u32[]{:S(2)}) %all-to-all-start) | async-done | bytes 327712 | tf_op jit(solution)/shard_map/all_to_all | solution.py:484
  16.0 0.0 copy-start
  16.0 0.8 %copy-done = f32[64,128]{1,0:T(8,128)S(1)} copy-done((f32[64,128]{1,0:T(8,128)S(1)}, f32[64,128]{1,0:T(8,128)}, u32[]{:S(2)}) %copy-start) | copy-done | bytes 32792
  16.7 0.0 copy-start.2
  16.7 0.8 %copy-done.2 = f32[64,128]{1,0:T(8,128)S(1)} copy-done((f32[64,128]{1,0:T(8,128)S(1)}, f32[64,128]{1,0:T(8,128)}, u32[]{:S(2)}) %copy-start.2) | copy-done | bytes 32792
  17.5 0.8 %copy-done.4 = s32[64,128]{1,0:T(8,128)S(1)} copy-done((s32[64,128]{1,0:T(8,128)S(1)}, s32[64,128]{1,0:T(8,128)}, u32[]{:S(2)}) %copy-start.4) | copy-done | bytes 32792
  18.2 0.3 shard_map.69
  18.5 0.7 %collective-permute-start.1 = (f32[2,64,128]{2,1,0:T(8,128)S(1)}, f32[2,64,128]{2,1,0:T(8,128)S(1)}, u32[]{:S(2)}, u32[]{:S(2)}) collective-permute-start(f32[2,64,128]{2,1,0:T(8,128)S(1)} %get-tuple-element.34), channel_id=1, source_target_pairs={{1,2},{2,1},{3,4},{4,3},{5,6},{6,5},{7,8},{8,7},{9,10},{10,9},{11,... | collective-permute-start | bytes 196616 | tf_op jit(solution)/shard_map/ppermute | solution.py:478
  19.2 3.8 %collective-permute-start = (f32[2,64,128]{2,1,0:T(8,128)S(1)}, f32[2,64,128]{2,1,0:T(8,128)S(1)}, u32[]{:S(2)}, u32[]{:S(2)}) collective-permute-start(f32[2,64,128]{2,1,0:T(8,128)S(1)} %get-tuple-element.35), channel_id=1, source_target_pairs={{0,1},{1,0},{2,3},{3,2},{4,5},{5,4},{6,7},{7,6},{8,9},{9,8},{10,11... | collective-permute-start | bytes 196616 | tf_op jit(solution)/shard_map/ppermute | solution.py:478
  23.1 0.0 collective-permute-done.1
  23.1 0.9 %collective-permute-done = f32[2,64,128]{2,1,0:T(8,128)S(1)} collective-permute-done((f32[2,64,128]{2,1,0:T(8,128)S(1)}, f32[2,64,128]{2,1,0:T(8,128)S(1)}, u32[]{:S(2)}, u32[]{:S(2)}) %collective-permute-start) | collective-permute-done | bytes 65568 | tf_op jit(solution)/shard_map/ppermute | solution.py:478
  23.9 0.0 copy-done.5
  23.9 0.0 copy-done.3
  24.0 0.0 copy-done.1
  24.0 0.1 shard_map.71
  24.1 2.4 %collective-permute-start.3 = (f32[192,128]{1,0:T(8,128)S(1)}, f32[192,128]{1,0:T(8,128)S(1)}, u32[]{:S(2)}, u32[]{:S(2)}) collective-permute-start(f32[192,128]{1,0:T(8,128)S(1)} %get-tuple-element.30), channel_id=1, source_target_pairs={{64,128},{65,129},{66,130},{67,131},{68,132},{69,133},{70,134},{71... | collective-permute-start | bytes 294920 | tf_op jit(solution)/shard_map/ppermute | solution.py:478
  26.5 16.3 %collective-permute-start.2 = (f32[192,128]{1,0:T(8,128)S(1)}, f32[192,128]{1,0:T(8,128)S(1)}, u32[]{:S(2)}, u32[]{:S(2)}) collective-permute-start(f32[192,128]{1,0:T(8,128)S(1)} %get-tuple-element.31), channel_id=1, source_target_pairs={{0,64},{1,65},{2,66},{3,67},{4,68},{5,69},{6,70},{7,71},{8,72},{9,... | collective-permute-start | bytes 294920 | tf_op jit(solution)/shard_map/ppermute | solution.py:478
  42.8 7.6 %shard_map.70 = (f32[64,128]{1,0:T(8,128)S(1)}, f32[8,5,8,128]{3,2,1,0:T(8,128)S(1)}, f32[12,2,2,5,16,128]{5,4,3,2,1,0:T(8,128)S(1)}, f32[2,2,5,16,128]{4,3,2,1,...) custom-call(f32[8,10,8,128]{3,2,1,0:T(8,128)S(1)} %all-to-all-done.s, ...), custom_call_target="tpu_custom_call" | custom-call | tf_op jit(solution)/shard_map/pallas_call | solution.py:451
  50.4 0.0 collective-permute-done.3
  50.4 0.0 collective-permute-done.2
  50.4 4.0 %shard_map.72 = (f32[64,128]{1,0:T(8,128)}, f32[8,5,8,128]{3,2,1,0:T(8,128)S(1)}) custom-call(f32[64,128]{1,0:T(8,128)S(1)} %get-tuple-element.17.inner_depth, f32[8,5,8,128]{3,2,1,0:T(8,128)S(1)} %get-tuple-element.18.inner_pressure, f32[12,2,2,5,16,128]{5,4,3,2,1,0:T(8,128)S(1)} %get-tuple-element.19.seen, ...), custom_call_target="tpu_custom_call" | custom-call | tf_op jit(solution)/shard_map/pallas_call | solution.py:451
  54.5 10.7 %all_to_all.10.pieces = f32[8,5,8,128]{3,2,1,0:T(8,128)S(1)} all-to-all(f32[8,5,8,128]{3,2,1,0:T(8,128)S(1)} %get-tuple-element.27), channel_id=1, replica_groups=mesh['sec'=8,'band'=8,'place'=8] {'place'}, dimensions={0} | all-to-all | bytes 327680 | tf_op jit(solution)/shard_map/all_to_all | solution.py:513
  65.1 0.7 %shard_map.73 = f32[5,1,8,1024]{3,2,1,0:T(8,128)} custom-call(f32[8,5,8,128]{3,2,1,0:T(8,128)S(1)} %all_to_all.10.pieces), custom_call_target="tpu_custom_call" | custom-call | tf_op jit(solution)/shard_map/pallas_call | solution.py:451
  (5 shorter events, 0.1 us)
Async XLA Ops:
  0.6 23.3 %copy-start.5 = (s32[64,128]{1,0:T(8,128)S(1)}, s32[64,128]{1,0:T(8,128)}, u32[]{:S(2)}) copy-start(s32[64,128]{1,0:T(8,128)} %mask.3) | copy-start | bytes 98308
  0.6 23.3 %copy-start.3 = (f32[64,128]{1,0:T(8,128)S(1)}, f32[64,128]{1,0:T(8,128)}, u32[]{:S(2)}) copy-start(f32[64,128]{1,0:T(8,128)} %elevation.3) | copy-start | bytes 98308
  0.7 0.9 %copy-start.6 = (f32[5,1,8,1024]{3,2,1,0:T(8,128)S(1)}, f32[5,1,8,1024]{3,2,1,0:T(8,128)}, u32[]{:S(2)}) copy-start(f32[5,1,8,1024]{3,2,1,0:T(8,128)} %pressure.1) | copy-start | bytes 491524
  1.6 0.9 %copy-start.7 = (f32[5,1,8,1024]{3,2,1,0:T(8,128)S(1)}, f32[5,1,8,1024]{3,2,1,0:T(8,128)}, u32[]{:S(2)}) copy-start(f32[5,1,8,1024]{3,2,1,0:T(8,128)} %conductance.1) | copy-start | bytes 491524
  2.5 21.5 %copy-start.1 = (f32[64,128]{1,0:T(8,128)S(1)}, f32[64,128]{1,0:T(8,128)}, u32[]{:S(2)}) copy-start(f32[64,128]{1,0:T(8,128)} %depth.3) | copy-start | bytes 98308
  3.3 12.7 %all-to-all-start = ((f32[8,10,8,128]{3,2,1,0:T(8,128)}), f32[8,10,8,128]{3,2,1,0:T(8,128)S(1)}, u32[]{:S(2)}, u32[]{:S(2)}) async-start(f32[8,10,8,128]{3,2,1,0:T(8,128)} %shard_map.68), calls=%async_computation | async-start | bytes 655360 | tf_op jit(solution)/shard_map/all_to_all | solution.py:484
  16.0 0.8 %copy-start = (f32[64,128]{1,0:T(8,128)S(1)}, f32[64,128]{1,0:T(8,128)}, u32[]{:S(2)}) copy-start(f32[64,128]{1,0:T(8,128)} %depth.3) | copy-start | bytes 98308
  16.7 0.8 %copy-start.2 = (f32[64,128]{1,0:T(8,128)S(1)}, f32[64,128]{1,0:T(8,128)}, u32[]{:S(2)}) copy-start(f32[64,128]{1,0:T(8,128)} %elevation.3) | copy-start | bytes 98308
  17.5 0.8 %copy-start.4 = (s32[64,128]{1,0:T(8,128)S(1)}, s32[64,128]{1,0:T(8,128)}, u32[]{:S(2)}) copy-start(s32[64,128]{1,0:T(8,128)} %mask.3) | copy-start | bytes 98308
  18.5 4.5 %collective-permute-start.1 = (f32[2,64,128]{2,1,0:T(8,128)S(1)}, f32[2,64,128]{2,1,0:T(8,128)S(1)}, u32[]{:S(2)}, u32[]{:S(2)}) collective-permute-start(f32[2,64,128]{2,1,0:T(8,128)S(1)} %get-tuple-element.34), channel_id=1, source_target_pairs={{1,2},{2,1},{3,4},{4,3},{5,6},{6,5},{7,8},{8,7},{9,10},{10,9},{11,... | collective-permute-start | bytes 196616 | tf_op jit(solution)/shard_map/ppermute | solution.py:478
  19.2 4.7 %collective-permute-start = (f32[2,64,128]{2,1,0:T(8,128)S(1)}, f32[2,64,128]{2,1,0:T(8,128)S(1)}, u32[]{:S(2)}, u32[]{:S(2)}) collective-permute-start(f32[2,64,128]{2,1,0:T(8,128)S(1)} %get-tuple-element.35), channel_id=1, source_target_pairs={{0,1},{1,0},{2,3},{3,2},{4,5},{5,4},{6,7},{7,6},{8,9},{9,8},{10,11... | collective-permute-start | bytes 196616 | tf_op jit(solution)/shard_map/ppermute | solution.py:478
  24.1 26.3 %collective-permute-start.3 = (f32[192,128]{1,0:T(8,128)S(1)}, f32[192,128]{1,0:T(8,128)S(1)}, u32[]{:S(2)}, u32[]{:S(2)}) collective-permute-start(f32[192,128]{1,0:T(8,128)S(1)} %get-tuple-element.30), channel_id=1, source_target_pairs={{64,128},{65,129},{66,130},{67,131},{68,132},{69,133},{70,134},{71... | collective-permute-start | bytes 294920 | tf_op jit(solution)/shard_map/ppermute | solution.py:478
  26.5 23.9 %collective-permute-start.2 = (f32[192,128]{1,0:T(8,128)S(1)}, f32[192,128]{1,0:T(8,128)S(1)}, u32[]{:S(2)}, u32[]{:S(2)}) collective-permute-start(f32[192,128]{1,0:T(8,128)S(1)} %get-tuple-element.31), channel_id=1, source_target_pairs={{0,64},{1,65},{2,66},{3,67},{4,68},{5,69},{6,70},{7,71},{8,72},{9,... | collective-permute-start | bytes 294920 | tf_op jit(solution)/shard_map/ppermute | solution.py:478

commit v3 on v2

--- a/solution.py
+++ b/solution.py
@@ -44,21 +44,20 @@
     return pltpu.roll(value, shift, 1) if shift else value
 
 
-def own_rows(soil, depth, elevation, mask, field, p):
+def own_rows(soil, surface, field, p):
     if field < SOIL:
         return soil[p, field]
-    rows = pl.ds(p * SUB, SUB)
-    return (depth, elevation, mask)[field - SOIL][rows, :].astype(jnp.float32)
-
-
-def pack_columns(soil, depth, elevation, mask, left, right):
+    return surface[field - SOIL, pl.ds(p * SUB, SUB), :]
+
+
+def pack_columns(soil, surface, left, right):
     lane = lane_index(SUB)
     for p in range(GROUP):
         for plane, fields in ((0, range(SOIL)), (1, range(SOIL, FIELDS))):
             lefts = jnp.zeros((SUB, LANES), jnp.float32)
             rights = jnp.zeros((SUB, LANES), jnp.float32)
             for slot, field in enumerate(fields):
-                value = own_rows(soil, depth, elevation, mask, field, p)
+                value = own_rows(soil, surface, field, p)
                 here = (lane >= slot * HALO) & (lane < slot * HALO + HALO)
                 lefts = jnp.where(here, turn(value, slot * HALO), lefts)
                 rights = jnp.where(here, turn(value, slot * HALO + HALO), rights)
@@ -66,11 +65,11 @@
             right[plane, pl.ds(p * SUB, SUB), :] = rights
 
 
-def pack_rows(soil, depth, elevation, mask, from_left, from_right, top, bottom):
+def pack_rows(soil, surface, from_left, from_right, top, bottom):
     half = HALO - SUB
     for field in range(FIELDS):
         at = field * HALO
-        get = lambda p: own_rows(soil, depth, elevation, mask, field, p)
+        get = lambda p: own_rows(soil, surface, field, p)
         top[pl.ds(at, SUB), :] = get(0)
         top[pl.ds(at + SUB, half), :] = get(1)[:half]
         bottom[pl.ds(at, half), :] = get(GROUP - 2)[SUB - half :]
@@ -94,18 +93,43 @@
     return right, left
 
 
-def gather_blocks(pressure, conductance, pieces):
-    for j in range(GROUP):
-        columns = pl.ds(j * LANES, LANES)
-        for layer in range(LAYERS):
-            pieces[j, layer] = pressure[layer, 0, :, columns]
-            pieces[j, LAYERS + layer] = conductance[layer, 0, :, columns]
-
-
-def scatter_blocks(pieces, pressure):
-    for j in range(GROUP):
-        for layer in range(LAYERS):
-            pressure[layer, 0, :, pl.ds(j * LANES, LANES)] = pieces[j, layer]
+def gather_blocks(
+    pressure, conductance, depth, elevation, mask, pieces, surface, mask_here, sems
+):
+    copies = [
+        pltpu.make_async_copy(
+            source.at[:, 0, :, pl.ds(j * LANES, LANES)],
+            pieces.at[j, pl.ds(first, LAYERS)],
+            sems.at[2 * j + first // LAYERS],
+        )
+        for j in range(GROUP)
+        for source, first in ((pressure, 0), (conductance, LAYERS))
+    ]
+    count = len(copies)
+    copies += [
+        pltpu.make_async_copy(source, goal, sems.at[count + i])
+        for i, (source, goal) in enumerate(
+            ((depth, surface.at[0]), (elevation, surface.at[1]), (mask, mask_here))
+        )
+    ]
+    for copy in copies:
+        copy.start()
+    for copy in reversed(copies):
+        copy.wait()
+    surface[2] = mask_here[...].astype(jnp.float32)
+
+
+def scatter_blocks(pieces, pressure, sems):
+    copies = [
+        pltpu.make_async_copy(
+            pieces.at[j], pressure.at[:, 0, :, pl.ds(j * LANES, LANES)], sems.at[j]
+        )
+        for j in range(GROUP)
+    ]
+    for copy in copies:
+        copy.start()
+    for copy in copies:
+        copy.wait()
 
 
 def spread(lefts, rights, lane, slot, shift=0):
@@ -243,7 +267,7 @@
 
 
 def inner(
-    soil, depth_in, elevation_in, mask_in, from_left, from_right,
+    soil, surface, from_left, from_right,
     depth_out, pressure_out, seen, seen_k, seen_d, seen_e, seen_m,
     K, U, X, Y, C, east, west, south, north, down, inverse, side, D, E, M, H, B,
 ):
@@ -261,7 +285,7 @@
             name = lambda plane, rows: (plane, rows, slice(None))
         for p in range(GROUP):
             rows, here = pl.ds(SUB + p * SUB, SUB), pl.ds(p * SUB, SUB)
-            at[name(0, rows)] = own_rows(soil, depth_in, elevation_in, mask_in, field, p)
+            at[name(0, rows)] = own_rows(soil, surface, field, p)
             at[name(1, rows)] = spread(
                 from_left[half, here, :], from_right[half, here, :], lane, slot
             )
@@ -290,17 +314,13 @@
     wide = 2 * SUB
     lane2 = lane_index(wide)
 
-    def step(number, carry):
+    def step(number):
         last = number == STEPS - 1
-        low = jnp.where(last, 2 * SUB, SUB)
-        trips = jnp.where(last, 3, 4)
+        low, trips = (2 * SUB, 3) if last else (SUB, 4)
 
         def loop(count, begin, body):
-            def one(i, carry):
-                body(pl.multiple_of(begin + wide * i, SUB))
-                return carry
-
-            lax.fori_loop(0, count, one, 0)
+            for i in range(count):
+                body(begin + wide * i)
 
         loop(4, SUB, lambda row: set_conduct(pl.ds(row, wide), K, U, C, D, E, H, B))
         loop(
@@ -320,14 +340,12 @@
             lambda row: later_sweep(row, wide, pl.ds(row, wide), lane2, factors[2], Y, U, faces),
         )
 
-        @pl.when(number < STEPS - 1)
-        def _():
+        if not last:
             note(U, 3 * number + 3)
             note_depth(number + 1)
 
-        return carry
-
-    lax.fori_loop(0, STEPS, step, 0)
+    for number in range(STEPS):
+        step(number)
     depth_out[...] = D[0, pl.ds(SUB, ROWS), :]
     for p in range(GROUP):
         for layer in range(LAYERS):
@@ -376,7 +394,7 @@
     lane2, lane3 = lane_index(wide), lane_index(3 * SUB)
     at = pl.ds(0, wide)
 
-    def step(number, carry):
+    def step(number):
         starts = (NEAR - 11 + 3 * number, 2 * NEAR - 5 - 3 * number)
         both = range(2)
         of = lambda ref: [Field(ref, edge) for edge in both]
@@ -411,8 +429,7 @@
         for edge in both:
             later_sweep(starts[edge], wide, at, lane2, factors[2], y[edge], u[edge], faces[edge])
 
-        @pl.when(number < STEPS - 1)
-        def _():
+        if number < STEPS - 1:
             fill(U, 3 * number + 3, 4)
             for edge in both:
                 row = starts[0] + wide if edge == 0 else starts[1] - 4
@@ -421,9 +438,8 @@
                         number + 1, edge, plane, pl.ds(row - NEAR, 4), :
                     ]
 
-        return carry
-
-    lax.fori_loop(0, STEPS, step, 0)
+    for number in range(STEPS):
+        step(number)
     left = ROWS - HALO
     depth_out[pl.ds(HALO, ROWS - 2 * HALO), :] = inner_depth[pl.ds(HALO, ROWS - 2 * HALO), :]
     depth_out[pl.ds(0, HALO), :] = D[0, 0, pl.ds(NEAR, HALO), :]
@@ -446,14 +462,22 @@
         pressure_out[GROUP - 1, layer] = U[1, 0, layer, pl.ds(2 * NEAR - SUB, SUB), :]
 
 
-def call(kernel, outs, scratch, *args):
-    vmem = pl.BlockSpec(memory_space=pltpu.VMEM)
+def call(kernel, outs, scratch, *args, places=None):
+    places = places or [pltpu.VMEM] * (len(args) + len(outs))
+    specs = [pl.BlockSpec(memory_space=place) for place in places]
+    args = [
+        pltpu.with_memory_space_constraint(arg, place) if place == pltpu.HBM else arg
+        for arg, place in zip(args, places)
+    ]
     return pl.pallas_call(
         kernel,
         out_shape=[jax.ShapeDtypeStruct(shape, jnp.float32) for shape in outs],
-        in_specs=[vmem] * len(args),
-        out_specs=[vmem] * len(outs),
-        scratch_shapes=[pltpu.VMEM(shape, jnp.float32) for shape in scratch],
+        in_specs=specs[: len(args)],
+        out_specs=specs[len(args) :],
+        scratch_shapes=[
+            pltpu.VMEM(shape, jnp.float32) if isinstance(shape, tuple) else shape
+            for shape in scratch
+        ],
         compiler_params=pltpu.CompilerParams(vmem_limit_bytes=32 << 20),
     )(*args)
 
@@ -480,9 +504,15 @@
     def local(depth, elevation, land_mask, pressure, conductance):
         tile_odd = lax.axis_index("place") % 2 == 1
         sec_odd = lax.axis_index("sec") % 2 == 1
-        [pieces] = call(gather_blocks, [(GROUP, SOIL, SUB, LANES)], [], pressure, conductance)
+        pieces, surface = call(
+            gather_blocks,
+            [(GROUP, SOIL, SUB, LANES), (3, ROWS, LANES)],
+            [pltpu.VMEM((ROWS, LANES), jnp.int32), pltpu.SemaphoreType.DMA((2 * GROUP + 3,))],
+            pressure, conductance, depth, elevation, land_mask,
+            places=[pltpu.HBM] * 5 + [pl.ANY, pltpu.VMEM],
+        )
         soil = lax.all_to_all(pieces, "place", 0, 0)
-        own = (soil, depth, elevation, land_mask)
+        own = (soil, surface)
         left, right = call(pack_columns, [(2, ROWS, LANES)] * 2, [], *own)
         one = swap(jnp.where(tile_odd, left, right), "tile", 0)
         two = swap(jnp.where(tile_odd, right, left), "tile", 1)
@@ -511,7 +541,13 @@
             edges, shapes, [field] * 5 + [face] * 7 + [layer] * 5, *held, above, below
         )
         soil = lax.all_to_all(soil, "place", 0, 0)
-        [soil] = call(scatter_blocks, [(LAYERS, 1, SUB, GROUP * LANES)], [], soil)
+        [soil] = call(
+            scatter_blocks,
+            [(LAYERS, 1, SUB, GROUP * LANES)],
+            [pltpu.SemaphoreType.DMA((GROUP,))],
+            soil,
+            places=[pl.ANY, pltpu.HBM],
+        )
         return depth, soil
 
     surface = P("sec", ("band", "place"))

time: 66.4 us -> 69.3 us (1.044)
  the two profiles are of different devices: /device:TPU:4 before, /device:TPU:448 now
where the time goes in v3:
time: 69.3 us; the launch traced here: 68.9 us
  waiting for transfers between devices  20.7 us (30%)
  Pallas kernels  19.3 us (28%)
  starting transfers between devices  18.5 us (27%)
  blocking collectives  9.55 us (14%)
  between operations  0.72 us (1%)
    pallas_call x6, Pallas kernels, call(): pl.pallas_call(kernel, out_shape=[jax.ShapeDtypeStruct(shape, jnp.float32...  19.3 us
    ppermute x4, starting transfers between devices, swap(): return lax.ppermute(value, axes, pairs(along, odd))  14 us
    ppermute x4, waiting for transfers between devices, swap(): return lax.ppermute(value, axes, pairs(along, odd))  12.4 us
    all_to_all x1, blocking collectives, local(): soil = lax.all_to_all(soil, 'place', 0, 0)  9.55 us
    all_to_all x1, waiting for transfers between devices, local(): soil = lax.all_to_all(pieces, 'place', 0, 0)  8.24 us
    all_to_all x1, starting transfers between devices, local(): soil = lax.all_to_all(pieces, 'place', 0, 0)  4.48 us
  transfers between devices with their start and end apart: 5, of which 3 were waited for; matrix products, arithmetic and copies ran while one was open for 0% of the time, Pallas kernels for 6%

profile of v3, /device:TPU:448, one launch (start us, length us, event | category | flops | bytes accessed | tf_op | source)
XLA Modules:
  0.0 68.9 jit_solution(17179794438230895197)
XLA Ops:
  0.6 11.2 %shard_map.68 = (f32[8,10,8,128]{3,2,1,0:T(8,128)}, f32[3,64,128]{2,1,0:T(8,128)S(1)}) custom-call(f32[5,1,8,1024]{3,2,1,0:T(8,128)} %pressure.1, f32[5,1,8,1024]{3,2,1,0:T(8,128)} %conductance.1, f32[64,128]{1,0:T(8,128)} %depth.1, f32[64,128]{1,0:T(8,128)} %elevation.1, s32[64,128]{1,0:T(8,128)} %mask.1), custom_call_target="tpu_custom_call" | custom-call | tf_op jit(solution)/shard_map/pallas_call | solution.py:472
  11.9 4.5 %all-to-all-start = ((f32[8,10,8,128]{3,2,1,0:T(8,128)}), f32[8,10,8,128]{3,2,1,0:T(8,128)S(1)}, u32[]{:S(2)}, u32[]{:S(2)}) async-start(f32[8,10,8,128]{3,2,1,0:T(8,128)} %get-tuple-element.17), calls=%async_computation | async-start | bytes 655360 | tf_op jit(solution)/shard_map/all_to_all | solution.py:514
  16.3 8.2 %all-to-all-done.soil = f32[8,10,8,128]{3,2,1,0:T(8,128)S(1)} async-done(((f32[8,10,8,128]{3,2,1,0:T(8,128)}), f32[8,10,8,128]{3,2,1,0:T(8,128)S(1)}, u32[]{:S(2)}, u32[]{:S(2)}) %all-to-all-start) | async-done | bytes 327712 | tf_op jit(solution)/shard_map/all_to_all | solution.py:514
  24.6 0.3 shard_map.69
  24.9 2.5 %collective-permute-start.1 = (f32[2,64,128]{2,1,0:T(8,128)S(1)}, f32[2,64,128]{2,1,0:T(8,128)S(1)}, u32[]{:S(2)}, u32[]{:S(2)}) collective-permute-start(f32[2,64,128]{2,1,0:T(8,128)S(1)} %get-tuple-element.38), channel_id=1, source_target_pairs={{1,2},{2,1},{3,4},{4,3},{5,6},{6,5},{7,8},{8,7},{9,10},{10,9},{11,... | collective-permute-start | bytes 196616 | tf_op jit(solution)/shard_map/ppermute | solution.py:502
  27.4 2.0 %collective-permute-start = (f32[2,64,128]{2,1,0:T(8,128)S(1)}, f32[2,64,128]{2,1,0:T(8,128)S(1)}, u32[]{:S(2)}, u32[]{:S(2)}) collective-permute-start(f32[2,64,128]{2,1,0:T(8,128)S(1)} %get-tuple-element.39), channel_id=1, source_target_pairs={{0,1},{1,0},{2,3},{3,2},{4,5},{5,4},{6,7},{7,6},{8,9},{9,8},{10,11... | collective-permute-start | bytes 196616 | tf_op jit(solution)/shard_map/ppermute | solution.py:502
  29.4 3.2 %collective-permute-done.1 = f32[2,64,128]{2,1,0:T(8,128)S(1)} collective-permute-done((f32[2,64,128]{2,1,0:T(8,128)S(1)}, f32[2,64,128]{2,1,0:T(8,128)S(1)}, u32[]{:S(2)}, u32[]{:S(2)}) %collective-permute-start.1) | collective-permute-done | bytes 65568 | tf_op jit(solution)/shard_map/ppermute | solution.py:502
  32.6 0.0 collective-permute-done
  32.6 0.1 shard_map.71
  32.7 7.6 %collective-permute-start.3 = (f32[192,128]{1,0:T(8,128)S(1)}, f32[192,128]{1,0:T(8,128)S(1)}, u32[]{:S(2)}, u32[]{:S(2)}) collective-permute-start(f32[192,128]{1,0:T(8,128)S(1)} %get-tuple-element.34), channel_id=1, source_target_pairs={{64,128},{65,129},{66,130},{67,131},{68,132},{69,133},{70,134},{71... | collective-permute-start | bytes 294920 | tf_op jit(solution)/shard_map/ppermute | solution.py:502
  40.3 1.9 %collective-permute-start.2 = (f32[192,128]{1,0:T(8,128)S(1)}, f32[192,128]{1,0:T(8,128)S(1)}, u32[]{:S(2)}, u32[]{:S(2)}) collective-permute-start(f32[192,128]{1,0:T(8,128)S(1)} %get-tuple-element.35), channel_id=1, source_target_pairs={{0,64},{1,65},{2,66},{3,67},{4,68},{5,69},{6,70},{7,71},{8,72},{9,... | collective-permute-start | bytes 294920 | tf_op jit(solution)/shard_map/ppermute | solution.py:502
  42.3 4.1 %shard_map.70 = (f32[64,128]{1,0:T(8,128)S(1)}, f32[8,5,8,128]{3,2,1,0:T(8,128)S(1)}, f32[12,2,2,5,16,128]{5,4,3,2,1,0:T(8,128)S(1)}, f32[2,2,5,16,128]{4,3,2,1,...) custom-call(f32[8,10,8,128]{3,2,1,0:T(8,128)S(1)} %all-to-all-done.s, ...), custom_call_target="tpu_custom_call" | custom-call | tf_op jit(solution)/shard_map/pallas_call | solution.py:472
  46.3 9.3 %collective-permute-done.3 = f32[192,128]{1,0:T(8,128)S(1)} collective-permute-done((f32[192,128]{1,0:T(8,128)S(1)}, f32[192,128]{1,0:T(8,128)S(1)}, u32[]{:S(2)}, u32[]{:S(2)}) %collective-permute-start.3) | collective-permute-done | bytes 98336 | tf_op jit(solution)/shard_map/ppermute | solution.py:502
  55.6 0.0 collective-permute-done.2
  55.6 3.0 %shard_map.72 = (f32[64,128]{1,0:T(8,128)}, f32[8,5,8,128]{3,2,1,0:T(8,128)S(1)}) custom-call(f32[64,128]{1,0:T(8,128)S(1)} %get-tuple-element.21.inner_depth, f32[8,5,8,128]{3,2,1,0:T(8,128)S(1)} %get-tuple-element.22.inner_pressure, f32[12,2,2,5,16,128]{5,4,3,2,1,0:T(8,128)S(1)} %get-tuple-element.23.seen, ...), custom_call_target="tpu_custom_call" | custom-call | tf_op jit(solution)/shard_map/pallas_call | solution.py:472
  58.6 9.6 %all_to_all.10.pieces = f32[8,5,8,128]{3,2,1,0:T(8,128)S(1)} all-to-all(f32[8,5,8,128]{3,2,1,0:T(8,128)S(1)} %get-tuple-element.31), channel_id=1, replica_groups=mesh['sec'=8,'band'=8,'place'=8] {'place'}, dimensions={0} | all-to-all | bytes 327680 | tf_op jit(solution)/shard_map/all_to_all | solution.py:543
  68.2 0.7 %shard_map.73 = f32[5,1,8,1024]{3,2,1,0:T(8,128)} custom-call(f32[8,5,8,128]{3,2,1,0:T(8,128)S(1)} %all_to_all.10.pieces), custom_call_target="tpu_custom_call" | custom-call | tf_op jit(solution)/shard_map/pallas_call | solution.py:472
  (4 shorter events, 0.1 us)
Async XLA Ops:
  11.9 12.7 %all-to-all-start = ((f32[8,10,8,128]{3,2,1,0:T(8,128)}), f32[8,10,8,128]{3,2,1,0:T(8,128)S(1)}, u32[]{:S(2)}, u32[]{:S(2)}) async-start(f32[8,10,8,128]{3,2,1,0:T(8,128)} %get-tuple-element.17), calls=%async_computation | async-start | bytes 655360 | tf_op jit(solution)/shard_map/all_to_all | solution.py:514
  24.9 7.7 %collective-permute-start.1 = (f32[2,64,128]{2,1,0:T(8,128)S(1)}, f32[2,64,128]{2,1,0:T(8,128)S(1)}, u32[]{:S(2)}, u32[]{:S(2)}) collective-permute-start(f32[2,64,128]{2,1,0:T(8,128)S(1)} %get-tuple-element.38), channel_id=1, source_target_pairs={{1,2},{2,1},{3,4},{4,3},{5,6},{6,5},{7,8},{8,7},{9,10},{10,9},{11,... | collective-permute-start | bytes 196616 | tf_op jit(solution)/shard_map/ppermute | solution.py:502
  27.4 5.2 %collective-permute-start = (f32[2,64,128]{2,1,0:T(8,128)S(1)}, f32[2,64,128]{2,1,0:T(8,128)S(1)}, u32[]{:S(2)}, u32[]{:S(2)}) collective-permute-start(f32[2,64,128]{2,1,0:T(8,128)S(1)} %get-tuple-element.39), channel_id=1, source_target_pairs={{0,1},{1,0},{2,3},{3,2},{4,5},{5,4},{6,7},{7,6},{8,9},{9,8},{10,11... | collective-permute-start | bytes 196616 | tf_op jit(solution)/shard_map/ppermute | solution.py:502
  32.7 22.9 %collective-permute-start.3 = (f32[192,128]{1,0:T(8,128)S(1)}, f32[192,128]{1,0:T(8,128)S(1)}, u32[]{:S(2)}, u32[]{:S(2)}) collective-permute-start(f32[192,128]{1,0:T(8,128)S(1)} %get-tuple-element.34), channel_id=1, source_target_pairs={{64,128},{65,129},{66,130},{67,131},{68,132},{69,133},{70,134},{71... | collective-permute-start | bytes 294920 | tf_op jit(solution)/shard_map/ppermute | solution.py:502
  40.3 15.3 %collective-permute-start.2 = (f32[192,128]{1,0:T(8,128)S(1)}, f32[192,128]{1,0:T(8,128)S(1)}, u32[]{:S(2)}, u32[]{:S(2)}) collective-permute-start(f32[192,128]{1,0:T(8,128)S(1)} %get-tuple-element.35), channel_id=1, source_target_pairs={{0,64},{1,65},{2,66},{3,67},{4,68},{5,69},{6,70},{7,71},{8,72},{9,... | collective-permute-start | bytes 294920 | tf_op jit(solution)/shard_map/ppermute | solution.py:502

commit v4 on v3

--- a/solution.py
+++ b/solution.py
@@ -94,29 +94,38 @@
 
 
 def gather_blocks(
-    pressure, conductance, depth, elevation, mask, pieces, surface, mask_here, sems
+    pressure, conductance, depth, elevation, mask, pieces, surface, soil_here, mask_here, sems, sent
 ):
-    copies = [
-        pltpu.make_async_copy(
-            source.at[:, 0, :, pl.ds(j * LANES, LANES)],
-            pieces.at[j, pl.ds(first, LAYERS)],
-            sems.at[2 * j + first // LAYERS],
-        )
-        for j in range(GROUP)
-        for source, first in ((pressure, 0), (conductance, LAYERS))
+    arriving = [
+        pltpu.make_async_copy(source, goal, sems.at[i])
+        for i, (source, goal) in enumerate(
+            (
+                (pressure.at[:, 0], soil_here.at[0]),
+                (conductance.at[:, 0], soil_here.at[1]),
+                (depth, surface.at[0]),
+                (elevation, surface.at[1]),
+                (mask, mask_here),
+            )
+        )
     ]
-    count = len(copies)
-    copies += [
-        pltpu.make_async_copy(source, goal, sems.at[count + i])
-        for i, (source, goal) in enumerate(
-            ((depth, surface.at[0]), (elevation, surface.at[1]), (mask, mask_here))
-        )
-    ]
-    for copy in copies:
+    for copy in arriving:
         copy.start()
-    for copy in reversed(copies):
+    leaving = []
+    for half in range(2):
+        arriving[half].wait()
+        for j in range(GROUP):
+            copy = pltpu.make_async_copy(
+                soil_here.at[half, :, :, pl.ds(j * LANES, LANES)],
+                pieces.at[j, pl.ds(half * LAYERS, LAYERS)],
+                sent.at[half * GROUP + j],
+            )
+            copy.start()
+            leaving.append(copy)
+    for copy in arriving[2:]:
         copy.wait()
     surface[2] = mask_here[...].astype(jnp.float32)
+    for copy in leaving:
+        copy.wait()
 
 
 def scatter_blocks(pieces, pressure, sems):
@@ -507,7 +516,12 @@
         pieces, surface = call(
             gather_blocks,
             [(GROUP, SOIL, SUB, LANES), (3, ROWS, LANES)],
-            [pltpu.VMEM((ROWS, LANES), jnp.int32), pltpu.SemaphoreType.DMA((2 * GROUP + 3,))],
+            [
+                (2, LAYERS, SUB, GROUP * LANES),
+                pltpu.VMEM((ROWS, LANES), jnp.int32),
+                pltpu.SemaphoreType.DMA((5,)),
+                pltpu.SemaphoreType.DMA((2 * GROUP,)),
+            ],
             pressure, conductance, depth, elevation, land_mask,
             places=[pltpu.HBM] * 5 + [pl.ANY, pltpu.VMEM],
         )

time: 69.3 us -> 59.8 us (0.86)
  Pallas kernels: 19.3 us -> 9.95 us
    pallas_call x6, Pallas kernels: 19.3 us -> 9.95 us  [call(): pl.pallas_call(kernel, out_shape=[jax.ShapeDtypeStruct(shape, jnp.float32...]
  transfers between devices with their start and end apart: 5 -> 5, of which waited for: 3 -> 3; matrix products, arithmetic and copies ran while one was open for 0% -> 0% of each run, Pallas kernels for 6% -> 7%
where the time goes in v4:
time: 59.8 us; the launch traced here: 59.5 us
  waiting for transfers between devices  20.7 us (35%)
  starting transfers between devices  18.5 us (31%)
  Pallas kernels  9.95 us (17%)
  blocking collectives  9.55 us (16%)
  between operations  0.72 us (1%)
    ppermute x4, starting transfers between devices, swap(): return lax.ppermute(value, axes, pairs(along, odd))  14 us
    ppermute x4, waiting for transfers between devices, swap(): return lax.ppermute(value, axes, pairs(along, odd))  12.4 us
    pallas_call x6, Pallas kernels, call(): pl.pallas_call(kernel, out_shape=[jax.ShapeDtypeStruct(shape, jnp.float32...  9.95 us
    all_to_all x1, blocking collectives, local(): soil = lax.all_to_all(soil, 'place', 0, 0)  9.55 us
    all_to_all x1, waiting for transfers between devices, local(): soil = lax.all_to_all(pieces, 'place', 0, 0)  8.24 us
    all_to_all x1, starting transfers between devices, local(): soil = lax.all_to_all(pieces, 'place', 0, 0)  4.48 us
  transfers between devices with their start and end apart: 5, of which 3 were waited for; matrix products, arithmetic and copies ran while one was open for 0% of the time, Pallas kernels for 7%

profile of v4, /device:TPU:448, one launch (start us, length us, event | category | flops | bytes accessed | tf_op | source)
XLA Modules:
  0.0 59.5 jit_solution(15393093971851071088)
XLA Ops:
  0.6 1.8 %shard_map.68 = (f32[8,10,8,128]{3,2,1,0:T(8,128)}, f32[3,64,128]{2,1,0:T(8,128)S(1)}) custom-call(f32[5,1,8,1024]{3,2,1,0:T(8,128)} %pressure.1, f32[5,1,8,1024]{3,2,1,0:T(8,128)} %conductance.1, f32[64,128]{1,0:T(8,128)} %depth.1, f32[64,128]{1,0:T(8,128)} %elevation.1, s32[64,128]{1,0:T(8,128)} %mask.1), custom_call_target="tpu_custom_call" | custom-call | tf_op jit(solution)/shard_map/pallas_call | solution.py:481
  2.5 4.5 %all-to-all-start = ((f32[8,10,8,128]{3,2,1,0:T(8,128)}), f32[8,10,8,128]{3,2,1,0:T(8,128)S(1)}, u32[]{:S(2)}, u32[]{:S(2)}) async-start(f32[8,10,8,128]{3,2,1,0:T(8,128)} %get-tuple-element.17), calls=%async_computation | async-start | bytes 655360 | tf_op jit(solution)/shard_map/all_to_all | solution.py:528
  7.0 8.2 %all-to-all-done.soil = f32[8,10,8,128]{3,2,1,0:T(8,128)S(1)} async-done(((f32[8,10,8,128]{3,2,1,0:T(8,128)}), f32[8,10,8,128]{3,2,1,0:T(8,128)S(1)}, u32[]{:S(2)}, u32[]{:S(2)}) %all-to-all-start) | async-done | bytes 327712 | tf_op jit(solution)/shard_map/all_to_all | solution.py:528
  15.2 0.3 shard_map.69
  15.5 2.5 %collective-permute-start.1 = (f32[2,64,128]{2,1,0:T(8,128)S(1)}, f32[2,64,128]{2,1,0:T(8,128)S(1)}, u32[]{:S(2)}, u32[]{:S(2)}) collective-permute-start(f32[2,64,128]{2,1,0:T(8,128)S(1)} %get-tuple-element.38), channel_id=1, source_target_pairs={{1,2},{2,1},{3,4},{4,3},{5,6},{6,5},{7,8},{8,7},{9,10},{10,9},{11,... | collective-permute-start | bytes 196616 | tf_op jit(solution)/shard_map/ppermute | solution.py:511
  18.0 2.0 %collective-permute-start = (f32[2,64,128]{2,1,0:T(8,128)S(1)}, f32[2,64,128]{2,1,0:T(8,128)S(1)}, u32[]{:S(2)}, u32[]{:S(2)}) collective-permute-start(f32[2,64,128]{2,1,0:T(8,128)S(1)} %get-tuple-element.39), channel_id=1, source_target_pairs={{0,1},{1,0},{2,3},{3,2},{4,5},{5,4},{6,7},{7,6},{8,9},{9,8},{10,11... | collective-permute-start | bytes 196616 | tf_op jit(solution)/shard_map/ppermute | solution.py:511
  20.0 3.2 %collective-permute-done.1 = f32[2,64,128]{2,1,0:T(8,128)S(1)} collective-permute-done((f32[2,64,128]{2,1,0:T(8,128)S(1)}, f32[2,64,128]{2,1,0:T(8,128)S(1)}, u32[]{:S(2)}, u32[]{:S(2)}) %collective-permute-start.1) | collective-permute-done | bytes 65568 | tf_op jit(solution)/shard_map/ppermute | solution.py:511
  23.2 0.0 collective-permute-done
  23.2 0.1 shard_map.71
  23.3 7.6 %collective-permute-start.3 = (f32[192,128]{1,0:T(8,128)S(1)}, f32[192,128]{1,0:T(8,128)S(1)}, u32[]{:S(2)}, u32[]{:S(2)}) collective-permute-start(f32[192,128]{1,0:T(8,128)S(1)} %get-tuple-element.34), channel_id=1, source_target_pairs={{64,128},{65,129},{66,130},{67,131},{68,132},{69,133},{70,134},{71... | collective-permute-start | bytes 294920 | tf_op jit(solution)/shard_map/ppermute | solution.py:511
  31.0 1.9 %collective-permute-start.2 = (f32[192,128]{1,0:T(8,128)S(1)}, f32[192,128]{1,0:T(8,128)S(1)}, u32[]{:S(2)}, u32[]{:S(2)}) collective-permute-start(f32[192,128]{1,0:T(8,128)S(1)} %get-tuple-element.35), channel_id=1, source_target_pairs={{0,64},{1,65},{2,66},{3,67},{4,68},{5,69},{6,70},{7,71},{8,72},{9,... | collective-permute-start | bytes 294920 | tf_op jit(solution)/shard_map/ppermute | solution.py:511
  32.9 4.1 %shard_map.70 = (f32[64,128]{1,0:T(8,128)S(1)}, f32[8,5,8,128]{3,2,1,0:T(8,128)S(1)}, f32[12,2,2,5,16,128]{5,4,3,2,1,0:T(8,128)S(1)}, f32[2,2,5,16,128]{4,3,2,1,...) custom-call(f32[8,10,8,128]{3,2,1,0:T(8,128)S(1)} %all-to-all-done.s, ...), custom_call_target="tpu_custom_call" | custom-call | tf_op jit(solution)/shard_map/pallas_call | solution.py:481
  37.0 9.3 %collective-permute-done.3 = f32[192,128]{1,0:T(8,128)S(1)} collective-permute-done((f32[192,128]{1,0:T(8,128)S(1)}, f32[192,128]{1,0:T(8,128)S(1)}, u32[]{:S(2)}, u32[]{:S(2)}) %collective-permute-start.3) | collective-permute-done | bytes 98336 | tf_op jit(solution)/shard_map/ppermute | solution.py:511
  46.2 0.0 collective-permute-done.2
  46.3 3.0 %shard_map.72 = (f32[64,128]{1,0:T(8,128)}, f32[8,5,8,128]{3,2,1,0:T(8,128)S(1)}) custom-call(f32[64,128]{1,0:T(8,128)S(1)} %get-tuple-element.21.inner_depth, f32[8,5,8,128]{3,2,1,0:T(8,128)S(1)} %get-tuple-element.22.inner_pressure, f32[12,2,2,5,16,128]{5,4,3,2,1,0:T(8,128)S(1)} %get-tuple-element.23.seen, ...), custom_call_target="tpu_custom_call" | custom-call | tf_op jit(solution)/shard_map/pallas_call | solution.py:481
  49.2 9.6 %all_to_all.10.pieces = f32[8,5,8,128]{3,2,1,0:T(8,128)S(1)} all-to-all(f32[8,5,8,128]{3,2,1,0:T(8,128)S(1)} %get-tuple-element.31), channel_id=1, replica_groups=mesh['sec'=8,'band'=8,'place'=8] {'place'}, dimensions={0} | all-to-all | bytes 327680 | tf_op jit(solution)/shard_map/all_to_all | solution.py:557
  58.8 0.7 %shard_map.73 = f32[5,1,8,1024]{3,2,1,0:T(8,128)} custom-call(f32[8,5,8,128]{3,2,1,0:T(8,128)S(1)} %all_to_all.10.pieces), custom_call_target="tpu_custom_call" | custom-call | tf_op jit(solution)/shard_map/pallas_call | solution.py:481
  (4 shorter events, 0.1 us)
Async XLA Ops:
  2.5 12.7 %all-to-all-start = ((f32[8,10,8,128]{3,2,1,0:T(8,128)}), f32[8,10,8,128]{3,2,1,0:T(8,128)S(1)}, u32[]{:S(2)}, u32[]{:S(2)}) async-start(f32[8,10,8,128]{3,2,1,0:T(8,128)} %get-tuple-element.17), calls=%async_computation | async-start | bytes 655360 | tf_op jit(solution)/shard_map/all_to_all | solution.py:528
  15.5 7.7 %collective-permute-start.1 = (f32[2,64,128]{2,1,0:T(8,128)S(1)}, f32[2,64,128]{2,1,0:T(8,128)S(1)}, u32[]{:S(2)}, u32[]{:S(2)}) collective-permute-start(f32[2,64,128]{2,1,0:T(8,128)S(1)} %get-tuple-element.38), channel_id=1, source_target_pairs={{1,2},{2,1},{3,4},{4,3},{5,6},{6,5},{7,8},{8,7},{9,10},{10,9},{11,... | collective-permute-start | bytes 196616 | tf_op jit(solution)/shard_map/ppermute | solution.py:511
  18.0 5.2 %collective-permute-start = (f32[2,64,128]{2,1,0:T(8,128)S(1)}, f32[2,64,128]{2,1,0:T(8,128)S(1)}, u32[]{:S(2)}, u32[]{:S(2)}) collective-permute-start(f32[2,64,128]{2,1,0:T(8,128)S(1)} %get-tuple-element.39), channel_id=1, source_target_pairs={{0,1},{1,0},{2,3},{3,2},{4,5},{5,4},{6,7},{7,6},{8,9},{9,8},{10,11... | collective-permute-start | bytes 196616 | tf_op jit(solution)/shard_map/ppermute | solution.py:511
  23.3 22.9 %collective-permute-start.3 = (f32[192,128]{1,0:T(8,128)S(1)}, f32[192,128]{1,0:T(8,128)S(1)}, u32[]{:S(2)}, u32[]{:S(2)}) collective-permute-start(f32[192,128]{1,0:T(8,128)S(1)} %get-tuple-element.34), channel_id=1, source_target_pairs={{64,128},{65,129},{66,130},{67,131},{68,132},{69,133},{70,134},{71... | collective-permute-start | bytes 294920 | tf_op jit(solution)/shard_map/ppermute | solution.py:511
  31.0 15.3 %collective-permute-start.2 = (f32[192,128]{1,0:T(8,128)S(1)}, f32[192,128]{1,0:T(8,128)S(1)}, u32[]{:S(2)}, u32[]{:S(2)}) collective-permute-start(f32[192,128]{1,0:T(8,128)S(1)} %get-tuple-element.35), channel_id=1, source_target_pairs={{0,64},{1,65},{2,66},{3,67},{4,68},{5,69},{6,70},{7,71},{8,72},{9,... | collective-permute-start | bytes 294920 | tf_op jit(solution)/shard_map/ppermute | solution.py:511

commit v5 on v4

--- a/solution.py
+++ b/solution.py
@@ -24,7 +24,12 @@
 SUB = 8
 LANES = 128
 ROWS = 64
-STRIP = FIELDS * HALO + 3 * HALO
+REACH = (HALO,) * SOIL + (HALO - 1, HALO - SWEEPS, HALO - SWEEPS - 1)
+STARTS = tuple(sum(REACH[:field]) for field in range(FIELDS))
+CORNERS = sum(REACH)
+CORNERS_TOP = CORNERS + HALO
+FOLD = 3 * HALO
+STRIP = -(-(CORNERS_TOP + HALO // 3) // SUB) * SUB
 
 
 def sweep_factors(number):
@@ -65,22 +70,53 @@
             right[plane, pl.ds(p * SUB, SUB), :] = rights
 
 
-def pack_rows(soil, surface, from_left, from_right, top, bottom):
-    half = HALO - SUB
-    for field in range(FIELDS):
-        at = field * HALO
-        get = lambda p: own_rows(soil, surface, field, p)
-        top[pl.ds(at, SUB), :] = get(0)
-        top[pl.ds(at + SUB, half), :] = get(1)[:half]
-        bottom[pl.ds(at, half), :] = get(GROUP - 2)[SUB - half :]
-        bottom[pl.ds(at + half, SUB), :] = get(GROUP - 1)
-    lane = lane_index(HALO)
-    for out, first in ((top, 0), (bottom, ROWS - HALO)):
-        rows = pl.ds(first, HALO)
-        out[pl.ds(FIELDS * HALO, HALO), :] = from_left[0, rows, :]
-        out[pl.ds((FIELDS + 1) * HALO, HALO), :] = from_right[0, rows, :]
-        out[pl.ds((FIELDS + 2) * HALO, HALO), :] = jnp.where(
-            lane < 64, from_left[1, rows, :], turn(from_right[1, rows, :], 64)
+def facing(edge):
+    if edge == 0:
+        return [(i, HALO - 2 - i, HALO - 1 - i) for i in range(HALO - 1)]
+    return [(i, HALO - i, i) for i in range(1, HALO)]
+
+
+def pack_rows(soil, surface, from_left, from_right, top, bottom, corner):
+    lane = lane_index(1)
+    column = lane
+    for slot in range(1, LANES // HALO + 1):
+        column = jnp.where(lane >= slot * HALO, lane - slot * HALO, column)
+    for edge, out in enumerate((top, bottom)):
+        for field in range(FIELDS):
+            at, count = STARTS[field], REACH[field]
+            rest = count - SUB
+            if edge == 0:
+                out[pl.ds(at, SUB), :] = own_rows(soil, surface, field, 0)
+                if rest:
+                    out[pl.ds(at + SUB, rest), :] = own_rows(soil, surface, field, 1)[:rest]
+            else:
+                if rest:
+                    out[pl.ds(at, rest), :] = own_rows(soil, surface, field, GROUP - 2)[SUB - rest :]
+                out[pl.ds(at + rest, SUB), :] = own_rows(soil, surface, field, GROUP - 1)
+        first = edge * (ROWS - HALO)
+        corner[...] = jnp.zeros((2 * SUB, LANES), jnp.float32)
+        out[pl.ds(STRIP - SUB, SUB), :] = jnp.zeros((SUB, LANES), jnp.float32)
+        for i, j, right in facing(edge):
+            here, there = pl.ds(first + i, 1), pl.ds(first + j, 1)
+            take = column < right
+            out[pl.ds(CORNERS + i, 1), :] = jnp.where(
+                take, from_right[0, here, :], from_left[0, there, :]
+            )
+            corner[pl.ds(i, 1), :] = jnp.where(
+                take, from_right[1, here, :], from_left[1, there, :]
+            )
+        spare = 0 if edge else HALO - 1
+        out[pl.ds(CORNERS + spare, 1), :] = jnp.zeros((1, LANES), jnp.float32)
+        some = HALO // 3
+        lanes = lane_index(some)
+        out[pl.ds(CORNERS_TOP, some), :] = jnp.where(
+            lanes < FOLD,
+            corner[pl.ds(0, some), :],
+            jnp.where(
+                lanes < 2 * FOLD,
+                turn(corner[pl.ds(some, some), :], FOLD),
+                turn(corner[pl.ds(2 * some, some), :], 2 * FOLD),
+            ),
         )
 
 
@@ -141,10 +177,10 @@
         copy.wait()
 
 
-def spread(lefts, rights, lane, slot, shift=0):
+def spread(lefts, rights, lane, slot):
     return jnp.where(
         lane < HALO,
-        turn(rights, -slot * HALO - shift),
+        turn(rights, -slot * HALO),
         jnp.where(lane >= LANES - HALO, turn(lefts, LANES - HALO - slot * HALO), 0.0),
     )
 
@@ -367,7 +403,7 @@
 def edges(
     inner_depth, inner_pressure, seen, seen_k, seen_d, seen_e, seen_m, above, below,
     depth_out, pressure_out,
-    K, U, X, Y, C, east, west, south, north, down, inverse, side, D, E, M, H, B,
+    K, U, X, Y, C, east, west, south, north, down, inverse, side, D, E, M, H, B, corner,
 ):
     factors = sweep_factors(SWEEPS)
     wide = 2 * SUB
@@ -376,22 +412,36 @@
     clear(everything, pl.ds(2 * NEAR, EDGE - 2 * NEAR))
     clear((X, Y), pl.ds(NEAR, NEAR))
     lane = lane_index(HALO)
+    some = HALO // 3
     own = pl.ds(NEAR, NEAR)
-    for edge, (packed, top) in enumerate(((above, NEAR - HALO), (below, 2 * NEAR))):
-        rows = pl.ds(top, HALO)
-        lefts = packed[pl.ds(FIELDS * HALO, HALO), :]
-        rights = packed[pl.ds((FIELDS + 1) * HALO, HALO), :]
-        both = packed[pl.ds((FIELDS + 2) * HALO, HALO), :]
+    clear((corner,), pl.ds(0, NEAR))
+    for edge, packed in enumerate((above, below)):
+        for part in range(3):
+            corner[edge, 1, pl.ds(part * some, some), :] = turn(
+                packed[pl.ds(CORNERS_TOP, some), :], -part * FOLD
+            )
+        corner[edge, 0, pl.ds(0, HALO), :] = packed[pl.ds(CORNERS, HALO), :]
+        for i, j, _ in facing(1 - edge):
+            for half in range(2):
+                corner[edge, 2 + half, pl.ds(j, 1), :] = corner[edge, half, pl.ds(i, 1), :]
+        whole = pl.ds(0, HALO)
+        rows = pl.ds(2 * NEAR if edge else NEAR - HALO, HALO)
         for field in range(FIELDS):
-            value = packed[pl.ds(field * HALO, HALO), :]
+            count = REACH[field]
+            filled = pl.ds(2 * NEAR if edge else NEAR - count, count)
+            value = packed[pl.ds(STARTS[field], count), :]
+            half, slot = (0, field) if field < SOIL else (1, field - SOIL)
+            sides = spread(
+                corner[edge, 2 + half, whole, :], corner[edge, half, whole, :], lane, slot
+            )
             if field < SOIL:
                 ref, layer = (U, K)[field // LAYERS], field % LAYERS
-                ref[edge, 0, layer, rows, :] = value
-                ref[edge, 1, layer, rows, :] = spread(lefts, rights, lane, field)
+                ref[edge, 0, layer, filled, :] = value
+                ref[edge, 1, layer, rows, :] = sides
             else:
                 ref = (D, E, M)[field - SOIL]
-                ref[edge, 0, rows, :] = value
-                ref[edge, 1, rows, :] = spread(both, both, lane, field - SOIL, 64)
+                ref[edge, 0, filled, :] = value
+                ref[edge, 1, rows, :] = sides
         for plane in PLANES:
             D[edge, plane, own, :] = seen_d[0, edge, plane]
             E[edge, plane, own, :] = seen_e[edge, plane]
@@ -525,6 +575,7 @@
             pressure, conductance, depth, elevation, land_mask,
             places=[pltpu.HBM] * 5 + [pl.ANY, pltpu.VMEM],
         )
+        pieces, tile_odd, sec_odd = lax.optimization_barrier((pieces, tile_odd, sec_odd))
         soil = lax.all_to_all(pieces, "place", 0, 0)
         own = (soil, surface)
         left, right = call(pack_columns, [(2, ROWS, LANES)] * 2, [], *own)
@@ -532,7 +583,9 @@
         two = swap(jnp.where(tile_odd, right, left), "tile", 1)
         from_left = jnp.where(tile_odd, one, two)
         from_right = jnp.where(tile_odd, two, one)
-        top, bottom = call(pack_rows, [(STRIP, LANES)] * 2, [], *own, from_left, from_right)
+        top, bottom = call(
+            pack_rows, [(STRIP, LANES)] * 2, [(2 * SUB, LANES)], *own, from_left, from_right
+        )
         one = swap(jnp.where(sec_odd, bottom, top), "sec", 1)
         two = swap(jnp.where(sec_odd, top, bottom), "sec", 0)
         above = jnp.where(sec_odd, two, one)
@@ -552,7 +605,7 @@
             (2, 2, EDGE, LANES),
         )
         depth, soil = call(
-            edges, shapes, [field] * 5 + [face] * 7 + [layer] * 5, *held, above, below
+            edges, shapes, [field] * 5 + [face] * 7 + [layer] * 5 + [(2, 4, NEAR, LANES)], *held, above, below
         )
         soil = lax.all_to_all(soil, "place", 0, 0)
         [soil] = call(

time: 59.8 us -> 58 us (0.970)
  blocking collectives: 9.55 us -> 21.6 us
  waiting for transfers between devices: 20.7 us -> 11.6 us
  starting transfers between devices: 18.5 us -> 14.4 us
    all_to_all x0 -> x1, blocking collectives: none -> 12.5 us  [local(): soil = lax.all_to_all(pieces, 'place', 0, 0)]
    all_to_all x1 -> x0, waiting for transfers between devices: 8.24 us -> none  [local(): soil = lax.all_to_all(pieces, 'place', 0, 0)]
    all_to_all x1 -> x0, starting transfers between devices: 4.48 us -> none  [local(): soil = lax.all_to_all(pieces, 'place', 0, 0)]
    ppermute x4, waiting for transfers between devices: 12.4 us -> 11.6 us  [swap(): return lax.ppermute(value, axes, pairs(along, odd))]
  transfers between devices with their start and end apart: 5 -> 4, of which waited for: 3 -> 2; matrix products, arithmetic and copies ran while one was open for 0% -> 0% of each run, Pallas kernels for 7% -> 7%
where the time goes in v5:
time: 58 us; the launch traced here: 57.7 us
  blocking collectives  21.6 us (37%)
  starting transfers between devices  14.4 us (25%)
  waiting for transfers between devices  11.6 us (20%)
  Pallas kernels  9.44 us (16%)
  between operations  0.74 us (1%)
    ppermute x4, starting transfers between devices, swap(): return lax.ppermute(value, axes, pairs(along, odd))  14.4 us
    all_to_all x1, blocking collectives, local(): soil = lax.all_to_all(pieces, 'place', 0, 0)  12.5 us
    ppermute x4, waiting for transfers between devices, swap(): return lax.ppermute(value, axes, pairs(along, odd))  11.6 us
    pallas_call x6, Pallas kernels, call(): pl.pallas_call(kernel, out_shape=[jax.ShapeDtypeStruct(shape, jnp.float32...  9.44 us
    all_to_all x1, blocking collectives, local(): soil = lax.all_to_all(soil, 'place', 0, 0)  9.04 us
  transfers between devices with their start and end apart: 4, of which 2 were waited for; matrix products, arithmetic and copies ran while one was open for 0% of the time, Pallas kernels for 7%

profile of v5, /device:TPU:448, one launch (start us, length us, event | category | flops | bytes accessed | tf_op | source)
XLA Modules:
  0.0 57.7 jit_solution(10889732055216464037)
XLA Ops:
  0.7 1.2 %shard_map.68 = (f32[8,10,8,128]{3,2,1,0:T(8,128)S(1)}, f32[3,64,128]{2,1,0:T(8,128)S(1)}) custom-call(f32[5,1,8,1024]{3,2,1,0:T(8,128)} %pressure.1, f32[5,1,8,1024]{3,2,1,0:T(8,128)} %conductance.1, f32[64,128]{1,0:T(8,128)} %depth.1, f32[64,128]{1,0:T(8,128)} %elevation.1, s32[64,128]{1,0:T(8,128)} %mask.1), custom_call_target="tpu_custom_call" | custom-call | tf_op jit(solution)/shard_map/pallas_call | solution.py:531
  1.9 12.5 %all_to_all.10.soil = f32[8,10,8,128]{3,2,1,0:T(8,128)S(1)} all-to-all(f32[8,10,8,128]{3,2,1,0:T(8,128)S(1)} %get-tuple-element.21), channel_id=1, replica_groups=mesh['sec'=8,'band'=8,'place'=8] {'place'}, dimensions={0} | all-to-all | bytes 655360 | tf_op jit(solution)/shard_map/all_to_all | solution.py:579
  14.4 0.3 shard_map.69
  14.7 2.9 %collective-permute-start.1 = (f32[2,64,128]{2,1,0:T(8,128)S(1)}, f32[2,64,128]{2,1,0:T(8,128)S(1)}, u32[]{:S(2)}, u32[]{:S(2)}) collective-permute-start(f32[2,64,128]{2,1,0:T(8,128)S(1)} %get-tuple-element.44), channel_id=1, source_target_pairs={{1,2},{2,1},{3,4},{4,3},{5,6},{6,5},{7,8},{8,7},{9,10},{10,9},{11,... | collective-permute-start | bytes 196616 | tf_op jit(solution)/shard_map/ppermute | solution.py:561
  17.6 1.9 %collective-permute-start = (f32[2,64,128]{2,1,0:T(8,128)S(1)}, f32[2,64,128]{2,1,0:T(8,128)S(1)}, u32[]{:S(2)}, u32[]{:S(2)}) collective-permute-start(f32[2,64,128]{2,1,0:T(8,128)S(1)} %get-tuple-element.45), channel_id=1, source_target_pairs={{0,1},{1,0},{2,3},{3,2},{4,5},{5,4},{6,7},{7,6},{8,9},{9,8},{10,11... | collective-permute-start | bytes 196616 | tf_op jit(solution)/shard_map/ppermute | solution.py:561
  19.5 2.9 %collective-permute-done.1 = f32[2,64,128]{2,1,0:T(8,128)S(1)} collective-permute-done((f32[2,64,128]{2,1,0:T(8,128)S(1)}, f32[2,64,128]{2,1,0:T(8,128)S(1)}, u32[]{:S(2)}, u32[]{:S(2)}) %collective-permute-start.1) | collective-permute-done | bytes 65568 | tf_op jit(solution)/shard_map/ppermute | solution.py:561
  22.4 0.0 collective-permute-done
  22.4 0.1 shard_map.71
  22.6 7.6 %collective-permute-start.3 = (f32[168,128]{1,0:T(8,128)S(1)}, f32[168,128]{1,0:T(8,128)S(1)}, u32[]{:S(2)}, u32[]{:S(2)}) collective-permute-start(f32[168,128]{1,0:T(8,128)S(1)} %get-tuple-element.40), channel_id=1, source_target_pairs={{64,128},{65,129},{66,130},{67,131},{68,132},{69,133},{70,134},{71... | collective-permute-start | bytes 258056 | tf_op jit(solution)/shard_map/ppermute | solution.py:561
  30.2 1.9 %collective-permute-start.2 = (f32[168,128]{1,0:T(8,128)S(1)}, f32[168,128]{1,0:T(8,128)S(1)}, u32[]{:S(2)}, u32[]{:S(2)}) collective-permute-start(f32[168,128]{1,0:T(8,128)S(1)} %get-tuple-element.41), channel_id=1, source_target_pairs={{0,64},{1,65},{2,66},{3,67},{4,68},{5,69},{6,70},{7,71},{8,72},{9,... | collective-permute-start | bytes 258056 | tf_op jit(solution)/shard_map/ppermute | solution.py:561
  32.1 4.1 %shard_map.70 = (f32[64,128]{1,0:T(8,128)S(1)}, f32[8,5,8,128]{3,2,1,0:T(8,128)S(1)}, f32[12,2,2,5,16,128]{5,4,3,2,1,0:T(8,128)S(1)}, f32[2,2,5,16,128]{4,3,2,1,...) custom-call(f32[8,10,8,128]{3,2,1,0:T(8,128)S(1)} %all_to_all.10.soi, ...), custom_call_target="tpu_custom_call" | custom-call | tf_op jit(solution)/shard_map/pallas_call | solution.py:531
  36.2 8.7 %collective-permute-done.3 = f32[168,128]{1,0:T(8,128)S(1)} collective-permute-done((f32[168,128]{1,0:T(8,128)S(1)}, f32[168,128]{1,0:T(8,128)S(1)}, u32[]{:S(2)}, u32[]{:S(2)}) %collective-permute-start.3) | collective-permute-done | bytes 86048 | tf_op jit(solution)/shard_map/ppermute | solution.py:561
  44.9 0.0 collective-permute-done.2
  44.9 3.0 %shard_map.72 = (f32[64,128]{1,0:T(8,128)}, f32[8,5,8,128]{3,2,1,0:T(8,128)S(1)}) custom-call(f32[64,128]{1,0:T(8,128)S(1)} %get-tuple-element.26.inner_depth, f32[8,5,8,128]{3,2,1,0:T(8,128)S(1)} %get-tuple-element.27.inner_pressure, f32[12,2,2,5,16,128]{5,4,3,2,1,0:T(8,128)S(1)} %get-tuple-element.28.seen, ...), custom_call_target="tpu_custom_call" | custom-call | tf_op jit(solution)/shard_map/pallas_call | solution.py:531
  48.0 9.0 %all_to_all.11.pieces = f32[8,5,8,128]{3,2,1,0:T(8,128)S(1)} all-to-all(f32[8,5,8,128]{3,2,1,0:T(8,128)S(1)} %get-tuple-element.37), channel_id=1, replica_groups=mesh['sec'=8,'band'=8,'place'=8] {'place'}, dimensions={0} | all-to-all | bytes 327680 | tf_op jit(solution)/shard_map/all_to_all | solution.py:610
  57.0 0.7 %shard_map.73 = f32[5,1,8,1024]{3,2,1,0:T(8,128)} custom-call(f32[8,5,8,128]{3,2,1,0:T(8,128)S(1)} %all_to_all.11.pieces), custom_call_target="tpu_custom_call" | custom-call | tf_op jit(solution)/shard_map/pallas_call | solution.py:531
  (4 shorter events, 0.1 us)
Async XLA Ops:
  14.7 7.7 %collective-permute-start.1 = (f32[2,64,128]{2,1,0:T(8,128)S(1)}, f32[2,64,128]{2,1,0:T(8,128)S(1)}, u32[]{:S(2)}, u32[]{:S(2)}) collective-permute-start(f32[2,64,128]{2,1,0:T(8,128)S(1)} %get-tuple-element.44), channel_id=1, source_target_pairs={{1,2},{2,1},{3,4},{4,3},{5,6},{6,5},{7,8},{8,7},{9,10},{10,9},{11,... | collective-permute-start | bytes 196616 | tf_op jit(solution)/shard_map/ppermute | solution.py:561
  17.6 4.8 %collective-permute-start = (f32[2,64,128]{2,1,0:T(8,128)S(1)}, f32[2,64,128]{2,1,0:T(8,128)S(1)}, u32[]{:S(2)}, u32[]{:S(2)}) collective-permute-start(f32[2,64,128]{2,1,0:T(8,128)S(1)} %get-tuple-element.45), channel_id=1, source_target_pairs={{0,1},{1,0},{2,3},{3,2},{4,5},{5,4},{6,7},{7,6},{8,9},{9,8},{10,11... | collective-permute-start | bytes 196616 | tf_op jit(solution)/shard_map/ppermute | solution.py:561
  22.6 22.4 %collective-permute-start.3 = (f32[168,128]{1,0:T(8,128)S(1)}, f32[168,128]{1,0:T(8,128)S(1)}, u32[]{:S(2)}, u32[]{:S(2)}) collective-permute-start(f32[168,128]{1,0:T(8,128)S(1)} %get-tuple-element.40), channel_id=1, source_target_pairs={{64,128},{65,129},{66,130},{67,131},{68,132},{69,133},{70,134},{71... | collective-permute-start | bytes 258056 | tf_op jit(solution)/shard_map/ppermute | solution.py:561
  30.2 14.7 %collective-permute-start.2 = (f32[168,128]{1,0:T(8,128)S(1)}, f32[168,128]{1,0:T(8,128)S(1)}, u32[]{:S(2)}, u32[]{:S(2)}) collective-permute-start(f32[168,128]{1,0:T(8,128)S(1)} %get-tuple-element.41), channel_id=1, source_target_pairs={{0,64},{1,65},{2,66},{3,67},{4,68},{5,69},{6,70},{7,71},{8,72},{9,... | collective-permute-start | bytes 258056 | tf_op jit(solution)/shard_map/ppermute | solution.py:561

commit v6 on v5

--- a/solution.py
+++ b/solution.py
@@ -55,19 +55,24 @@
     return surface[field - SOIL, pl.ds(p * SUB, SUB), :]
 
 
-def pack_columns(soil, surface, left, right):
+def edge_columns(values, lane):
+    left = right = jnp.zeros(values[0].shape, jnp.float32)
+    for slot, value in enumerate(values):
+        here = (lane >= slot * HALO) & (lane < slot * HALO + HALO)
+        left = jnp.where(here, turn(value, slot * HALO), left)
+        right = jnp.where(here, turn(value, slot * HALO + HALO), right)
+    return left, right
+
+
+def pack_columns(soil, left, right):
     lane = lane_index(SUB)
     for p in range(GROUP):
-        for plane, fields in ((0, range(SOIL)), (1, range(SOIL, FIELDS))):
-            lefts = jnp.zeros((SUB, LANES), jnp.float32)
-            rights = jnp.zeros((SUB, LANES), jnp.float32)
-            for slot, field in enumerate(fields):
-                value = own_rows(soil, surface, field, p)
-                here = (lane >= slot * HALO) & (lane < slot * HALO + HALO)
-                lefts = jnp.where(here, turn(value, slot * HALO), lefts)
-                rights = jnp.where(here, turn(value, slot * HALO + HALO), rights)
-            left[plane, pl.ds(p * SUB, SUB), :] = lefts
-            right[plane, pl.ds(p * SUB, SUB), :] = rights
+        rows = pl.ds(p * SUB, SUB)
+        left[rows, :], right[rows, :] = edge_columns([soil[p, f] for f in range(SOIL)], lane)
+
+
+def pack_surface(surface, left, right):
+    left[...], right[...] = edge_columns([surface[i] for i in range(3)], lane_index(ROWS))
 
 
 def facing(edge):
@@ -76,7 +81,9 @@
     return [(i, HALO - i, i) for i in range(1, HALO)]
 
 
-def pack_rows(soil, surface, from_left, from_right, top, bottom, corner):
+def pack_rows(
+    soil, surface, from_left, from_right, over_left, over_right, top, bottom, corner
+):
     lane = lane_index(1)
     column = lane
     for slot in range(1, LANES // HALO + 1):
@@ -100,10 +107,10 @@
             here, there = pl.ds(first + i, 1), pl.ds(first + j, 1)
             take = column < right
             out[pl.ds(CORNERS + i, 1), :] = jnp.where(
-                take, from_right[0, here, :], from_left[0, there, :]
+                take, from_right[here, :], from_left[there, :]
             )
             corner[pl.ds(i, 1), :] = jnp.where(
-                take, from_right[1, here, :], from_left[1, there, :]
+                take, over_right[here, :], over_left[there, :]
             )
         spare = 0 if edge else HALO - 1
         out[pl.ds(CORNERS + spare, 1), :] = jnp.zeros((1, LANES), jnp.float32)
@@ -130,7 +137,7 @@
 
 
 def gather_blocks(
-    pressure, conductance, depth, elevation, mask, pieces, surface, soil_here, mask_here, sems, sent
+    pressure, conductance, depth, elevation, mask, pieces, surface, soil_here, band, mask_here, sems, sent
 ):
     arriving = [
         pltpu.make_async_copy(source, goal, sems.at[i])
@@ -157,6 +164,24 @@
             )
             copy.start()
             leaving.append(copy)
+    lane = lane_index(SUB)
+    ends = [
+        edge_columns(
+            [
+                soil_here[f // LAYERS, f % LAYERS, :, pl.ds(j * LANES, LANES)]
+                for f in range(SOIL)
+            ],
+            lane,
+        )
+        for j in (0, GROUP - 1)
+    ]
+    band[0], band[1] = ends[1][1], ends[0][0]
+    for j in range(GROUP):
+        copy = pltpu.make_async_copy(
+            band.at[min(j, 1)], pieces.at[j, SOIL], sent.at[2 * GROUP + j]
+        )
+        copy.start()
+        leaving.append(copy)
     for copy in arriving[2:]:
         copy.wait()
     surface[2] = mask_here[...].astype(jnp.float32)
@@ -312,7 +337,7 @@
 
 
 def inner(
-    soil, surface, from_left, from_right,
+    soil, surface, from_left, from_right, over_left, over_right,
     depth_out, pressure_out, seen, seen_k, seen_d, seen_e, seen_m,
     K, U, X, Y, C, east, west, south, north, down, inverse, side, D, E, M, H, B,
 ):
@@ -332,7 +357,10 @@
             rows, here = pl.ds(SUB + p * SUB, SUB), pl.ds(p * SUB, SUB)
             at[name(0, rows)] = own_rows(soil, surface, field, p)
             at[name(1, rows)] = spread(
-                from_left[half, here, :], from_right[half, here, :], lane, slot
+                (from_left, over_left)[half][here, :],
+                (from_right, over_right)[half][here, :],
+                lane,
+                slot,
             )
 
     def note(source, number):
@@ -557,34 +585,59 @@
                     found.append((s * tiles + t, goal[0] * tiles + goal[1]))
         return found
 
+    def bands():
+        found = [
+            (i, j)
+            for i, j in pairs("tile", 1)
+            if i % tiles // GROUP == j % tiles // GROUP
+        ]
+        for s in range(secs):
+            for t in range(0, tiles - GROUP, GROUP):
+                here = s * tiles + t
+                found.append((here, here + GROUP))
+                found.append((here + 2 * GROUP - 1, here + GROUP - 1))
+        return found
+
     def swap(value, along, odd):
         return lax.ppermute(value, axes, pairs(along, odd))
 
     def local(depth, elevation, land_mask, pressure, conductance):
-        tile_odd = lax.axis_index("place") % 2 == 1
+        place = lax.axis_index("place")
+        tile_odd = place % 2 == 1
+        tile_end = (place == 0) | (place == GROUP - 1)
         sec_odd = lax.axis_index("sec") % 2 == 1
         pieces, surface = call(
             gather_blocks,
-            [(GROUP, SOIL, SUB, LANES), (3, ROWS, LANES)],
+            [(GROUP, SOIL + 1, SUB, LANES), (3, ROWS, LANES)],
             [
                 (2, LAYERS, SUB, GROUP * LANES),
+                (2, SUB, LANES),
                 pltpu.VMEM((ROWS, LANES), jnp.int32),
                 pltpu.SemaphoreType.DMA((5,)),
-                pltpu.SemaphoreType.DMA((2 * GROUP,)),
+                pltpu.SemaphoreType.DMA((3 * GROUP,)),
             ],
             pressure, conductance, depth, elevation, land_mask,
             places=[pltpu.HBM] * 5 + [pl.ANY, pltpu.VMEM],
         )
-        pieces, tile_odd, sec_odd = lax.optimization_barrier((pieces, tile_odd, sec_odd))
         soil = lax.all_to_all(pieces, "place", 0, 0)
         own = (soil, surface)
-        left, right = call(pack_columns, [(2, ROWS, LANES)] * 2, [], *own)
-        one = swap(jnp.where(tile_odd, left, right), "tile", 0)
-        two = swap(jnp.where(tile_odd, right, left), "tile", 1)
-        from_left = jnp.where(tile_odd, one, two)
-        from_right = jnp.where(tile_odd, two, one)
+        edge = (ROWS, LANES)
+
+        def exchange(left, right, outer, second):
+            one = lax.ppermute(jnp.where(tile_odd, left, right), axes, pairs("tile", 0))
+            two = jnp.where(tile_odd, right, left)
+            if outer is not None:
+                two = jnp.where(tile_end, outer, two)
+            two = lax.ppermute(two, axes, second)
+            return jnp.where(tile_odd, one, two), jnp.where(tile_odd, two, one)
+
+        left, right = call(pack_surface, [edge] * 2, [], surface)
+        over = exchange(left, right, None, pairs("tile", 1))
+        left, right = call(pack_columns, [edge] * 2, [], soil)
+        beyond = exchange(left, right, soil[:, SOIL].reshape(edge), bands())
+        halos = (*beyond, *over)
         top, bottom = call(
-            pack_rows, [(STRIP, LANES)] * 2, [(2 * SUB, LANES)], *own, from_left, from_right
+            pack_rows, [(STRIP, LANES)] * 2, [(2 * SUB, LANES)], *own, *halos
         )
         one = swap(jnp.where(sec_odd, bottom, top), "sec", 1)
         two = swap(jnp.where(sec_odd, top, bottom), "sec", 0)
@@ -597,7 +650,7 @@
             inner,
             shapes + [(SWEEPS * STEPS,) + near, near, (STEPS, 2, 2, NEAR, LANES)] + [(2, 2, NEAR, LANES)] * 2,
             [field] * 12 + [layer] * 5,
-            *own, from_left, from_right,
+            *own, *halos,
         )
         field, face, layer = (
             (2, 2, LAYERS, EDGE, LANES),

time: 58 us -> 58.4 us (level)
  the two profiles are of different devices: /device:TPU:448 before, /device:TPU:4 now
where the time goes in v6:
time: 58.4 us; the launch traced here: 58 us
  starting transfers between devices  34 us (58%)
  Pallas kernels  10.2 us (17%)
  blocking collectives  8.86 us (15%)
  waiting for transfers between devices  3.96 us (7%)
  between operations  0.81 us (1%)
    ppermute x2, starting transfers between devices, swap(): return lax.ppermute(value, axes, pairs(along, odd))  17.8 us
    pallas_call x7, Pallas kernels, call(): pl.pallas_call(kernel, out_shape=[jax.ShapeDtypeStruct(shape, jnp.float32...  10.2 us
    all_to_all x1, blocking collectives, local(): soil = lax.all_to_all(soil, 'place', 0, 0)  8.86 us
    ppermute x2, starting transfers between devices, exchange(): one = lax.ppermute(jnp.where(tile_odd, left, right), axes, pairs('tile', 0))  7.21 us
    ppermute x2, starting transfers between devices, exchange(): two = lax.ppermute(two, axes, second)  4.49 us
    all_to_all x1, starting transfers between devices, local(): soil = lax.all_to_all(pieces, 'place', 0, 0)  4.48 us
    all_to_all x1, waiting for transfers between devices, local(): soil = lax.all_to_all(pieces, 'place', 0, 0)  2.83 us
  transfers between devices with their start and end apart: 7, of which 2 were waited for; matrix products, arithmetic and copies ran while one was open for 0% of the time, Pallas kernels for 8%

profile of v6, /device:TPU:4, one launch (start us, length us, event | category | flops | bytes accessed | tf_op | source)
XLA Modules:
  0.0 58.0 jit_solution(10406394784125109118)
XLA Ops:
  0.6 2.0 %shard_map.68 = (f32[8,11,8,128]{3,2,1,0:T(8,128)}, f32[3,64,128]{2,1,0:T(8,128)S(1)}) custom-call(f32[5,1,8,1024]{3,2,1,0:T(8,128)} %pressure.1, f32[5,1,8,1024]{3,2,1,0:T(8,128)} %conductance.1, f32[64,128]{1,0:T(8,128)} %depth.1, f32[64,128]{1,0:T(8,128)} %elevation.1, s32[64,128]{1,0:T(8,128)} %mask.1), custom_call_target="tpu_custom_call" | custom-call | tf_op jit(solution)/shard_map/pallas_call | solution.py:559
  2.6 4.5 %all-to-all-start = ((f32[8,11,8,128]{3,2,1,0:T(8,128)}), f32[8,11,8,128]{3,2,1,0:T(8,128)S(1)}, u32[]{:S(2)}, u32[]{:S(2)}) async-start(f32[8,11,8,128]{3,2,1,0:T(8,128)} %get-tuple-element.19), calls=%async_computation | async-start | bytes 720896 | tf_op jit(solution)/shard_map/all_to_all | solution.py:622
  7.1 0.1 shard_map.70
  7.2 0.7 %collective-permute-start.3 = (f32[64,128]{1,0:T(8,128)S(1)}, f32[64,128]{1,0:T(8,128)S(1)}, u32[]{:S(2)}, u32[]{:S(2)}) collective-permute-start(f32[64,128]{1,0:T(8,128)S(1)} %get-tuple-element.42), channel_id=1, source_target_pairs={{1,2},{2,1},{3,4},{4,3},{5,6},{6,5},{7,8},{8,7},{9,10},{10,9},{11,... | collective-permute-start | bytes 98312 | tf_op jit(solution)/shard_map/ppermute | solution.py:631
  7.9 5.3 %collective-permute-start.2 = (f32[64,128]{1,0:T(8,128)S(1)}, f32[64,128]{1,0:T(8,128)S(1)}, u32[]{:S(2)}, u32[]{:S(2)}) collective-permute-start(f32[64,128]{1,0:T(8,128)S(1)} %get-tuple-element.43), channel_id=1, source_target_pairs={{0,1},{1,0},{2,3},{3,2},{4,5},{5,4},{6,7},{7,6},{8,9},{9,8},{10,11... | collective-permute-start | bytes 98312 | tf_op jit(solution)/shard_map/ppermute | solution.py:627
  13.2 2.8 %all-to-all-done.soil = f32[8,11,8,128]{3,2,1,0:T(8,128)S(1)} async-done(((f32[8,11,8,128]{3,2,1,0:T(8,128)}), f32[8,11,8,128]{3,2,1,0:T(8,128)S(1)}, u32[]{:S(2)}, u32[]{:S(2)}) %all-to-all-start) | async-done | bytes 360480 | tf_op jit(solution)/shard_map/all_to_all | solution.py:622
  16.0 0.2 shard_map.69
  16.3 3.8 %collective-permute-start.1 = (f32[64,128]{1,0:T(8,128)S(1)}, f32[64,128]{1,0:T(8,128)S(1)}, u32[]{:S(2)}, u32[]{:S(2)}) collective-permute-start(f32[64,128]{1,0:T(8,128)S(1)} %get-tuple-element.46), channel_id=1, source_target_pairs={{1,2},{2,1},{3,4},{4,3},{5,6},{6,5},{9,10},{10,9},{11,12},{12,11},... | collective-permute-start | bytes 98312 | tf_op jit(solution)/shard_map/ppermute | solution.py:631
  20.1 1.9 %collective-permute-start = (f32[64,128]{1,0:T(8,128)S(1)}, f32[64,128]{1,0:T(8,128)S(1)}, u32[]{:S(2)}, u32[]{:S(2)}) collective-permute-start(f32[64,128]{1,0:T(8,128)S(1)} %get-tuple-element.47), channel_id=1, source_target_pairs={{0,1},{1,0},{2,3},{3,2},{4,5},{5,4},{6,7},{7,6},{8,9},{9,8},{10,11... | collective-permute-start | bytes 98312 | tf_op jit(solution)/shard_map/ppermute | solution.py:627
  22.0 0.0 collective-permute-done.3
  22.0 0.0 collective-permute-done.2
  22.1 0.0 collective-permute-done.1
  22.1 1.1 %collective-permute-done = f32[64,128]{1,0:T(8,128)S(1)} collective-permute-done((f32[64,128]{1,0:T(8,128)S(1)}, f32[64,128]{1,0:T(8,128)S(1)}, u32[]{:S(2)}, u32[]{:S(2)}) %collective-permute-start) | collective-permute-done | bytes 32800 | tf_op jit(solution)/shard_map/ppermute | solution.py:627
  23.2 0.1 shard_map.72
  23.4 2.4 %collective-permute-start.5 = (f32[168,128]{1,0:T(8,128)S(1)}, f32[168,128]{1,0:T(8,128)S(1)}, u32[]{:S(2)}, u32[]{:S(2)}) collective-permute-start(f32[168,128]{1,0:T(8,128)S(1)} %get-tuple-element.38), channel_id=1, source_target_pairs={{64,128},{65,129},{66,130},{67,131},{68,132},{69,133},{70,134},{71... | collective-permute-start | bytes 258056 | tf_op jit(solution)/shard_map/ppermute | solution.py:602
  25.8 15.4 %collective-permute-start.4 = (f32[168,128]{1,0:T(8,128)S(1)}, f32[168,128]{1,0:T(8,128)S(1)}, u32[]{:S(2)}, u32[]{:S(2)}) collective-permute-start(f32[168,128]{1,0:T(8,128)S(1)} %get-tuple-element.39), channel_id=1, source_target_pairs={{0,64},{1,65},{2,66},{3,67},{4,68},{5,69},{6,70},{7,71},{8,72},{9,... | collective-permute-start | bytes 258056 | tf_op jit(solution)/shard_map/ppermute | solution.py:602
  41.2 4.1 %shard_map.71 = (f32[64,128]{1,0:T(8,128)S(1)}, f32[8,5,8,128]{3,2,1,0:T(8,128)S(1)}, f32[12,2,2,5,16,128]{5,4,3,2,1,0:T(8,128)S(1)}, f32[2,2,5,16,128]{4,3,2,1,...) custom-call(f32[8,11,8,128]{3,2,1,0:T(8,128)S(1)} %all-to-all-done.s, ...), custom_call_target="tpu_custom_call" | custom-call | tf_op jit(solution)/shard_map/pallas_call | solution.py:559
  45.3 0.0 collective-permute-done.5
  45.3 0.0 collective-permute-done.4
  45.3 3.0 %shard_map.73 = (f32[64,128]{1,0:T(8,128)}, f32[8,5,8,128]{3,2,1,0:T(8,128)S(1)}) custom-call(f32[64,128]{1,0:T(8,128)S(1)} %get-tuple-element.25.inner_depth, f32[8,5,8,128]{3,2,1,0:T(8,128)S(1)} %get-tuple-element.26.inner_pressure, f32[12,2,2,5,16,128]{5,4,3,2,1,0:T(8,128)S(1)} %get-tuple-element.27.seen, ...), custom_call_target="tpu_custom_call" | custom-call | tf_op jit(solution)/shard_map/pallas_call | solution.py:559
  48.4 8.9 %all_to_all.10.pieces = f32[8,5,8,128]{3,2,1,0:T(8,128)S(1)} all-to-all(f32[8,5,8,128]{3,2,1,0:T(8,128)S(1)} %get-tuple-element.35), channel_id=1, replica_groups=mesh['sec'=8,'band'=8,'place'=8] {'place'}, dimensions={0} | all-to-all | bytes 327680 | tf_op jit(solution)/shard_map/all_to_all | solution.py:663
  57.2 0.7 %shard_map.74 = f32[5,1,8,1024]{3,2,1,0:T(8,128)} custom-call(f32[8,5,8,128]{3,2,1,0:T(8,128)S(1)} %all_to_all.10.pieces), custom_call_target="tpu_custom_call" | custom-call | tf_op jit(solution)/shard_map/pallas_call | solution.py:559
  (6 shorter events, 0.1 us)
Async XLA Ops:
  2.6 13.4 %all-to-all-start = ((f32[8,11,8,128]{3,2,1,0:T(8,128)}), f32[8,11,8,128]{3,2,1,0:T(8,128)S(1)}, u32[]{:S(2)}, u32[]{:S(2)}) async-start(f32[8,11,8,128]{3,2,1,0:T(8,128)} %get-tuple-element.19), calls=%async_computation | async-start | bytes 720896 | tf_op jit(solution)/shard_map/all_to_all | solution.py:622
  7.2 14.8 %collective-permute-start.3 = (f32[64,128]{1,0:T(8,128)S(1)}, f32[64,128]{1,0:T(8,128)S(1)}, u32[]{:S(2)}, u32[]{:S(2)}) collective-permute-start(f32[64,128]{1,0:T(8,128)S(1)} %get-tuple-element.42), channel_id=1, source_target_pairs={{1,2},{2,1},{3,4},{4,3},{5,6},{6,5},{7,8},{8,7},{9,10},{10,9},{11,... | collective-permute-start | bytes 98312 | tf_op jit(solution)/shard_map/ppermute | solution.py:631
  7.9 14.2 %collective-permute-start.2 = (f32[64,128]{1,0:T(8,128)S(1)}, f32[64,128]{1,0:T(8,128)S(1)}, u32[]{:S(2)}, u32[]{:S(2)}) collective-permute-start(f32[64,128]{1,0:T(8,128)S(1)} %get-tuple-element.43), channel_id=1, source_target_pairs={{0,1},{1,0},{2,3},{3,2},{4,5},{5,4},{6,7},{7,6},{8,9},{9,8},{10,11... | collective-permute-start | bytes 98312 | tf_op jit(solution)/shard_map/ppermute | solution.py:627
  16.3 5.8 %collective-permute-start.1 = (f32[64,128]{1,0:T(8,128)S(1)}, f32[64,128]{1,0:T(8,128)S(1)}, u32[]{:S(2)}, u32[]{:S(2)}) collective-permute-start(f32[64,128]{1,0:T(8,128)S(1)} %get-tuple-element.46), channel_id=1, source_target_pairs={{1,2},{2,1},{3,4},{4,3},{5,6},{6,5},{9,10},{10,9},{11,12},{12,11},... | collective-permute-start | bytes 98312 | tf_op jit(solution)/shard_map/ppermute | solution.py:631
  20.1 3.1 %collective-permute-start = (f32[64,128]{1,0:T(8,128)S(1)}, f32[64,128]{1,0:T(8,128)S(1)}, u32[]{:S(2)}, u32[]{:S(2)}) collective-permute-start(f32[64,128]{1,0:T(8,128)S(1)} %get-tuple-element.47), channel_id=1, source_target_pairs={{0,1},{1,0},{2,3},{3,2},{4,5},{5,4},{6,7},{7,6},{8,9},{9,8},{10,11... | collective-permute-start | bytes 98312 | tf_op jit(solution)/shard_map/ppermute | solution.py:627
  23.4 21.9 %collective-permute-start.5 = (f32[168,128]{1,0:T(8,128)S(1)}, f32[168,128]{1,0:T(8,128)S(1)}, u32[]{:S(2)}, u32[]{:S(2)}) collective-permute-start(f32[168,128]{1,0:T(8,128)S(1)} %get-tuple-element.38), channel_id=1, source_target_pairs={{64,128},{65,129},{66,130},{67,131},{68,132},{69,133},{70,134},{71... | collective-permute-start | bytes 258056 | tf_op jit(solution)/shard_map/ppermute | solution.py:602
  25.8 19.5 %collective-permute-start.4 = (f32[168,128]{1,0:T(8,128)S(1)}, f32[168,128]{1,0:T(8,128)S(1)}, u32[]{:S(2)}, u32[]{:S(2)}) collective-permute-start(f32[168,128]{1,0:T(8,128)S(1)} %get-tuple-element.39), channel_id=1, source_target_pairs={{0,64},{1,65},{2,66},{3,67},{4,68},{5,69},{6,70},{7,71},{8,72},{9,... | collective-permute-start | bytes 258056 | tf_op jit(solution)/shard_map/ppermute | solution.py:602

commit v7 on v5

--- a/solution.py
+++ b/solution.py
@@ -130,7 +130,7 @@
 
 
 def gather_blocks(
-    pressure, conductance, depth, elevation, mask, pieces, surface, soil_here, mask_here, sems, sent
+    pressure, conductance, depth, elevation, mask, pieces, surface, soil_here, mask_here, sems
 ):
     arriving = [
         pltpu.make_async_copy(source, goal, sems.at[i])
@@ -146,22 +146,16 @@
     ]
     for copy in arriving:
         copy.start()
-    leaving = []
     for half in range(2):
         arriving[half].wait()
         for j in range(GROUP):
-            copy = pltpu.make_async_copy(
-                soil_here.at[half, :, :, pl.ds(j * LANES, LANES)],
-                pieces.at[j, pl.ds(half * LAYERS, LAYERS)],
-                sent.at[half * GROUP + j],
-            )
-            copy.start()
-            leaving.append(copy)
+            for layer in range(LAYERS):
+                pieces[j, half * LAYERS + layer] = soil_here[
+                    half, layer, :, pl.ds(j * LANES, LANES)
+                ]
     for copy in arriving[2:]:
         copy.wait()
     surface[2] = mask_here[...].astype(jnp.float32)
-    for copy in leaving:
-        copy.wait()
 
 
 def scatter_blocks(pieces, pressure, sems):
@@ -570,10 +564,9 @@
                 (2, LAYERS, SUB, GROUP * LANES),
                 pltpu.VMEM((ROWS, LANES), jnp.int32),
                 pltpu.SemaphoreType.DMA((5,)),
-                pltpu.SemaphoreType.DMA((2 * GROUP,)),
             ],
             pressure, conductance, depth, elevation, land_mask,
-            places=[pltpu.HBM] * 5 + [pl.ANY, pltpu.VMEM],
+            places=[pltpu.HBM] * 5 + [pltpu.VMEM] * 2,
         )
         pieces, tile_odd, sec_odd = lax.optimization_barrier((pieces, tile_odd, sec_odd))
         soil = lax.all_to_all(pieces, "place", 0, 0)

time: 58 us -> 57.8 us (level)
  no operation moved by 1% of the time
where the time goes in v7:
time: 57.8 us; the launch traced here: 57.6 us
  blocking collectives  21.6 us (37%)
  starting transfers between devices  14.4 us (25%)
  waiting for transfers between devices  11.6 us (20%)
  Pallas kernels  9.25 us (16%)
  between operations  0.74 us (1%)
    ppermute x4, starting transfers between devices, swap(): return lax.ppermute(value, axes, pairs(along, odd))  14.4 us
    all_to_all x1, blocking collectives, local(): soil = lax.all_to_all(pieces, 'place', 0, 0)  12.5 us
    ppermute x4, waiting for transfers between devices, swap(): return lax.ppermute(value, axes, pairs(along, odd))  11.6 us
    pallas_call x6, Pallas kernels, call(): pl.pallas_call(kernel, out_shape=[jax.ShapeDtypeStruct(shape, jnp.float32...  9.25 us
    all_to_all x1, blocking collectives, local(): soil = lax.all_to_all(soil, 'place', 0, 0)  9.04 us
  transfers between devices with their start and end apart: 4, of which 2 were waited for; matrix products, arithmetic and copies ran while one was open for 0% of the time, Pallas kernels for 7%

profile of v7, /device:TPU:448, one launch (start us, length us, event | category | flops | bytes accessed | tf_op | source)
XLA Modules:
  0.0 57.6 jit_solution(7375459646919458028)
XLA Ops:
  0.7 1.1 %shard_map.68 = (f32[8,10,8,128]{3,2,1,0:T(8,128)S(1)}, f32[3,64,128]{2,1,0:T(8,128)S(1)}) custom-call(f32[5,1,8,1024]{3,2,1,0:T(8,128)} %pressure.1, f32[5,1,8,1024]{3,2,1,0:T(8,128)} %conductance.1, f32[64,128]{1,0:T(8,128)} %depth.1, f32[64,128]{1,0:T(8,128)} %elevation.1, s32[64,128]{1,0:T(8,128)} %mask.1), custom_call_target="tpu_custom_call" | custom-call | tf_op jit(solution)/shard_map/pallas_call | solution.py:525
  1.7 12.5 %all_to_all.10.soil = f32[8,10,8,128]{3,2,1,0:T(8,128)S(1)} all-to-all(f32[8,10,8,128]{3,2,1,0:T(8,128)S(1)} %get-tuple-element.21), channel_id=1, replica_groups=mesh['sec'=8,'band'=8,'place'=8] {'place'}, dimensions={0} | all-to-all | bytes 655360 | tf_op jit(solution)/shard_map/all_to_all | solution.py:572
  14.2 0.3 shard_map.69
  14.5 2.9 %collective-permute-start.1 = (f32[2,64,128]{2,1,0:T(8,128)S(1)}, f32[2,64,128]{2,1,0:T(8,128)S(1)}, u32[]{:S(2)}, u32[]{:S(2)}) collective-permute-start(f32[2,64,128]{2,1,0:T(8,128)S(1)} %get-tuple-element.44), channel_id=1, source_target_pairs={{1,2},{2,1},{3,4},{4,3},{5,6},{6,5},{7,8},{8,7},{9,10},{10,9},{11,... | collective-permute-start | bytes 196616 | tf_op jit(solution)/shard_map/ppermute | solution.py:555
  17.4 1.9 %collective-permute-start = (f32[2,64,128]{2,1,0:T(8,128)S(1)}, f32[2,64,128]{2,1,0:T(8,128)S(1)}, u32[]{:S(2)}, u32[]{:S(2)}) collective-permute-start(f32[2,64,128]{2,1,0:T(8,128)S(1)} %get-tuple-element.45), channel_id=1, source_target_pairs={{0,1},{1,0},{2,3},{3,2},{4,5},{5,4},{6,7},{7,6},{8,9},{9,8},{10,11... | collective-permute-start | bytes 196616 | tf_op jit(solution)/shard_map/ppermute | solution.py:555
  19.3 2.9 %collective-permute-done.1 = f32[2,64,128]{2,1,0:T(8,128)S(1)} collective-permute-done((f32[2,64,128]{2,1,0:T(8,128)S(1)}, f32[2,64,128]{2,1,0:T(8,128)S(1)}, u32[]{:S(2)}, u32[]{:S(2)}) %collective-permute-start.1) | collective-permute-done | bytes 65568 | tf_op jit(solution)/shard_map/ppermute | solution.py:555
  22.2 0.0 collective-permute-done
  22.2 0.1 shard_map.71
  22.4 7.6 %collective-permute-start.3 = (f32[168,128]{1,0:T(8,128)S(1)}, f32[168,128]{1,0:T(8,128)S(1)}, u32[]{:S(2)}, u32[]{:S(2)}) collective-permute-start(f32[168,128]{1,0:T(8,128)S(1)} %get-tuple-element.40), channel_id=1, source_target_pairs={{64,128},{65,129},{66,130},{67,131},{68,132},{69,133},{70,134},{71... | collective-permute-start | bytes 258056 | tf_op jit(solution)/shard_map/ppermute | solution.py:555
  30.0 1.9 %collective-permute-start.2 = (f32[168,128]{1,0:T(8,128)S(1)}, f32[168,128]{1,0:T(8,128)S(1)}, u32[]{:S(2)}, u32[]{:S(2)}) collective-permute-start(f32[168,128]{1,0:T(8,128)S(1)} %get-tuple-element.41), channel_id=1, source_target_pairs={{0,64},{1,65},{2,66},{3,67},{4,68},{5,69},{6,70},{7,71},{8,72},{9,... | collective-permute-start | bytes 258056 | tf_op jit(solution)/shard_map/ppermute | solution.py:555
  31.9 4.1 %shard_map.70 = (f32[64,128]{1,0:T(8,128)S(1)}, f32[8,5,8,128]{3,2,1,0:T(8,128)S(1)}, f32[12,2,2,5,16,128]{5,4,3,2,1,0:T(8,128)S(1)}, f32[2,2,5,16,128]{4,3,2,1,...) custom-call(f32[8,10,8,128]{3,2,1,0:T(8,128)S(1)} %all_to_all.10.soi, ...), custom_call_target="tpu_custom_call" | custom-call | tf_op jit(solution)/shard_map/pallas_call | solution.py:525
  36.0 8.7 %collective-permute-done.3 = f32[168,128]{1,0:T(8,128)S(1)} collective-permute-done((f32[168,128]{1,0:T(8,128)S(1)}, f32[168,128]{1,0:T(8,128)S(1)}, u32[]{:S(2)}, u32[]{:S(2)}) %collective-permute-start.3) | collective-permute-done | bytes 86048 | tf_op jit(solution)/shard_map/ppermute | solution.py:555
  44.7 0.0 collective-permute-done.2
  44.8 3.0 %shard_map.72 = (f32[64,128]{1,0:T(8,128)}, f32[8,5,8,128]{3,2,1,0:T(8,128)S(1)}) custom-call(f32[64,128]{1,0:T(8,128)S(1)} %get-tuple-element.26.inner_depth, f32[8,5,8,128]{3,2,1,0:T(8,128)S(1)} %get-tuple-element.27.inner_pressure, f32[12,2,2,5,16,128]{5,4,3,2,1,0:T(8,128)S(1)} %get-tuple-element.28.seen, ...), custom_call_target="tpu_custom_call" | custom-call | tf_op jit(solution)/shard_map/pallas_call | solution.py:525
  47.8 9.0 %all_to_all.11.pieces = f32[8,5,8,128]{3,2,1,0:T(8,128)S(1)} all-to-all(f32[8,5,8,128]{3,2,1,0:T(8,128)S(1)} %get-tuple-element.37), channel_id=1, replica_groups=mesh['sec'=8,'band'=8,'place'=8] {'place'}, dimensions={0} | all-to-all | bytes 327680 | tf_op jit(solution)/shard_map/all_to_all | solution.py:603
  56.8 0.7 %shard_map.73 = f32[5,1,8,1024]{3,2,1,0:T(8,128)} custom-call(f32[8,5,8,128]{3,2,1,0:T(8,128)S(1)} %all_to_all.11.pieces), custom_call_target="tpu_custom_call" | custom-call | tf_op jit(solution)/shard_map/pallas_call | solution.py:525
  (4 shorter events, 0.1 us)
Async XLA Ops:
  14.5 7.7 %collective-permute-start.1 = (f32[2,64,128]{2,1,0:T(8,128)S(1)}, f32[2,64,128]{2,1,0:T(8,128)S(1)}, u32[]{:S(2)}, u32[]{:S(2)}) collective-permute-start(f32[2,64,128]{2,1,0:T(8,128)S(1)} %get-tuple-element.44), channel_id=1, source_target_pairs={{1,2},{2,1},{3,4},{4,3},{5,6},{6,5},{7,8},{8,7},{9,10},{10,9},{11,... | collective-permute-start | bytes 196616 | tf_op jit(solution)/shard_map/ppermute | solution.py:555
  17.4 4.8 %collective-permute-start = (f32[2,64,128]{2,1,0:T(8,128)S(1)}, f32[2,64,128]{2,1,0:T(8,128)S(1)}, u32[]{:S(2)}, u32[]{:S(2)}) collective-permute-start(f32[2,64,128]{2,1,0:T(8,128)S(1)} %get-tuple-element.45), channel_id=1, source_target_pairs={{0,1},{1,0},{2,3},{3,2},{4,5},{5,4},{6,7},{7,6},{8,9},{9,8},{10,11... | collective-permute-start | bytes 196616 | tf_op jit(solution)/shard_map/ppermute | solution.py:555
  22.4 22.4 %collective-permute-start.3 = (f32[168,128]{1,0:T(8,128)S(1)}, f32[168,128]{1,0:T(8,128)S(1)}, u32[]{:S(2)}, u32[]{:S(2)}) collective-permute-start(f32[168,128]{1,0:T(8,128)S(1)} %get-tuple-element.40), channel_id=1, source_target_pairs={{64,128},{65,129},{66,130},{67,131},{68,132},{69,133},{70,134},{71... | collective-permute-start | bytes 258056 | tf_op jit(solution)/shard_map/ppermute | solution.py:555
  30.0 14.7 %collective-permute-start.2 = (f32[168,128]{1,0:T(8,128)S(1)}, f32[168,128]{1,0:T(8,128)S(1)}, u32[]{:S(2)}, u32[]{:S(2)}) collective-permute-start(f32[168,128]{1,0:T(8,128)S(1)} %get-tuple-element.41), channel_id=1, source_target_pairs={{0,64},{1,65},{2,66},{3,67},{4,68},{5,69},{6,70},{7,71},{8,72},{9,... | collective-permute-start | bytes 258056 | tf_op jit(solution)/shard_map/ppermute | solution.py:555

commit v8 on v7

--- a/solution.py
+++ b/solution.py
@@ -55,19 +55,36 @@
     return surface[field - SOIL, pl.ds(p * SUB, SUB), :]
 
 
+FOLDED = 3 * SUB
+TALL = ROWS + FOLDED
+
+
 def pack_columns(soil, surface, left, right):
     lane = lane_index(SUB)
+    folded = [[jnp.zeros((SUB, LANES), jnp.float32)] * 3 for _ in range(2)]
     for p in range(GROUP):
         for plane, fields in ((0, range(SOIL)), (1, range(SOIL, FIELDS))):
-            lefts = jnp.zeros((SUB, LANES), jnp.float32)
-            rights = jnp.zeros((SUB, LANES), jnp.float32)
+            ends = [jnp.zeros((SUB, LANES), jnp.float32)] * 2
             for slot, field in enumerate(fields):
                 value = own_rows(soil, surface, field, p)
                 here = (lane >= slot * HALO) & (lane < slot * HALO + HALO)
-                lefts = jnp.where(here, turn(value, slot * HALO), lefts)
-                rights = jnp.where(here, turn(value, slot * HALO + HALO), rights)
-            left[plane, pl.ds(p * SUB, SUB), :] = lefts
-            right[plane, pl.ds(p * SUB, SUB), :] = rights
+                ends = [
+                    jnp.where(here, turn(value, slot * HALO + HALO * end), ends[end])
+                    for end in range(2)
+                ]
+            for end, out in enumerate((left, right)):
+                if plane == 0:
+                    out[pl.ds(p * SUB, SUB), :] = ends[end]
+                else:
+                    folded[end][p % 3] += turn(ends[end], FOLD * (p // 3))
+    for end, out in enumerate((left, right)):
+        for part in range(3):
+            out[pl.ds(ROWS + part * SUB, SUB), :] = folded[end][part]
+
+
+def unfolded(packed, row, count):
+    group, first = divmod(row, FOLDED)
+    return turn(packed[pl.ds(ROWS + first, count), :], -FOLD * group)
 
 
 def facing(edge):
@@ -97,13 +114,12 @@
         corner[...] = jnp.zeros((2 * SUB, LANES), jnp.float32)
         out[pl.ds(STRIP - SUB, SUB), :] = jnp.zeros((SUB, LANES), jnp.float32)
         for i, j, right in facing(edge):
-            here, there = pl.ds(first + i, 1), pl.ds(first + j, 1)
             take = column < right
             out[pl.ds(CORNERS + i, 1), :] = jnp.where(
-                take, from_right[0, here, :], from_left[0, there, :]
+                take, from_right[pl.ds(first + i, 1), :], from_left[pl.ds(first + j, 1), :]
             )
             corner[pl.ds(i, 1), :] = jnp.where(
-                take, from_right[1, here, :], from_left[1, there, :]
+                take, unfolded(from_right, first + i, 1), unfolded(from_left, first + j, 1)
             )
         spare = 0 if edge else HALO - 1
         out[pl.ds(CORNERS + spare, 1), :] = jnp.zeros((1, LANES), jnp.float32)
@@ -323,11 +339,13 @@
             at, slot, half = Field((D, E, M)[field - SOIL]), field - SOIL, 1
             name = lambda plane, rows: (plane, rows, slice(None))
         for p in range(GROUP):
-            rows, here = pl.ds(SUB + p * SUB, SUB), pl.ds(p * SUB, SUB)
+            rows = pl.ds(SUB + p * SUB, SUB)
             at[name(0, rows)] = own_rows(soil, surface, field, p)
-            at[name(1, rows)] = spread(
-                from_left[half, here, :], from_right[half, here, :], lane, slot
-            )
+            sides = [
+                unfolded(packed, p * SUB, SUB) if half else packed[pl.ds(p * SUB, SUB), :]
+                for packed in (from_left, from_right)
+            ]
+            at[name(1, rows)] = spread(*sides, lane, slot)
 
     def note(source, number):
         for edge, top in enumerate(TOPS):
@@ -571,7 +589,7 @@
         pieces, tile_odd, sec_odd = lax.optimization_barrier((pieces, tile_odd, sec_odd))
         soil = lax.all_to_all(pieces, "place", 0, 0)
         own = (soil, surface)
-        left, right = call(pack_columns, [(2, ROWS, LANES)] * 2, [], *own)
+        left, right = call(pack_columns, [(TALL, LANES)] * 2, [], *own)
         one = swap(jnp.where(tile_odd, left, right), "tile", 0)
         two = swap(jnp.where(tile_odd, right, left), "tile", 1)
         from_left = jnp.where(tile_odd, one, two)

time: 57.8 us -> 58.7 us (1.016)
  the two profiles are of different devices: /device:TPU:448 before, /device:TPU:4 now
where the time goes in v8:
time: 58.7 us; the launch traced here: 58.4 us
  blocking collectives  23.2 us (40%)
  starting transfers between devices  23.2 us (40%)
  Pallas kernels  10.3 us (18%)
  waiting for transfers between devices  0.85 us (1%)
  between operations  0.76 us (1%)
    ppermute x4, starting transfers between devices, swap(): return lax.ppermute(value, axes, pairs(along, odd))  23.2 us
    all_to_all x1, blocking collectives, local(): soil = lax.all_to_all(pieces, 'place', 0, 0)  12.5 us
    all_to_all x1, blocking collectives, local(): soil = lax.all_to_all(soil, 'place', 0, 0)  10.7 us
    pallas_call x6, Pallas kernels, call(): pl.pallas_call(kernel, out_shape=[jax.ShapeDtypeStruct(shape, jnp.float32...  10.3 us
  transfers between devices with their start and end apart: 4, of which 1 were waited for; matrix products, arithmetic and copies ran while one was open for 0% of the time, Pallas kernels for 8%

profile of v8, /device:TPU:4, one launch (start us, length us, event | category | flops | bytes accessed | tf_op | source)
XLA Modules:
  0.0 58.4 jit_solution(12872083080734507331)
XLA Ops:
  0.7 1.1 %shard_map.68 = (f32[8,10,8,128]{3,2,1,0:T(8,128)S(1)}, f32[3,64,128]{2,1,0:T(8,128)S(1)}) custom-call(f32[5,1,8,1024]{3,2,1,0:T(8,128)} %pressure.1, f32[5,1,8,1024]{3,2,1,0:T(8,128)} %conductance.1, f32[64,128]{1,0:T(8,128)} %depth.1, f32[64,128]{1,0:T(8,128)} %elevation.1, s32[64,128]{1,0:T(8,128)} %mask.1), custom_call_target="tpu_custom_call" | custom-call | tf_op jit(solution)/shard_map/pallas_call | solution.py:543
  1.7 12.5 %all_to_all.10.soil = f32[8,10,8,128]{3,2,1,0:T(8,128)S(1)} all-to-all(f32[8,10,8,128]{3,2,1,0:T(8,128)S(1)} %get-tuple-element.21), channel_id=1, replica_groups=mesh['sec'=8,'band'=8,'place'=8] {'place'}, dimensions={0} | all-to-all | bytes 655360 | tf_op jit(solution)/shard_map/all_to_all | solution.py:590
  14.2 0.5 shard_map.69
  14.7 0.7 %collective-permute-start.1 = (f32[88,128]{1,0:T(8,128)S(1)}, f32[88,128]{1,0:T(8,128)S(1)}, u32[]{:S(2)}, u32[]{:S(2)}) collective-permute-start(f32[88,128]{1,0:T(8,128)S(1)} %get-tuple-element.44), channel_id=1, source_target_pairs={{1,2},{2,1},{3,4},{4,3},{5,6},{6,5},{7,8},{8,7},{9,10},{10,9},{11,... | collective-permute-start | bytes 135176 | tf_op jit(solution)/shard_map/ppermute | solution.py:573
  15.4 3.8 %collective-permute-start = (f32[88,128]{1,0:T(8,128)S(1)}, f32[88,128]{1,0:T(8,128)S(1)}, u32[]{:S(2)}, u32[]{:S(2)}) collective-permute-start(f32[88,128]{1,0:T(8,128)S(1)} %get-tuple-element.45), channel_id=1, source_target_pairs={{0,1},{1,0},{2,3},{3,2},{4,5},{5,4},{6,7},{7,6},{8,9},{9,8},{10,11... | collective-permute-start | bytes 135176 | tf_op jit(solution)/shard_map/ppermute | solution.py:573
  19.2 0.0 collective-permute-done.1
  19.2 0.8 %collective-permute-done = f32[88,128]{1,0:T(8,128)S(1)} collective-permute-done((f32[88,128]{1,0:T(8,128)S(1)}, f32[88,128]{1,0:T(8,128)S(1)}, u32[]{:S(2)}, u32[]{:S(2)}) %collective-permute-start) | collective-permute-done | bytes 45088 | tf_op jit(solution)/shard_map/ppermute | solution.py:573
  20.1 0.1 shard_map.71
  20.3 2.4 %collective-permute-start.3 = (f32[168,128]{1,0:T(8,128)S(1)}, f32[168,128]{1,0:T(8,128)S(1)}, u32[]{:S(2)}, u32[]{:S(2)}) collective-permute-start(f32[168,128]{1,0:T(8,128)S(1)} %get-tuple-element.40), channel_id=1, source_target_pairs={{64,128},{65,129},{66,130},{67,131},{68,132},{69,133},{70,134},{71... | collective-permute-start | bytes 258056 | tf_op jit(solution)/shard_map/ppermute | solution.py:573
  22.7 16.3 %collective-permute-start.2 = (f32[168,128]{1,0:T(8,128)S(1)}, f32[168,128]{1,0:T(8,128)S(1)}, u32[]{:S(2)}, u32[]{:S(2)}) collective-permute-start(f32[168,128]{1,0:T(8,128)S(1)} %get-tuple-element.41), channel_id=1, source_target_pairs={{0,64},{1,65},{2,66},{3,67},{4,68},{5,69},{6,70},{7,71},{8,72},{9,... | collective-permute-start | bytes 258056 | tf_op jit(solution)/shard_map/ppermute | solution.py:573
  39.0 4.8 %shard_map.70 = (f32[64,128]{1,0:T(8,128)S(1)}, f32[8,5,8,128]{3,2,1,0:T(8,128)S(1)}, f32[12,2,2,5,16,128]{5,4,3,2,1,0:T(8,128)S(1)}, f32[2,2,5,16,128]{4,3,2,1,...) custom-call(f32[8,10,8,128]{3,2,1,0:T(8,128)S(1)} %all_to_all.10.soi, ...), custom_call_target="tpu_custom_call" | custom-call | tf_op jit(solution)/shard_map/pallas_call | solution.py:543
  43.9 0.0 collective-permute-done.3
  43.9 0.0 collective-permute-done.2
  43.9 3.1 %shard_map.72 = (f32[64,128]{1,0:T(8,128)}, f32[8,5,8,128]{3,2,1,0:T(8,128)S(1)}) custom-call(f32[64,128]{1,0:T(8,128)S(1)} %get-tuple-element.26.inner_depth, f32[8,5,8,128]{3,2,1,0:T(8,128)S(1)} %get-tuple-element.27.inner_pressure, f32[12,2,2,5,16,128]{5,4,3,2,1,0:T(8,128)S(1)} %get-tuple-element.28.seen, ...), custom_call_target="tpu_custom_call" | custom-call | tf_op jit(solution)/shard_map/pallas_call | solution.py:543
  47.0 10.7 %all_to_all.11.pieces = f32[8,5,8,128]{3,2,1,0:T(8,128)S(1)} all-to-all(f32[8,5,8,128]{3,2,1,0:T(8,128)S(1)} %get-tuple-element.37), channel_id=1, replica_groups=mesh['sec'=8,'band'=8,'place'=8] {'place'}, dimensions={0} | all-to-all | bytes 327680 | tf_op jit(solution)/shard_map/all_to_all | solution.py:621
  57.7 0.7 %shard_map.73 = f32[5,1,8,1024]{3,2,1,0:T(8,128)} custom-call(f32[8,5,8,128]{3,2,1,0:T(8,128)S(1)} %all_to_all.11.pieces), custom_call_target="tpu_custom_call" | custom-call | tf_op jit(solution)/shard_map/pallas_call | solution.py:543
  (4 shorter events, 0.1 us)
Async XLA Ops:
  14.7 4.5 %collective-permute-start.1 = (f32[88,128]{1,0:T(8,128)S(1)}, f32[88,128]{1,0:T(8,128)S(1)}, u32[]{:S(2)}, u32[]{:S(2)}) collective-permute-start(f32[88,128]{1,0:T(8,128)S(1)} %get-tuple-element.44), channel_id=1, source_target_pairs={{1,2},{2,1},{3,4},{4,3},{5,6},{6,5},{7,8},{8,7},{9,10},{10,9},{11,... | collective-permute-start | bytes 135176 | tf_op jit(solution)/shard_map/ppermute | solution.py:573
  15.4 4.7 %collective-permute-start = (f32[88,128]{1,0:T(8,128)S(1)}, f32[88,128]{1,0:T(8,128)S(1)}, u32[]{:S(2)}, u32[]{:S(2)}) collective-permute-start(f32[88,128]{1,0:T(8,128)S(1)} %get-tuple-element.45), channel_id=1, source_target_pairs={{0,1},{1,0},{2,3},{3,2},{4,5},{5,4},{6,7},{7,6},{8,9},{9,8},{10,11... | collective-permute-start | bytes 135176 | tf_op jit(solution)/shard_map/ppermute | solution.py:573
  20.3 23.6 %collective-permute-start.3 = (f32[168,128]{1,0:T(8,128)S(1)}, f32[168,128]{1,0:T(8,128)S(1)}, u32[]{:S(2)}, u32[]{:S(2)}) collective-permute-start(f32[168,128]{1,0:T(8,128)S(1)} %get-tuple-element.40), channel_id=1, source_target_pairs={{64,128},{65,129},{66,130},{67,131},{68,132},{69,133},{70,134},{71... | collective-permute-start | bytes 258056 | tf_op jit(solution)/shard_map/ppermute | solution.py:573
  22.7 21.2 %collective-permute-start.2 = (f32[168,128]{1,0:T(8,128)S(1)}, f32[168,128]{1,0:T(8,128)S(1)}, u32[]{:S(2)}, u32[]{:S(2)}) collective-permute-start(f32[168,128]{1,0:T(8,128)S(1)} %get-tuple-element.41), channel_id=1, source_target_pairs={{0,64},{1,65},{2,66},{3,67},{4,68},{5,69},{6,70},{7,71},{8,72},{9,... | collective-permute-start | bytes 258056 | tf_op jit(solution)/shard_map/ppermute | solution.py:573
